TPU v7x, 32 devices: a whole 2x2x4 slice. The times are simulated.
32 devices in a mesh: row: 4 (over y, core), col: 8 (over z, x).
Axes of the slice: x: 2, y: 2, z: 4, core: 2. Of those that a mesh axis runs over, the one named last changes fastest.
Arguments:
- block_in: bfloat16 [32768, 1024], P('col', 'row'), may hold values from -6 to 6
- norm_gain: float32 [1024], P('row'), may hold values from 0.25 to 1.75
- proj_inner: bfloat16 [1024, 32, 128], P('row', 'col'), may hold values from -0.1875 to 0.1875
- proj_state: bfloat16 [1024, 288], P('row'), may hold values from -0.1875 to 0.1875
- conv_inner: float32 [4, 2048], P(None, 'col'), may hold values from -3 to 3
- conv_inner_bias: float32 [2048], P('col'), may hold values from -3 to 3
- conv_state: float32 [4, 256], replicated, may hold values from -3 to 3
- conv_state_bias: float32 [256], replicated, may hold values from -3 to 3
- step_bias: float32 [32], P('col'), may hold values from -6.9 to -2.3
- decay_log: float32 [32], P('col'), may hold values from 0 to 2.77
- skip_gain: float32 [32], P('col'), may hold values from 0.5 to 1.5
- gate_gain: float32 [2048], P('col'), may hold values from 0.25 to 1.75
- proj_out: bfloat16 [2048, 1024], P('col', 'row'), may hold values from -0.125 to 0.125
- adapt_in_down: bfloat16 [1024, 128], P('row'), may hold values from -0.1875 to 0.1875
- adapt_in_up: bfloat16 [128, 32, 128], P(None, 'col'), may hold values from -1.5 to 1.5
- adapt_out_down: bfloat16 [128, 2048], P(None, 'col'), may hold values from -0.125 to 0.125
- adapt_out_up: bfloat16 [1024, 128], P('row'), may hold values from -1.5 to 1.5
- adapter_id: int32 [8], replicated, may hold values from 0 to 7, as said below
- cotangent: bfloat16 [32768, 1024], P('col', 'row'), may hold values from -6 to 6
Outputs:
- block_out: bfloat16 [32768, 1024], P('col', 'row')
- input_grad: float32 [32768, 1024], P('col', 'row')
- grad_in_down: float32 [1024, 128], P('row', 'col')
- grad_in_up: float32 [128, 32, 128], P(None, 'col')
- grad_out_down: float32 [128, 2048], P(None, 'col')
- grad_out_up: float32 [1024, 128], P('row', 'col')
Inputs may be any that keep to these rules, and one draw needn't show every extreme that they name: `adapter_id`: each adapter is chosen by exactly 1 sequence.
All inputs are finite; a program needn't handle non-finite values.
Results may differ from a plain program's by a relative error of at most 0.025.
Values may be sent and summed in bfloat16 or wider, within the bound.
A program may use at most 640 MiB of HBM per device.

v0:
```python
import jax
import jax.numpy as jnp
from jax import lax
from jax.sharding import PartitionSpec as P

D = 1024
P_SIZE = 64
BLOCK = 256
NA = 8
SEQ = 4096
DI = 2048


EPS = 1e-05
HIGHEST = lax.Precision.HIGHEST


def half_round(value):
    rounded = lax.optimization_barrier(value.astype(jnp.bfloat16)).astype(jnp.float32)
    return value + lax.stop_gradient(rounded - value)


def causal_conv(values, kernel, bias_row, seq_len):
    length = values.shape[0]
    position = jnp.arange(length) % seq_len
    summed = values * kernel[0] + bias_row
    for offset in range(1, kernel.shape[0]):
        shifted = jnp.concatenate(
            [jnp.zeros((offset, values.shape[1]), jnp.float32), values[:-offset]], axis=0
        )
        summed = summed + jnp.where((position >= offset)[:, None], shifted, 0.0) * kernel[offset]
    return summed


def scan_blocks(value_heads, b_rows, c_rows, step_size, log_decay, seq_len, block):
    length, head_count, head_dim = value_heads.shape
    states = b_rows.shape[1]
    blocks = length // block
    per_seq = seq_len // block
    seq_count = blocks // per_seq
    value_block = value_heads.reshape(blocks, block, head_count, head_dim)
    b_block = b_rows.reshape(blocks, block, states)
    c_block = c_rows.reshape(blocks, block, states)
    step_block = jnp.swapaxes(step_size.reshape(blocks, block, head_count), 1, 2)
    cumul = jnp.cumsum(jnp.swapaxes(log_decay.reshape(blocks, block, head_count), 1, 2), axis=2)
    scores = jnp.einsum("ctn,csn->cts", c_block, b_block, precision=HIGHEST)
    causal = (jnp.arange(block)[:, None] >= jnp.arange(block)[None, :])[None, None]
    spread = cumul[:, :, :, None] - cumul[:, :, None, :]
    damping = jnp.where(causal, jnp.exp(jnp.where(causal, spread, 0.0)), 0.0)
    weights = half_round(scores[:, None] * damping * step_block[:, :, None, :])
    within = jnp.einsum("chts,cshp->cthp", weights, value_block, precision=HIGHEST)
    to_end = jnp.exp(cumul[:, :, -1:] - cumul) * step_block
    b_weighted = half_round(b_block[:, None, :, :] * to_end[..., None])
    added = jnp.einsum("chsn,cshp->chnp", b_weighted, value_block, precision=HIGHEST)
    falloff = jnp.exp(cumul[:, :, -1])

    def advance(carried, inputs):
        factor, addend = inputs
        return (factor[:, :, None, None] * carried + addend, carried)

    initial = jnp.zeros((seq_count, head_count, states, head_dim), jnp.float32)
    fall_steps = jnp.swapaxes(falloff.reshape(seq_count, per_seq, head_count), 0, 1)
    add_steps = jnp.swapaxes(added.reshape(seq_count, per_seq, head_count, states, head_dim), 0, 1)
    _, entering = lax.scan(jax.checkpoint(advance), initial, (fall_steps, add_steps))
    entering = half_round(
        jnp.swapaxes(entering, 0, 1).reshape(blocks, head_count, states, head_dim)
    )
    carried_out = jnp.exp(cumul)[..., None] * jnp.einsum(
        "ctn,chnp->chtp", c_block, entering, precision=HIGHEST
    )
    return (within + jnp.swapaxes(carried_out, 1, 2)).reshape(length, head_count, head_dim)


def mix_heads(
    inner_value,
    state_cols,
    head_first,
    conv_inner,
    conv_inner_bias,
    conv_state,
    conv_state_bias,
    step_bias,
    decay_log,
    skip_gain,
    seq_len,
    block,
):
    length, head_count, double = inner_value.shape
    head_dim = double // 2
    states = conv_state.shape[1] // 2
    gate_part = inner_value[:, :, :head_dim]
    value_part = inner_value[:, :, head_dim:].reshape(length, head_count * head_dim)
    value_conv = jax.nn.silu(causal_conv(value_part, conv_inner, conv_inner_bias, seq_len))
    state_conv = jax.nn.silu(
        causal_conv(state_cols[:, : 2 * states], conv_state, conv_state_bias, seq_len)
    )
    step_raw = lax.dynamic_slice_in_dim(state_cols, 2 * states + head_first, head_count, 1)
    step_size = jax.nn.softplus(step_raw + step_bias)
    log_decay = -jnp.exp(decay_log) * step_size
    value_low = half_round(value_conv).reshape(length, head_count, head_dim)
    scanned = scan_blocks(
        value_low,
        half_round(state_conv[:, :states]),
        half_round(state_conv[:, states:]),
        step_size,
        log_decay,
        seq_len,
        block,
    )
    output = scanned + skip_gain[:, None] * value_conv.reshape(length, head_count, head_dim)
    return (output * jax.nn.silu(gate_part)).reshape(length, head_count * head_dim)


def adapter_mask(first_row, length, adapter_id, rank_total):
    seq_of = (first_row + jnp.arange(length, dtype=jnp.int32)) // SEQ
    lookup = seq_of[:, None] == jnp.arange(adapter_id.shape[0], dtype=jnp.int32)[None, :]
    chosen = jnp.sum(jnp.where(lookup, adapter_id[None, :], 0), axis=1)
    groups = jnp.arange(rank_total, dtype=jnp.int32) // (rank_total // NA)
    return (chosen[:, None] == groups[None, :]).astype(jnp.float32)


def front_product(rows_in, weight, first_row, adapter_id, inner_width, rank_total):
    product = jnp.dot(rows_in, weight, preferred_element_type=jnp.float32)
    picked = adapter_mask(first_row, rows_in.shape[0], adapter_id, rank_total)
    return jnp.concatenate(
        [
            product[:, :inner_width],
            product[:, inner_width : inner_width + rank_total] * picked,
            product[:, inner_width + rank_total :],
        ],
        axis=1,
    )


def per_device(
    block_in,
    norm_gain,
    proj_inner,
    proj_state,
    conv_inner,
    conv_inner_bias,
    conv_state,
    conv_state_bias,
    step_bias,
    decay_log,
    skip_gain,
    gate_gain,
    proj_out,
    adapt_in_down,
    adapt_in_up,
    adapt_out_down,
    adapt_out_up,
    adapter_id,
    cotangent,
):
    row_count = lax.axis_size("row")
    col_count = lax.axis_size("col")
    row_index = lax.axis_index("row")
    col_index = lax.axis_index("col")
    width_rows = block_in.shape[1]
    local_heads = proj_inner.shape[1]
    inner_width = local_heads * 2 * P_SIZE
    head_width = local_heads * P_SIZE
    rank_total = adapt_in_down.shape[1]
    state_width = proj_state.shape[1]
    state_share = state_width // col_count
    rank_share = rank_total // col_count
    x_value = block_in.astype(jnp.float32)
    square_sum = lax.psum(jnp.sum(x_value * x_value, axis=1), "row")
    inv_rms = lax.rsqrt(square_sum / D + EPS)[:, None]
    normed = (x_value * inv_rms * norm_gain).astype(jnp.bfloat16)
    normed_all = lax.all_gather(normed, "col", axis=0, tiled=True)
    token_total = normed_all.shape[0]
    token_rows = token_total // row_count
    token_cols = token_total // col_count
    inner_cols = proj_inner.reshape(width_rows, inner_width)
    state_cut = lax.dynamic_slice_in_dim(proj_state, col_index * state_share, state_share, 1)
    front_weight = jnp.concatenate([inner_cols, adapt_in_down, proj_state], axis=1)
    return_weight = jnp.concatenate([proj_out.T, adapt_out_up], axis=1)
    rows_in = normed_all
    front_sum = lax.psum_scatter(
        front_product(
            rows_in, front_weight, jnp.int32(0), adapter_id, inner_width, rank_total
        ).astype(jnp.bfloat16),
        "row",
        scatter_dimension=0,
        tiled=True,
    ).astype(jnp.float32)
    inner_base = front_sum[:, :inner_width]
    adapt_low = front_sum[:, inner_width : inner_width + rank_total].astype(jnp.bfloat16)
    state_part = front_sum[:, inner_width + rank_total :]
    up_cols = adapt_in_up.reshape(rank_total, inner_width)
    inner_value = inner_base + jnp.dot(adapt_low, up_cols, preferred_element_type=jnp.float32)
    head_first = col_index * local_heads

    def local_mix(inner_arg, state_arg):
        return mix_heads(
            inner_arg.reshape(token_rows, local_heads, 2 * P_SIZE),
            state_arg,
            head_first,
            conv_inner,
            conv_inner_bias,
            conv_state,
            conv_state_bias,
            step_bias,
            decay_log,
            skip_gain,
            SEQ,
            BLOCK,
        )

    gated, mix_pullback = jax.vjp(local_mix, inner_value, state_part)
    gate_square = lax.psum(jnp.sum(gated * gated, axis=1).astype(jnp.bfloat16), "col").astype(
        jnp.float32
    )
    gate_rms = lax.rsqrt(gate_square / DI + EPS)[:, None]
    mixed = (gated * gate_rms * gate_gain).astype(jnp.bfloat16)
    mixed_all = lax.all_gather(mixed, "row", axis=0, tiled=True)
    back_weight = jnp.concatenate([proj_out, adapt_out_down.T], axis=1)
    rows_in = mixed_all
    product = jnp.dot(rows_in, back_weight, preferred_element_type=jnp.float32)
    picked = adapter_mask(jnp.int32(0), lax.axis_size("col") * token_cols, adapter_id, rank_total)
    out_sum = lax.psum_scatter(
        jnp.concatenate([product[:, :width_rows], product[:, width_rows:] * picked], axis=1).astype(
            jnp.bfloat16
        ),
        "col",
        scatter_dimension=0,
        tiled=True,
    ).astype(jnp.float32)
    side_low = out_sum[:, width_rows:].astype(jnp.bfloat16)
    block_out = (
        x_value
        + out_sum[:, :width_rows]
        + jnp.dot(side_low, adapt_out_up.T, preferred_element_type=jnp.float32)
    ).astype(jnp.bfloat16)
    up_out_part = jnp.dot(cotangent.T, side_low, preferred_element_type=jnp.float32)
    cot_all = lax.all_gather(cotangent, "col", axis=0, tiled=True)
    rows_in = cot_all
    mix_sum = lax.psum_scatter(
        jnp.dot(rows_in, return_weight, preferred_element_type=jnp.float32).astype(jnp.bfloat16),
        "row",
        scatter_dimension=0,
        tiled=True,
    ).astype(jnp.float32)
    row_mask = adapter_mask(row_index * token_rows, token_rows, adapter_id, rank_total)
    side_grad = mix_sum[:, head_width:].astype(jnp.bfloat16) * row_mask.astype(jnp.bfloat16)
    mixed_grad = mix_sum[:, :head_width] + jnp.dot(
        side_grad, adapt_out_down, preferred_element_type=jnp.float32
    )
    down_out_part = jnp.dot(side_grad.T, mixed, preferred_element_type=jnp.float32)
    gate_inner = lax.psum(
        jnp.sum(gated * gate_gain * mixed_grad, axis=1).astype(jnp.bfloat16), "col"
    ).astype(jnp.float32)
    gated_grad = gate_rms * gate_gain * mixed_grad - gated * gate_rms**3 / DI * gate_inner[:, None]
    inner_grad, state_grad = mix_pullback(gated_grad)
    inner_low = inner_grad.astype(jnp.bfloat16)
    up_in_part = jnp.dot(adapt_low.T, inner_low, preferred_element_type=jnp.float32)
    adapt_grad = jnp.dot(inner_low, up_cols.T, preferred_element_type=jnp.float32)
    state_share_grad, adapt_share, up_out_grad = (
        lax.psum_scatter(
            state_grad.astype(jnp.bfloat16), "col", scatter_dimension=1, tiled=True
        ).astype(jnp.float32),
        lax.psum_scatter(
            adapt_grad.astype(jnp.bfloat16), "col", scatter_dimension=1, tiled=True
        ).astype(jnp.float32),
        lax.psum_scatter(
            up_out_part.astype(jnp.bfloat16), "col", scatter_dimension=1, tiled=True
        ).astype(jnp.float32),
    )
    state_low = state_share_grad.astype(jnp.bfloat16)
    mask_share = lax.dynamic_slice_in_dim(row_mask, col_index * rank_share, rank_share, 1)
    adapt_low_grad = adapt_share.astype(jnp.bfloat16) * mask_share.astype(jnp.bfloat16)
    inner_all, state_all, adapt_all = (
        lax.all_gather(inner_low, "row", axis=0, tiled=True),
        lax.all_gather(state_low, "row", axis=0, tiled=True),
        lax.all_gather(adapt_low_grad, "row", axis=0, tiled=True),
    )
    in_down_grad = jnp.dot(normed_all.T, adapt_all, preferred_element_type=jnp.float32)
    down_cut = lax.dynamic_slice_in_dim(adapt_in_down, col_index * rank_share, rank_share, 1)
    summed = jnp.einsum("te,de->td", inner_all, inner_cols, preferred_element_type=jnp.float32)
    summed = summed + jnp.einsum(
        "te,de->td", state_all, state_cut, preferred_element_type=jnp.float32
    )
    normed_grad = lax.psum_scatter(
        (
            summed
            + jnp.einsum("te,de->td", adapt_all, down_cut, preferred_element_type=jnp.float32)
        ).astype(jnp.bfloat16),
        "col",
        scatter_dimension=0,
        tiled=True,
    ).astype(jnp.float32)
    norm_part = jnp.sum(x_value * norm_gain * normed_grad, axis=1)
    norm_inner, up_in_grad, down_out_grad = (
        lax.psum(norm_part.astype(jnp.bfloat16), "row").astype(jnp.float32),
        lax.psum(up_in_part.astype(jnp.bfloat16), "row").astype(jnp.float32),
        lax.psum(down_out_part.astype(jnp.bfloat16), "row").astype(jnp.float32),
    )
    input_grad = (
        cotangent.astype(jnp.float32)
        + inv_rms * norm_gain * normed_grad
        - x_value * inv_rms**3 / D * norm_inner[:, None]
    )
    return (
        block_out,
        input_grad,
        in_down_grad,
        up_in_grad.reshape(rank_total, local_heads, 2 * P_SIZE),
        down_out_grad,
        up_out_grad,
    )


def solution(mesh):
    placed = (
        P("col", "row"),
        P("row"),
        P("row", "col", None),
        P("row", None),
        P(None, "col"),
        P("col"),
        P(),
        P(),
        P("col"),
        P("col"),
        P("col"),
        P("col"),
        P("col", "row"),
        P("row", None),
        P(None, "col", None),
        P(None, "col"),
        P("row", None),
        P(),
        P("col", "row"),
    )
    return jax.shard_map(
        per_device,
        mesh=mesh,
        in_specs=placed,
        out_specs=(
            P("col", "row"),
            P("col", "row"),
            P("row", "col"),
            P(None, "col", None),
            P(None, "col"),
            P("row", "col"),
        ),
        check_vma=False,
    )
```

profile of v0, /device:TPU:0, one launch (start us, length us, event | category | flops | bytes accessed | tf_op | source)
XLA Modules:
  0.0 2866.5 jit_solution(1814981605550988414)
XLA Ops:
  10.7 12.7 psum.42
  28.2 226.5 %all-gather.7.cloned.1.call-done = bf16[32768,256]{0,1:T(8,128)(2,1)} async-done(((bf16[4096,256]{0,1:T(8,128)(2,1)}), bf16[32768,256]{0,1:T(8,128)(2,1)}) %all-gather.7.cloned.1.call-update) | async-done | bytes 16777232 | tf_op jit(solution)/shard_map/all_gather | solution.py:172
  254.7 29.8 %fusion.103 = bf16[32768,928]{0,1:T(8,128)(2,1)} fusion(bf16[32768,256]{0,1:T(8,128)(2,1)} %all-gather.7.cloned.1.call-done, bf16[256,288]{1,0:T(8,128)(2,1)S(1)} %copy.431, bf16[256,128]{1,0:T(8,128)(2,1)S(1)} %copy-done.48, bf16[256,512]{1,0:T(8,128)(2,1)S(1)} %bitcast.327), kind=kOutput, calls=%fused_computation.178 | convolution fusion | flops 15570681856 | bytes 78069760 | tf_op jit(solution)/shard_map/dot_general | solution.py:123
  284.5 16.5 slice.180
  301.1 23.0 slice.178
  332.9 41.4 %pad_maximum_fusion = bf16[32768,928]{0,1:T(8,128)(2,1)} fusion(bf16[32768,288]{0,1:T(8,128)(2,1)} %slice.180, bf16[32768,128]{0,1:T(8,128)(2,1)} %fusion.12, bf16[32768,512]{0,1:T(8,128)(2,1)} %slice.178), kind=kLoop, calls=%fused_computation.12 | loop fusion | flops 182452224 | bytes 121634816 | tf_op jit(solution)/shard_map/concatenate | solution.py:125
  375.3 107.4 %all-gather.11.cloned.1.call-done = bf16[32768,256]{1,0:T(8,128)(2,1)} async-done(((bf16[4096,256]{1,0:T(8,128)(2,1)}), bf16[32768,256]{1,0:T(8,128)(2,1)}) %all-gather.11.cloned.1.call-update) | async-done | bytes 16777232 | tf_op jit(solution)/shard_map/all_gather | solution.py:238
  482.6 26.0 fusion.2
  513.6 381.2 %reduce-scatter.9.cloned.1.call-done = bf16[8192,928]{0,1:T(8,128)(2,1)} async-done(((bf16[32768,928]{0,1:T(8,128)(2,1)}), bf16[8192,928]{0,1:T(8,128)(2,1)}) %reduce-scatter.9.cloned.1.call-update) | async-done | bytes 15204368 | tf_op jit(solution)/shard_map/reduce_scatter | solution.py:181
  906.5 20.2 convert_element_type.140
  926.7 10.5 slice_add_fusion
  976.0 19.4 fusion.64
  1033.9 20.3 fusion.155
  1063.5 10.3 copy.561
  1073.8 27.9 fusion.15
  1108.6 32.6 %while.32 = (s32[]{:T(128)}, f32[2,4,128,64]{3,2,1,0:T(8,128)S(1)}, f32[16,2,4,128,64]{4,3,2,1,0:T(8,128)}, f32[16,2,4]{2,1,0:T(2,128)S(1)}, f32[16,2,4,128,64]{4,3,2,1,0:T(8,128)}, /*index=5*/s32[]{:T(128)}, s32[]{:T(128)}) while((s32[]{:T(128)}, f32[2,4,128,64]{3,2,1,0:T(8,128)S(1)}, f32[16,2,4,128,64]{4,3,2,1,0:T(8,128)}, ...), condition=%wide.region_7.8_spmd.clone, body=%wide.region_6.7_spmd.clone.sunk | while | flops 262147 | bytes 1573068 | solution.py:64
  1164.5 11.5 fusion.7
  1188.4 49.3 %fusion.54 = f32[32,4,8,8,256]{4,3,2,1,0:T(8,128)} fusion(f32[32,4,64,256]{3,2,1,0:T(8,128)} %fusion.165, f32[32,256,4]{1,2,0:T(4,128)S(1)} %copy.442, bf16[32,4,256,256]{3,2,1,0:T(8,128)(2,1)} %fusion.7, f32[32,4,256]{2,1,0:T(4,128)S(1)} %bitcast.323, f32[32,4,256]{2,1,0:T(4,128)S(1)} %copy-done.38, f32[32,256,256]{2,1,0:T(8,128)} %copy-done.19, ...), kind=kOutput, calls=%fused_computation.103 | convolution fusion | flops 6513754112 | bytes 50790400 | tf_op jit(solution)/shard_map/jvp(chts,cshp->cthp)/dot_general | solution.py:51
  1261.9 37.3 %all-reduce.21 = (bf16[8192]{0:T(1024)(128)(2,1)S(1)}, bf16[8192]{0:T(1024)(128)(2,1)S(1)}) all-reduce(bf16[8192]{0:T(1024)(128)(2,1)S(1)} %get-tuple-element.410, bf16[8192]{0:T(1024)(128)(2,1)S(1)} %get-tuple-element.454), channel_id=1, replica_groups=mesh['row'=4,'col'=8] {'col'}, use_global_device_ids=true, to_apply=%region_9.10 | all-reduce | flops 16384 | bytes 65536 | tf_op jit(solution)/shard_map/psum | solution.py:213
  1299.2 10.5 fusion.50
  1309.7 20.0 broadcast_multiply_fusion.1
  1342.7 12.3 fusion.71
  1364.7 39.4 %while.33 = (s32[]{:T(128)}, f32[2,4,128,64]{3,2,1,0:T(8,128)S(1)}, f32[16,2,4]{2,1,0:T(2,128)S(1)}, f32[16,2,4,128,64]{3,4,2,0,1:T(8,128)}, f32[16,2,4,128,64]{...) while((s32[]{:T(128)}, f32[2,4,128,64]{3,2,1,0:T(8,128)S(1)}, ...), condition=%wide.region_17.18_spmd.clone, body=%wide.region_15.17_spmd.clone.sunk | while | flops 327676 | bytes 3672339 | solution.py:64
  1404.1 63.3 %fusion.11 = (f32[32,4,256]{2,1,0:T(4,128)}, f32[32,4,256]{2,1,0:T(4,128)}, f32[32,4,256]{2,1,0:T(4,128)}, f32[32,256,256]{2,1,0:T(8,128)S(1)}) fusion(f32[32,4,256]{2,1,0:T(4,128)S(1)} %bitcast.324, f32[32,4,256]{2,1,0:T(4,128)S(1)} %copy-done.38, f32[32,256,256]{2,1,0:T(8,128)} %copy-done.19, pred[256,256]{1,0:T(8,128)(4,1)S(1)} %copy-done.47, ...), kind=kOutput, calls=%fused_computation.37 | convolution fusion | flops 6566084608 | bytes 34275328 | tf_op jit(solution)/shard_map/transpose(jvp(chts,cshp->cthp))/dot_general | solution.py:51
  1475.9 21.7 bitcast_add_fusion.2
  1503.3 15.8 fusion.14
  1519.1 39.9 %add_bitcast_fusion = f32[32,256,4,64]{1,3,2,0:T(8,128)} fusion(f32[32,4,64,256]{3,2,1,0:T(8,128)S(1)} %fusion.14, bf16[32,4,256,256]{3,2,1,0:T(8,128)(2,1)} %fusion.7, f32[32,4,256]{2,1,0:T(4,128)S(1)} %bitcast.325, f32[32,4,256]{2,1,0:T(4,128)S(1)} %copy-done.38, f32[32,256,256]{2,1,0:T(8,128)} %copy-done.19, pred[256,256]{1,0:T(8,128)(4,1)S(1)} %copy-done.47, ...), kind=kOutput, calls=%fused_computation.111 | convolution fusion | flops 6511656960 | bytes 50659328 | tf_op jit(solution)/shard_map/transpose(jvp(chts,cshp->cthp))/dot_general | solution.py:51
  1559.0 11.7 copy.466
  1570.7 14.9 copy.566
  1585.5 24.4 multiply_reduce_fusion.3
  1615.5 19.4 convolution_add_fusion.4
  1647.9 12.8 fusion.30
  1685.7 13.4 multiply_add_fusion.5
  1738.1 12.3 multiply_add_fusion.4
  1755.5 104.7 %fusion = bf16[8192,40]{0,1:T(8,128)(2,1)S(1)} fusion(bf16[8192,288]{0,1:T(8,128)(2,1)} %convert_element_type.166), kind=kCustom, calls=%all-reduce-scatter | all-reduce-scatter fusion | flops 2621441 | bytes 5374464
  1873.7 17.2 fusion.111
  1899.8 13.8 slice.259
  1913.6 17.4 pad_maximum_fusion.1
  1946.8 53.7 %all-gather.13.cloned.1.call-done = bf16[32768,512]{0,1:T(8,128)(2,1)} async-done(((bf16[8192,512]{0,1:T(8,128)(2,1)}), bf16[32768,512]{0,1:T(8,128)(2,1)}) %all-gather.13.cloned.1.call-update) | async-done | bytes 33554448 | tf_op jit(solution)/shard_map/all_gather | solution.py:275
  2000.5 28.0 fusion.148
  2028.5 25.6 convolution_add_fusion.1
  2054.1 381.9 %reduce-scatter.11.cloned.1.call-done = bf16[4096,384]{0,1:T(8,128)(2,1)} async-done(((bf16[32768,384]{0,1:T(8,128)(2,1)}), bf16[4096,384]{0,1:T(8,128)(2,1)}) %reduce-scatter.11.cloned.1.call-update) | async-done | bytes 3145744 | tf_op jit(solution)/shard_map/reduce_scatter | solution.py:223
  2438.5 15.2 all-gather.17.cloned.1.call-done
  2453.8 19.1 fusion.3
  2475.8 12.8 all-reduce.25.cloned.1.call-done
  2491.8 11.0 fusion.166
  2510.9 42.6 %reduce-scatter.19.cloned.1.call-done = bf16[256,16]{0,1:T(8,128)(2,1)} async-done(((bf16[256,128]{0,1:T(8,128)(2,1)}), bf16[256,16]{0,1:T(8,128)(2,1)}) %reduce-scatter.19.cloned.1.call-update) | async-done | bytes 8208 | tf_op jit(solution)/shard_map/reduce_scatter | solution.py:267
  2554.8 283.9 %reduce-scatter.17.cloned.1.call-done = bf16[4096,256]{0,1:T(8,128)(2,1)} async-done(((bf16[32768,256]{0,1:T(8,128)(2,1)}), bf16[4096,256]{0,1:T(8,128)(2,1)}) %reduce-scatter.17.cloned.1.call-update) | async-done | bytes 2097168 | tf_op jit(solution)/shard_map/reduce_scatter | solution.py:285
  (548 shorter events, 459.0 us)
Async XLA Ops:
  7.2 20.3 copy-start.50
  7.2 20.5 copy-start.29
  7.2 20.5 copy-start.93
  7.2 247.5 %copy-start.48 = (bf16[256,128]{1,0:T(8,128)(2,1)S(1)}, bf16[256,128]{1,0:T(8,128)(2,1)}, u32[]{:S(2)}) copy-start(bf16[256,128]{1,0:T(8,128)(2,1)} %param.36) | copy-start | bytes 196612
  7.2 247.5 %all-gather.7.cloned.1.call-start = ((), (), s32[]{:S(2)}) async-start(), calls=%async_computation.6 | async-start | bytes 18874368 | tf_op jit(solution)/shard_map/all_gather | solution.py:172
  10.3 274.2 %copy-start.11 = (bf16[4096,256]{0,1:T(8,128)(2,1)}, bf16[4096,256]{0,1:T(8,128)(2,1)S(1)}, u32[]{:S(2)}) copy-start(bf16[4096,256]{0,1:T(8,128)(2,1)S(1)} %copy.430) | copy-start | bytes 6291460
  26.6 456.0 %all-gather.11.cloned.1.call-start = ((), (), s32[]{:S(2)}) async-start(), calls=%async_computation.10 | async-start | bytes 18874368 | tf_op jit(solution)/shard_map/all_gather | solution.py:238
  27.4 867.4 %reduce-scatter.9.cloned.1.call-start = ((), (), s32[]{:S(2)}) async-start(), calls=%async_computation.7 | async-start | bytes 76021760 | tf_op jit(solution)/shard_map/reduce_scatter | solution.py:181
  27.7 296.3 %copy-start.87 = (s32[128]{0:T(128)}, s32[128]{0:T(128)S(1)}, u32[]{:S(2)}) copy-start(s32[128]{0:T(128)S(1)} %and_select_fusion) | copy-start | bytes 1540
  28.2 295.9 %copy-start.36 = (s32[32768]{0:T(1024)}, s32[32768]{0:T(1024)S(1)}, u32[]{:S(2)}) copy-start(s32[32768]{0:T(1024)S(1)} %select_reduce_fusion) | copy-start | bytes 393220
  374.3 108.3 %copy-start.39 = (bf16[256,256]{1,0:T(8,128)(2,1)S(1)}, bf16[256,256]{1,0:T(8,128)(2,1)}, u32[]{:S(2)}) copy-start(bf16[256,256]{1,0:T(8,128)(2,1)} %param.35) | copy-start | bytes 393220
  374.4 878.4 %reduce-scatter.13.cloned.1.call-start = ((), (), s32[]{:S(2)}) async-start(), calls=%async_computation.11 | async-start | bytes 31457280 | tf_op jit(solution)/shard_map/reduce_scatter | solution.py:240
  508.6 1365.0 %all-gather.9.cloned.1.call-start = ((), (), s32[]{:S(2)}) async-start(), calls=%async_computation.8 | async-start | bytes 20971520 | tf_op jit(solution)/shard_map/all_gather | solution.py:218
  509.6 388.7 %copy-start.53 = (pred[8192]{0:T(1024)(128)(4,1)}, pred[8192]{0:T(1024)(128)(4,1)S(1)}, u32[]{:S(2)}) copy-start(pred[8192]{0:T(1024)(128)(4,1)S(1)} %get-tuple-element.456) | copy-start | bytes 24580
  509.6 388.7 %copy-start.55 = (pred[8192]{0:T(1024)(128)(4,1)}, pred[8192]{0:T(1024)(128)(4,1)S(1)}, u32[]{:S(2)}) copy-start(pred[8192]{0:T(1024)(128)(4,1)S(1)} %get-tuple-element.457) | copy-start | bytes 24580
  512.4 385.9 %copy-start.96 = (f32[4]{0:T(128)}, f32[4]{0:T(128)S(1)}, u32[]{:S(2)}) copy-start(f32[4]{0:T(128)S(1)} %exponential_negate_fusion) | copy-start | bytes 52
  513.0 520.9 %copy-start.70 = (f32[1,256]{1,0:T(1,128)}, f32[1,256]{1,0:T(1,128)S(1)}, u32[]{:S(2)}) copy-start(f32[1,256]{1,0:T(1,128)S(1)} %get-tuple-element.448) | copy-start | bytes 3076
  513.6 388.3 %copy-start.94 = (f32[4]{0:T(128)S(1)}, f32[4]{0:T(128)}, u32[]{:S(2)}) copy-start(f32[4]{0:T(128)} %param.31) | copy-start | bytes 52
  906.5 49.7 %copy-start.24 = (f32[32,4,256]{0,1,2:T(4,128)}, f32[32,4,256]{0,1,2:T(4,128)S(1)}, u32[]{:S(2)}) copy-start(f32[32,4,256]{0,1,2:T(4,128)S(1)} %copy.441) | copy-start | bytes 393220
  957.6 116.3 %copy-start.32 = (f32[32,4,256]{2,1,0:T(4,128)}, f32[32,4,256]{2,1,0:T(4,128)S(1)}, u32[]{:S(2)}) copy-start(f32[32,4,256]{2,1,0:T(4,128)S(1)} %copy.446) | copy-start | bytes 393220
  1179.1 66.2 %slice-start.4 = ((s8[8388608]{0:T(1024)(128)(4,1)}), s8[4194304]{0:T(1024)(128)(4,1)S(1)}, s32[]{:S(2)}) async-start(s8[8388608]{0:T(1024)(128)(4,1)} %bitcast.277), calls=%async_computation.23 | async-start | bytes 8388608
  1188.4 56.9 %slice-start.5 = ((s8[8388608]{0:T(1024)(128)(4,1)}), s8[4194304]{0:T(1024)(128)(4,1)S(1)}, s32[]{:S(2)}) async-start(s8[8388608]{0:T(1024)(128)(4,1)} %bitcast.277), calls=%async_computation.24 | async-start | bytes 8388608
  1329.7 602.5 %reduce-scatter.15.cloned.1.call-start = ((), (), s32[]{:S(2)}) async-start(), calls=%async_computation.14 | async-start | bytes 2359296 | tf_op jit(solution)/shard_map/reduce_scatter | solution.py:264
  1404.1 63.3 %copy-start.61 = (f32[16,2,4]{2,1,0:T(2,128)}, f32[16,2,4]{2,1,0:T(2,128)S(1)}, u32[]{:S(2)}) copy-start(f32[16,2,4]{2,1,0:T(2,128)S(1)} %get-tuple-element.181) | copy-start | bytes 1540
  1404.1 63.3 %copy-start.10 = (f32[8192,128]{0,1:T(8,128)S(1)}, f32[8192,128]{0,1:T(8,128)}, u32[]{:S(2)}) copy-start(f32[8192,128]{0,1:T(8,128)} %get-tuple-element.427) | copy-start | bytes 12582916
  1559.0 26.5 slice-start.6
  1647.9 29.6 %copy-start.1 = (f32[8192,256]{0,1:T(8,128)}, f32[8192,256]{0,1:T(8,128)S(1)}, u32[]{:S(2)}) copy-start(f32[8192,256]{0,1:T(8,128)S(1)} %fusion.34) | copy-start | bytes 25165828
  1711.4 289.1 %all-gather.13.cloned.1.call-start = ((), (), s32[]{:S(2)}) async-start(), calls=%async_computation.12 | async-start | bytes 41943040 | tf_op jit(solution)/shard_map/all_gather | solution.py:275
  1712.1 316.4 %all-gather.15.cloned.1.call-start = ((), (), s32[]{:S(2)}) async-start(), calls=%async_computation.13 | async-start | bytes 3276800 | tf_op jit(solution)/shard_map/all_gather | solution.py:276
  1720.4 17.7 copy-start.85
  1752.7 112.1 %copy-start.46 = (bf16[128,256]{1,0:T(8,128)(2,1)S(1)}, bf16[128,256]{1,0:T(8,128)(2,1)}, u32[]{:S(2)}) copy-start(bf16[128,256]{1,0:T(8,128)(2,1)} %param.38) | copy-start | bytes 196612
  1752.7 112.2 %copy-start.101 = (u32[32]{0:T(128)S(1)}, u32[32]{0:T(128)}, u32[]{:S(2)}) copy-start(u32[32]{0:T(128)} %constant.246) | copy-start | bytes 388
  1755.5 118.1 %copy-start.40 = (bf16[256,256]{1,0:T(8,128)(2,1)S(1)}, bf16[256,256]{1,0:T(8,128)(2,1)}, u32[]{:S(2)}) copy-start(bf16[256,256]{1,0:T(8,128)(2,1)} %param.35) | copy-start | bytes 393220
  1860.3 11.1 collective-permute-start
  1873.4 17.5 copy-start.37
  1873.4 17.5 copy-start.89
  1873.4 562.5 %reduce-scatter.11.cloned.1.call-start = ((), (), s32[]{:S(2)}) async-start(), calls=%async_computation.9 | async-start | bytes 28311552 | tf_op jit(solution)/shard_map/reduce_scatter | solution.py:223
  1931.0 522.8 %all-gather.17.cloned.1.call-start = ((), (), s32[]{:S(2)}) async-start(), calls=%async_computation.15 | async-start | bytes 1310720 | tf_op jit(solution)/shard_map/all_gather | solution.py:277
  1934.0 554.7 %all-reduce.25.cloned.1.call-start = ((), (), s32[]{:S(2)}) async-start(), calls=%async_computation.18 | async-start | bytes 393216 | tf_op jit(solution)/shard_map/psum | solution.py:297
  1934.0 66.4 %copy-start.30 = (bf16[256,4,128]{2,1,0:T(4,128)(2,1)S(1)}, bf16[256,4,128]{2,1,0:T(4,128)(2,1)}, u32[]{:S(2)}) copy-start(bf16[256,4,128]{2,1,0:T(4,128)(2,1)} %param.25) | copy-start | bytes 786436
  1946.7 606.8 %reduce-scatter.19.cloned.1.call-start = ((), (), s32[]{:S(2)}) async-start(), calls=%async_computation.17 | async-start | bytes 73728 | tf_op jit(solution)/shard_map/reduce_scatter | solution.py:267
  2028.5 407.5 %copy-start.26 = (bf16[4096,256]{1,0:T(8,128)(2,1)S(1)}, bf16[4096,256]{1,0:T(8,128)(2,1)}, u32[]{:S(2)}) copy-start(bf16[4096,256]{1,0:T(8,128)(2,1)} %param.41) | copy-start | bytes 6291460
  2028.5 425.3 %copy-start.49 = (bf16[256,128]{1,0:T(8,128)(2,1)S(1)}, bf16[256,128]{1,0:T(8,128)(2,1)}, u32[]{:S(2)}) copy-start(bf16[256,128]{1,0:T(8,128)(2,1)} %param.36) | copy-start | bytes 196612
  2438.2 400.4 %reduce-scatter.17.cloned.1.call-start = ((), (), s32[]{:S(2)}) async-start(), calls=%async_computation.16 | async-start | bytes 18874368 | tf_op jit(solution)/shard_map/reduce_scatter | solution.py:285
  2472.9 18.9 copy-start.31
  2502.7 336.0 %copy-start.86 = (f32[256]{0:T(256)S(1)}, f32[256]{0:T(256)}, u32[]{:S(2)}) copy-start(f32[256]{0:T(256)} %param.24) | copy-start | bytes 3076
  2502.7 345.6 %copy-start.52 = (f32[4096]{0:T(1024)S(1)}, f32[4096]{0:T(1024)}, u32[]{:S(2)}) copy-start(f32[4096]{0:T(1024)} %copy-done.51) | copy-start | bytes 49156
  2502.7 345.6 %copy-start.60 = (f32[4096]{0:T(1024)S(1)}, f32[4096]{0:T(1024)}, u32[]{:S(2)}) copy-start(f32[4096]{0:T(1024)} %get-tuple-element.436) | copy-start | bytes 49156
  (77 other events, 588.3 us)
Sparse Core Ops, SparseCore 0:
  26.8 227.8 all-gather.6
  256.8 225.7 all-gather.10
  485.2 409.5 reduce-scatter.8
  897.5 180.4 reduce-scatter.12
  1329.8 102.6 all-gather.8
  1711.5 85.6 reduce-scatter.14
  1798.8 201.6 all-gather.12
  2002.0 25.5 all-gather.14
  2031.5 404.3 reduce-scatter.10
  2437.9 15.8 all-gather.16
  2456.8 31.7 all-reduce.24
  2492.3 61.2 reduce-scatter.18
  2557.8 280.8 reduce-scatter.16
where the time goes:
time: 2870 us
  waiting for transfers between devices  1510 us (53%)
  matrix products  498 us (17%)
  other arithmetic  375 us (13%)
  local copies, waits for them, and re-layouts  296 us (10%)
  blocking collectives  162 us (6%)
    reduce_scatter x1, waiting for transfers between devices, per_device(): lax.psum_scatter(jnp.concatenate([product[:, :width_rows], product[:, wid...  382 us
    reduce_scatter x1, waiting for transfers between devices, per_device(): lax.psum_scatter(front_product(rows_in, front_weight, jnp.int32(0), adapt...  381 us
    reduce_scatter x1, waiting for transfers between devices, per_device(): lax.psum_scatter((summed + jnp.einsum('te,de->td', adapt_all, down_cut, p...  284 us
    all_gather x1, waiting for transfers between devices, per_device(): normed_all = lax.all_gather(normed, 'col', axis=0, tiled=True)  227 us
    dot_general x3, matrix products, scan_blocks(): jnp.einsum('chts,cshp->cthp', weights, value_block, precision=HIGHEST)  152 us
    all_gather x1, waiting for transfers between devices, per_device(): cot_all = lax.all_gather(cotangent, 'col', axis=0, tiled=True)  107 us
    unnamed x1, blocking collectives  105 us
    unnamed x241, local copies, waits for them, and re-layouts  80.5 us
  transfers between devices with their start and end apart: 14, of which 10 were waited for; matrix products, arithmetic and copies ran while one was open for 41% of the time, Pallas kernels for 0%

commit v1 on v0

v1 whole, which is shorter than its diff:
```python
import functools

import jax
import jax.numpy as jnp
from jax import lax
from jax.experimental import pallas as pl
from jax.experimental.pallas import tpu as pltpu
from jax.sharding import PartitionSpec as P

D = 1024
HEADS = 32
P_SIZE = 64
STATES = 128
BLOCK = 256
RANK = 16
SEQ = 4096
DI = 2048
EPS = 1e-05
LOG2E = 1.4426950408889634

HALO = 16
QUAD = 4
WIDTH = QUAD * P_SIZE
GROUPS = HEADS // QUAD
LANES = 128
VMEM_BYTES = 60 * 1024 * 1024
F32 = jnp.float32
BF16 = jnp.bfloat16


def mm(left, right):
    return jnp.dot(left, right, preferred_element_type=F32)


def mm_nt(left, right):
    return lax.dot_general(left, right, (((1,), (1,)), ((), ())), preferred_element_type=F32)


def mm_tn(left, right):
    return lax.dot_general(left, right, (((0,), (0,)), ((), ())), preferred_element_type=F32)


def split_left(ones, value):
    high = value.astype(BF16)
    rest = value - high.astype(F32)
    middle = rest.astype(BF16)
    low = (rest - middle.astype(F32)).astype(BF16)
    return mm(ones, high) + mm(ones, middle) + mm(ones, low)


def split_right(value, ones):
    high = value.astype(BF16)
    low = (value - high.astype(F32)).astype(BF16)
    return mm(high, ones) + mm(low, ones)


def sigmoid(value):
    return 0.5 * jnp.tanh(0.5 * value) + 0.5


def iota(shape, axis):
    return lax.broadcasted_iota(jnp.int32, shape, axis)


def widen(cols):
    lane = iota((cols.shape[0], LANES), 1) < P_SIZE
    left = jnp.where(lane, cols[:, 0:1], cols[:, 1:2])
    right = jnp.where(lane, cols[:, 2:3], cols[:, 3:4])
    return jnp.concatenate([left, right], axis=1)


def to_front(cols, group):
    return pltpu.roll(cols, lax.rem(LANES - QUAD * group, LANES), 1)


def head_only(values, head):
    lane = iota(values.shape, 1) // P_SIZE
    return jnp.where(lane == head, values, jnp.zeros_like(values))


def delays(window, taps, bias):
    total = window[8:] * taps[0:1] + bias
    for k in range(1, 4):
        total = total + pltpu.roll(window, k, 0)[8:] * taps[k : k + 1]
    return total


def advances(window, taps, count):
    length = window.shape[0]
    total = window[:count] * taps[0:1]
    for k in range(1, 4):
        total = total + pltpu.roll(window, length - k, 0)[:count] * taps[k : k + 1]
    return total


def at_block(k):
    return pl.ds(pl.multiple_of(k * BLOCK, BLOCK), BLOCK)


def at_rows(k):
    return pl.ds(pl.multiple_of(HALO + k * BLOCK, HALO), BLOCK)


def front_kernel(
    x_ref, gain_ref, wst_ref, sp_ref, hp_ref, w_ref, up_ref, vp_ref,
    normed_ref, scpre_ref, raw_ref, step_ref, cum_ref, cum_t_ref, bs_ref, cs_ref, cs_t_ref, adv_ref,
    gate_ref, u_ref, eloc_ref, fin_ref, dec_ref,
    st_scr, bs_t_scr, val_scr,
):
    group = pl.program_id(0)
    row_count, _, part = x_ref.shape
    blocks = eloc_ref.shape[0]

    @pl.when(group == 0)
    def _():
        def project(rows):
            pieces = [x_ref[r, rows, :].astype(F32) for r in range(row_count)]
            square = sum(jnp.sum(piece * piece, axis=1, keepdims=True) for piece in pieces)
            inv = lax.rsqrt(square / D + EPS)
            total = None
            for r in range(row_count):
                normed = (pieces[r] * inv * gain_ref[r]).astype(BF16)
                normed_ref[rows, r * part : (r + 1) * part] = normed
                term = mm(normed, wst_ref[r])
                total = term if total is None else total + term
            st_scr[rows, :] = total
            adv_ref[rows, :] = total[:, 384:512].astype(BF16)

        project(pl.ds(0, HALO))

        @pl.loop(0, blocks)
        def _(k):
            project(at_rows(k))

        lower = (iota((BLOCK, BLOCK), 0) >= iota((BLOCK, BLOCK), 1)).astype(BF16)
        rate = -jnp.exp(hp_ref[1:2]) * LOG2E

        @pl.loop(0, blocks)
        def _(k):
            window = st_scr[pl.ds(pl.multiple_of(8 + k * BLOCK, 8), BLOCK + 8), :256]
            pre = delays(window, sp_ref[0:4], sp_ref[4:5])
            conv = pre * sigmoid(pre)
            b_rows = conv[:, :STATES].astype(BF16)
            c_rows = conv[:, STATES:].astype(BF16)
            scpre_ref[at_block(k), :] = pre
            bs_ref[at_block(k), :] = b_rows
            cs_ref[at_block(k), :] = c_rows
            bs_t_scr[k] = conv[:, :STATES].T.astype(BF16)
            cs_t_ref[k] = conv[:, STATES:].T.astype(BF16)
            raw = st_scr[at_rows(k), 256:384] + hp_ref[0:1]
            small = jnp.exp(-jnp.abs(raw))
            tail = jnp.where(
                small < 0.01, small * (1.0 - small * (0.5 - small * (1.0 / 3.0))), jnp.log(1.0 + small)
            )
            step = jnp.maximum(raw, 0.0) + tail
            cum = split_left(lower, step * rate)
            raw_ref[at_block(k), :] = raw
            step_ref[at_block(k), :] = step
            cum_ref[at_block(k), :] = cum
            flipped = cum.T
            for g in range(GROUPS):
                cum_t_ref[g, :, at_block(k)] = flipped[g * QUAD : (g + 1) * QUAD]

    def inner(rows):
        total = mm(adv_ref[rows, :], up_ref[0])
        for r in range(row_count):
            total = total + mm(normed_ref[rows, r * part : (r + 1) * part], w_ref[0, r, :part, :])
        return total

    val_scr[0:HALO, :] = inner(pl.ds(0, HALO))[:, WIDTH:]
    taps = vp_ref[0]

    def one_block(k, carry):
        state, decay = carry
        product = inner(at_rows(k))
        gate_ref[at_block(k), :] = product[:, :WIDTH].astype(BF16)
        val_scr[at_rows(k), :] = product[:, WIDTH:]
        window = val_scr[pl.ds(pl.multiple_of(8 + k * BLOCK, 8), BLOCK + 8), :]
        pre = delays(window, taps[0:4], taps[4:5])
        u_ref[at_block(k), :] = pre.astype(BF16)
        xs = (pre * sigmoid(pre)).astype(BF16).astype(F32)
        cum = cum_ref[at_block(k), :]
        last = cum[BLOCK - 1 : BLOCK]
        weight = to_front(step_ref[at_block(k), :] * jnp.exp2(last - cum), group)
        weighted = (xs * widen(weight)).astype(BF16)
        eloc_ref[k] = state
        last8 = to_front(jnp.broadcast_to(last, (8, LANES)), group)
        fall = widen(jnp.exp2(last8))[0:1]
        return fall * state + mm(bs_t_scr[k], weighted), decay * fall

    start = (jnp.zeros((STATES, WIDTH), F32), jnp.ones((1, WIDTH), F32))
    state, decay = lax.fori_loop(0, blocks, one_block, start)
    fin_ref[...] = state.astype(BF16)
    dec_ref[...] = jnp.broadcast_to(decay, (8, WIDTH))


def scan_kernel(
    x_ref, g_ref, oup_ref, w_ref, down_ref, vp_ref, gate_ref, u_ref, eloc_ref, ein_ref,
    step_ref, cum_ref, cum_t_ref, bs_ref, cs_ref,
    out_ref, o_ref, ent_ref, aux_ref, sg_ref, gup_ref,
    score_scr, acc_scr, side_scr, square_scr,
):
    group = pl.program_id(0)
    row_count, _, part = x_ref.shape
    blocks = eloc_ref.shape[0]

    @pl.when(group == 0)
    def _():
        acc_scr[...] = jnp.zeros_like(acc_scr)
        side_scr[...] = jnp.zeros_like(side_scr)
        square_scr[...] = jnp.zeros_like(square_scr)
        keep = iota((BLOCK, BLOCK), 0) >= iota((BLOCK, BLOCK), 1)

        @pl.loop(0, blocks)
        def _(k):
            score = mm_nt(cs_ref[at_block(k), :], bs_ref[at_block(k), :])
            score_scr[k] = jnp.where(keep, score, 0.0)

    taps = vp_ref[0]

    def one_block(k, before):
        rows = at_block(k)
        pre = u_ref[rows, :].astype(F32)
        conv = pre * sigmoid(pre)
        cum = to_front(cum_ref[rows, :], group)
        step = to_front(step_ref[rows, :], group)
        scaled = (conv.astype(BF16).astype(F32) * widen(step)).astype(BF16)
        score = score_scr[k]
        entering = (eloc_ref[k] + before * ein_ref[...]).astype(BF16)
        ent_ref[k] = entering
        total = widen(jnp.exp2(cum)) * mm(cs_ref[rows, :], entering)
        for h in range(QUAD):
            spread = cum[:, h : h + 1] - cum_t_ref[0, h : h + 1, rows]
            weights = (score * jnp.exp2(jnp.minimum(spread, 0.0))).astype(BF16)
            total = total + mm(weights, head_only(scaled, h))
        output = total + taps[6:7] * conv
        o_ref[rows, :] = output.astype(BF16)
        gate = gate_ref[rows, :].astype(F32)
        gated = output * gate * sigmoid(gate)
        square = gated * gated
        square_scr[rows, :] += square[:, :LANES] + square[:, LANES:]
        gained = (gated * taps[5:6]).astype(BF16)
        for r in range(row_count):
            cols = slice(r * part, (r + 1) * part)
            acc_scr[rows, cols] += mm(gained, w_ref[0, r, :, :part])
        side_scr[rows, :] += mm(gained, down_ref[0])
        return before * widen(jnp.exp2(cum[BLOCK - 8 :]))[7:8]

    lax.fori_loop(0, blocks, one_block, jnp.ones((1, WIDTH), F32))

    @pl.when(group == pl.num_programs(0) - 1)
    def _():
        gup_ref[...] = jnp.zeros_like(gup_ref)

        @pl.loop(0, blocks)
        def _(k):
            rows = at_block(k)
            mean = jnp.sum(square_scr[rows, :], axis=1, keepdims=True) / DI
            rms = lax.rsqrt(mean + EPS)
            side_raw = side_scr[rows, :]
            side = (side_raw * rms).astype(BF16)
            side_grad = None
            for r in range(row_count):
                term = mm(g_ref[r, rows, :], oup_ref[r])
                side_grad = term if side_grad is None else side_grad + term
            side_grad = side_grad.astype(BF16)
            product = jnp.sum(side_grad.astype(F32) * side_raw, axis=1, keepdims=True)
            for r in range(row_count):
                cols = slice(r * part, (r + 1) * part)
                raw = acc_scr[rows, cols]
                cot = g_ref[r, rows, :]
                product = product + jnp.sum(raw * cot.astype(F32), axis=1, keepdims=True)
                total = x_ref[r, at_rows(k), :].astype(F32) + raw * rms + mm_nt(side, oup_ref[r])
                out_ref[r, rows, :] = total.astype(BF16)
                gup_ref[:, cols] += mm_tn(side, cot)[:RANK]
            coefficient = rms * rms * rms * product / DI
            lane = iota((BLOCK, LANES), 1)
            aux_ref[rows, :] = jnp.where(lane == 0, rms, coefficient)
            sg_ref[rows, :] = side_grad


def gate_kernel(
    g_ref, w_ref, sg_ref, down_ref, vp_ref, gate_ref, o_ref, aux_ref, cum_ref, cs_t_ref,
    dgate_ref, dy_ref, gloc_ref, gfin_ref, gdown_ref,
    sg_t_scr,
):
    group = pl.program_id(0)
    row_count, _, part = g_ref.shape
    blocks = gloc_ref.shape[0]

    @pl.when(group == 0)
    def _():
        @pl.loop(0, blocks)
        def _(k):
            sg_t_scr[k] = sg_ref[at_block(k), :].astype(F32).T[:RANK].astype(BF16)

    taps = vp_ref[0]
    gdown_ref[...] = jnp.zeros_like(gdown_ref)

    def one_block(i, state):
        k = blocks - 1 - i
        rows = at_block(k)
        dmix = mm_nt(sg_ref[rows, :], down_ref[0])
        for r in range(row_count):
            dmix = dmix + mm_nt(g_ref[r, rows, :], w_ref[0, r, :, :part])
        gate = gate_ref[rows, :].astype(F32)
        output = o_ref[rows, :].astype(F32)
        sig = sigmoid(gate)
        act = gate * sig
        gated = output * act
        rms = aux_ref[rows, 0:1]
        coefficient = aux_ref[rows, 1:2]
        scale = rms * taps[5:6]
        mixed = (gated * scale).astype(BF16)
        gdown_ref[...] += mm(sg_t_scr[k], mixed)
        gated_grad = scale * dmix - gated * coefficient
        dy = gated_grad * act
        dgate = gated_grad * output * (sig + act * (1.0 - sig))
        dgate_ref[rows, :] = dgate.astype(BF16)
        dy_ref[rows, :] = dy.astype(BF16)
        cum = to_front(cum_ref[rows, :], group)
        factor = widen(jnp.exp2(cum))
        gloc_ref[k] = state
        return factor[BLOCK - 1 : BLOCK] * state + mm(cs_t_ref[k], (factor * dy).astype(BF16))

    state = lax.fori_loop(0, blocks, one_block, jnp.zeros((STATES, WIDTH), F32))
    gfin_ref[...] = state.astype(BF16)


def back_kernel(
    x_ref, gain_ref, normed_ref, wst_ref, w_ref, up_ref, adv_ref, vp_ref, sp_ref, hp_ref,
    u_ref, o_ref, dy_ref, dgate_ref, ent_ref, gloc_ref, gin_ref,
    step_ref, cum_ref, cum_t_ref, raw_ref, scpre_ref, bs_ref, cs_ref,
    corr_ref, gup_ref, gdown_ref,
    score_scr, dscore_scr, db_scr, dc_scr, dcum_scr, dstep_scr, dlast_scr, du_scr, ig_scr, ng_scr, adg_scr, adv_t_scr,
):
    group = pl.program_id(0)
    row_count, _, part = x_ref.shape
    blocks = gloc_ref.shape[0]
    total_rows = normed_ref.shape[0]

    @pl.when(group == 0)
    def _():
        for ref in (dscore_scr, db_scr, dc_scr, dcum_scr, dstep_scr, dlast_scr, ng_scr, adg_scr):
            ref[...] = jnp.zeros_like(ref)
        du_scr[0:HALO, :] = jnp.zeros((HALO, WIDTH), F32)
        du_scr[total_rows : total_rows + HALO, :] = jnp.zeros((HALO, WIDTH), F32)

        @pl.loop(0, blocks)
        def _(k):
            score_scr[k] = mm_nt(bs_ref[at_block(k), :], cs_ref[at_block(k), :])
            adv_t_scr[k] = adv_ref[at_rows(k), :].astype(F32).T[:RANK].astype(BF16)

    keep = iota((BLOCK, BLOCK), 0) <= iota((BLOCK, BLOCK), 1)
    taps = vp_ref[0]
    pick = (iota((WIDTH, LANES), 1) == QUAD * group + iota((WIDTH, LANES), 0) // P_SIZE).astype(BF16)

    def one_block(i, after):
        k = blocks - 1 - i
        rows = at_block(k)
        pre = u_ref[rows, :].astype(F32)
        sig = sigmoid(pre)
        conv = pre * sig
        xs = conv.astype(BF16).astype(F32)
        cum = to_front(cum_ref[rows, :], group)
        step_w = widen(to_front(step_ref[rows, :], group))
        scaled_low = (xs * step_w).astype(BF16)
        scaled = scaled_low.astype(F32)
        dy_low = dy_ref[rows, :]
        dy = dy_low.astype(F32)
        b_rows = bs_ref[rows, :]
        c_rows = cs_ref[rows, :]
        score = jnp.where(keep, score_scr[k], 0.0)
        dscore = dscore_scr[k]
        ending = gloc_ref[k] + after * gin_ref[...]
        ending_low = ending.astype(BF16)
        last = cum[BLOCK - 1 : BLOCK]
        to_end = widen(jnp.exp2(last - cum))
        dscaled_state = to_end * mm(b_rows, ending_low)
        dscaled = dscaled_state
        for h in range(QUAD):
            spread = cum_t_ref[0, h : h + 1, rows] - cum[:, h : h + 1]
            damp = jnp.exp2(jnp.minimum(spread, 0.0))
            weights = (score * damp).astype(BF16)
            dy_head = head_only(dy_low, h)
            dscaled = dscaled + mm(weights, dy_head)
            dscore = dscore + mm_nt(scaled_low, dy_head) * damp
        dscore_scr[k] = dscore
        from_start = widen(jnp.exp2(cum))
        fall = from_start[BLOCK - 1 : BLOCK]
        entering_low = ent_ref[k]
        entering = entering_low.astype(F32)
        dc_scr[rows, :] += mm_nt((from_start * dy).astype(BF16), entering_low)
        db_scr[rows, :] += mm_nt((to_end * scaled).astype(BF16), ending_low)
        scan_out = o_ref[rows, :].astype(F32) - taps[6:7] * conv
        dcum_scr[rows, :] += split_right(dy * scan_out - scaled * dscaled, pick)
        dstep_scr[rows, :] += split_right(xs * dscaled, pick)
        ends = jnp.sum(scaled * dscaled_state, axis=0, keepdims=True)
        ends = ends + fall * jnp.sum(entering * ending, axis=0, keepdims=True)
        dlast_scr[k] += split_right(jnp.broadcast_to(ends, (8, WIDTH)), pick)
        dconv = taps[6:7] * dy + step_w * dscaled
        du_scr[at_rows(k), :] = dconv * (sig + conv * (1.0 - sig))
        return after * fall

    lax.fori_loop(0, blocks, one_block, jnp.ones((1, WIDTH), F32))

    def spread_back(rows, window, count):
        dval = advances(window, taps[0:4], count)
        ig_scr[rows, WIDTH:] = dval.astype(BF16)
        grad = ig_scr[rows, :]
        adg_scr[rows, :] += mm_nt(grad, up_ref[0])
        for r in range(row_count):
            ng_scr[rows, r * part : (r + 1) * part] += mm_nt(grad, w_ref[0, r, :part, :])
        return grad

    ig_scr[0:HALO, :WIDTH] = jnp.zeros((HALO, WIDTH), BF16)
    first = spread_back(pl.ds(0, HALO), du_scr[0 : HALO + 8, :], HALO)
    gup_ref[0] = mm_tn(adv_ref[0:HALO, :], first)[:RANK]

    @pl.loop(0, blocks)
    def _(k):
        ig_scr[at_rows(k), :WIDTH] = dgate_ref[at_block(k), :]
        window = du_scr[pl.ds(pl.multiple_of(HALO + k * BLOCK, 8), BLOCK + 8), :]
        grad = spread_back(at_rows(k), window, BLOCK)
        gup_ref[0] += mm(adv_t_scr[k], grad)

    @pl.when(group == pl.num_programs(0) - 1)
    def _():
        upper = (iota((BLOCK, BLOCK), 0) <= iota((BLOCK, BLOCK), 1)).astype(BF16)
        rate = -jnp.exp(hp_ref[1:2])

        @pl.loop(0, blocks)
        def _(k):
            rows = at_block(k)
            dscore = jnp.where(keep, dscore_scr[k], 0.0).astype(BF16)
            db = db_scr[rows, :] + mm(dscore, cs_ref[rows, :])
            dc = dc_scr[rows, :] + mm_tn(dscore, bs_ref[rows, :])
            pre = scpre_ref[rows, :]
            sig = sigmoid(pre)
            slope = sig + pre * sig * (1.0 - sig)
            du_scr[at_rows(k), :] = jnp.concatenate([db, dc], axis=1) * slope
            is_last = iota((BLOCK, LANES), 0) == BLOCK - 1
            dcum = dcum_scr[rows, :] + jnp.where(is_last, dlast_scr[k, 0:1, :], 0.0)
            dstep = dstep_scr[rows, :] + split_left(upper, dcum) * rate
            dstep_scr[rows, :] = dstep * sigmoid(raw_ref[rows, :])

        def finish(rows, window, count, draw):
            dstate = advances(window, sp_ref[0:4], count).astype(BF16)
            adapt = adg_scr[rows, :].astype(BF16)
            total = jnp.zeros((count, 1), F32)
            square = jnp.zeros((count, 1), F32)
            grads = []
            for r in range(row_count):
                cols = slice(r * part, (r + 1) * part)
                grad = ng_scr[rows, cols] + mm_nt(dstate, wst_ref[r, :, 0:256])
                grad = grad + mm_nt(adapt, wst_ref[r, :, 384:512])
                if draw is not None:
                    grad = grad + mm_nt(draw, wst_ref[r, :, 256:384])
                grad = grad * gain_ref[r]
                piece = x_ref[r, rows, :].astype(F32)
                total = total + jnp.sum(piece * grad, axis=1, keepdims=True)
                square = square + jnp.sum(piece * piece, axis=1, keepdims=True)
                grads.append(grad)
                gdown_ref[:, cols] += mm_tn(adapt, normed_ref[rows, cols])[:RANK]
            inv = lax.rsqrt(square / D + EPS)
            factor = inv * inv * inv * total / D
            for r in range(row_count):
                piece = x_ref[r, rows, :].astype(F32)
                corr_ref[r, rows, :] = (inv * grads[r] - factor * piece).astype(BF16)

        gdown_ref[...] = jnp.zeros_like(gdown_ref)
        finish(pl.ds(0, HALO), du_scr[0 : HALO + 8, :], HALO, None)

        @pl.loop(0, blocks)
        def _(k):
            window = du_scr[pl.ds(pl.multiple_of(HALO + k * BLOCK, 8), BLOCK + 8), :]
            finish(at_rows(k), window, BLOCK, dstep_scr[at_block(k), :].astype(BF16))


def whole_spec(shape):
    return pl.BlockSpec(shape, lambda c: (0,) * len(shape))


def lead_spec(shape):
    return pl.BlockSpec((1,) + tuple(shape[1:]), lambda c: (c,) + (0,) * (len(shape) - 1))


def lane_spec(shape):
    block = tuple(shape[:-1]) + (WIDTH,)
    return pl.BlockSpec(block, lambda c: (0,) * (len(shape) - 1) + (c,))


KINDS = {"a": whole_spec, "c": lead_spec, "l": lane_spec}


def grouped_call(kernel, inputs, kinds, outputs, out_kinds, scratch):
    return pl.pallas_call(
        kernel,
        grid=(GROUPS,),
        in_specs=[KINDS[kind](value.shape) for kind, value in zip(kinds, inputs)],
        out_specs=[KINDS[kind](shape) for kind, (shape, _) in zip(out_kinds, outputs)],
        out_shape=[jax.ShapeDtypeStruct(shape, dtype) for shape, dtype in outputs],
        scratch_shapes=[pltpu.VMEM(shape, dtype) for shape, dtype in scratch],
        compiler_params=pltpu.CompilerParams(vmem_limit_bytes=VMEM_BYTES),
    )(*inputs)


def to_groups(value, heads_here):
    cols = value.shape[0]
    middle = value.shape[1:-1]
    if heads_here == QUAD:
        return value
    if heads_here > QUAD:
        parts = heads_here // QUAD
        value = value.reshape((cols,) + middle + (parts, WIDTH))
        value = jnp.moveaxis(value, -2, 1)
        return value.reshape((GROUPS,) + middle + (WIDTH,))
    parts = QUAD // heads_here
    value = value.reshape((GROUPS, parts) + middle + (heads_here * P_SIZE,))
    value = jnp.moveaxis(value, 1, -2)
    return value.reshape((GROUPS,) + middle + (WIDTH,))


def to_cols(value, heads_here, col_count):
    middle = value.shape[1:-1]
    if heads_here == QUAD:
        return value
    if heads_here > QUAD:
        parts = heads_here // QUAD
        value = value.reshape((col_count, parts) + middle + (WIDTH,))
        value = jnp.moveaxis(value, 1, -2)
        return value.reshape((col_count,) + middle + (heads_here * P_SIZE,))
    parts = QUAD // heads_here
    value = value.reshape((GROUPS,) + middle + (parts, heads_here * P_SIZE))
    value = jnp.moveaxis(value, -2, 1)
    return value.reshape((col_count,) + middle + (heads_here * P_SIZE,))


def pad_lanes(value, width):
    return jnp.pad(value, [(0, 0)] * (value.ndim - 1) + [(0, width - value.shape[-1])])


def carry_in(state, decay, row_count, col_count, seq_cols, forward):
    row = lax.axis_index("row")
    col = lax.axis_index("col")
    total = state
    factor = decay
    before = jnp.zeros(state.shape, F32)
    reach = jnp.ones_like(decay)
    span = 1
    while span < row_count:
        pairs = [(i, i ^ span) for i in range(row_count)]
        other = lax.ppermute(total, "row", pairs).astype(F32)
        other_factor = lax.ppermute(factor, "row", pairs)
        behind = ((row & span) != 0) == forward
        mine = total.astype(F32)
        before = jnp.where(behind, before + reach * other, before)
        reach = jnp.where(behind, reach * other_factor, reach)
        joined = jnp.where(behind, other * factor + mine, mine * other_factor + other)
        total = joined.astype(BF16)
        factor = factor * other_factor
        span *= 2
    place = lax.rem(col, seq_cols)
    for hop in range(1, seq_cols):
        shift = hop if forward else -hop
        pairs = [(i, (i + shift) % col_count) for i in range(col_count)]
        other = lax.ppermute(total, "col", pairs).astype(F32)
        other_factor = lax.ppermute(factor, "col", pairs)
        inside = place >= hop if forward else place < seq_cols - hop
        before = jnp.where(inside, before + reach * other, before)
        reach = jnp.where(inside, reach * other_factor, reach)
    return before


def per_device(
    block_in, norm_gain, proj_inner, proj_state, conv_inner, conv_inner_bias, conv_state, conv_state_bias,
    step_bias, decay_log, skip_gain, gate_gain, proj_out, adapt_in_down, adapt_in_up, adapt_out_down,
    adapt_out_up, adapter_id, cotangent,
):
    row_count = lax.axis_size("row")
    col_count = lax.axis_size("col")
    row = lax.axis_index("row")
    col = lax.axis_index("col")
    col_tokens, part = block_in.shape
    chunk = col_tokens // row_count
    total_rows = chunk + HALO
    blocks = chunk // BLOCK
    seq_cols = SEQ // col_tokens
    heads_here = proj_inner.shape[1]
    local = heads_here * P_SIZE
    rank_total = adapt_in_down.shape[1]
    rank_part = rank_total // row_count
    rank_share = rank_total // col_count
    adapter = lax.dynamic_index_in_dim(adapter_id, col // seq_cols, keepdims=False)

    head = jnp.zeros((HALO, part), BF16)
    if seq_cols > 1:
        pairs = [(i, (i + 1) % col_count) for i in range(col_count)]
        head = lax.ppermute(block_in[-HALO:], "col", pairs)
        head = jnp.where(lax.rem(col, seq_cols) > 0, head, jnp.zeros_like(head))
    padded = jnp.concatenate([head, block_in], axis=0)
    windows = jnp.stack([padded[r * chunk : r * chunk + total_rows] for r in range(row_count)])
    x_rows = lax.all_to_all(windows, "row", 0, 0, tiled=True)
    g_rows = lax.all_to_all(cotangent.reshape(row_count, chunk, part), "row", 0, 0, tiled=True)

    def split_pairs(value):
        value = value.reshape(value.shape[0], heads_here, 2, P_SIZE)
        return jnp.swapaxes(value, 1, 2).reshape(value.shape[0], 2, local)

    up_part = lax.dynamic_slice_in_dim(adapt_in_up, row * rank_part, rank_part, 0)
    w_block = jnp.concatenate([split_pairs(proj_inner), split_pairs(up_part)], axis=0)
    w_all = lax.all_gather(w_block.reshape(part + rank_part, 2 * local), ("col", "row"))
    w_all = w_all.reshape(col_count, row_count, part + rank_part, 2, local)
    w_all = to_groups(w_all, heads_here).reshape(GROUPS, row_count, part + rank_part, 2 * WIDTH)
    up_all = w_all[:, :, part:, :].reshape(GROUPS, rank_total, 2 * WIDTH)
    up_all = lax.dynamic_slice_in_dim(up_all, adapter * RANK, RANK, 1)
    up_all = jnp.pad(up_all, ((0, 0), (0, LANES - RANK), (0, 0)))

    down_part = lax.dynamic_slice_in_dim(adapt_out_down, row * rank_part, rank_part, 0)
    p_block = jnp.concatenate([proj_out, down_part.T], axis=1)
    p_all = lax.all_gather(p_block, ("col", "row")).reshape(col_count, row_count, local, part + rank_part)
    if heads_here != QUAD:
        p_all = jnp.moveaxis(p_all, 1, 0).reshape(row_count, GROUPS, WIDTH, part + rank_part)
        p_all = jnp.moveaxis(p_all, 0, 1)
    down_all = jnp.swapaxes(p_all[..., part:], 1, 2).reshape(GROUPS, WIDTH, rank_total)
    down_all = pad_lanes(lax.dynamic_slice_in_dim(down_all, adapter * RANK, RANK, 2), LANES)

    in_down = lax.dynamic_slice_in_dim(adapt_in_down, adapter * RANK, RANK, 1)
    out_up = lax.dynamic_slice_in_dim(adapt_out_up, adapter * RANK, RANK, 1)
    state_width = proj_state.shape[1]
    shared = lax.all_gather(jnp.concatenate([proj_state, in_down, out_up], axis=1), "row")
    w_state = jnp.concatenate(
        [
            pad_lanes(shared[..., :state_width], 384),
            pad_lanes(shared[..., state_width : state_width + RANK], LANES),
        ],
        axis=2,
    )
    out_up_all = pad_lanes(shared[..., state_width + RANK :], LANES)
    gain_all = lax.all_gather(norm_gain, "row").reshape(row_count, 1, part)

    scalars = jnp.concatenate([step_bias, decay_log, skip_gain])
    vectors = jnp.concatenate(
        [conv_inner, conv_inner_bias[None], gate_gain[None], pad_lanes(scalars, local)[None]], axis=0
    )
    vectors = lax.all_gather(vectors, "col")
    scalars = vectors[:, 6, : 3 * heads_here].reshape(col_count, 3, heads_here)
    scalars = jnp.swapaxes(scalars, 0, 1).reshape(3, HEADS)
    head_rows = jnp.pad(scalars[:2], ((0, 6), (0, LANES - HEADS)))
    skip_wide = jnp.repeat(scalars[2], P_SIZE).reshape(GROUPS, 1, WIDTH)
    vectors = jnp.concatenate(
        [to_groups(vectors[:, :6], heads_here), skip_wide, jnp.zeros_like(skip_wide)], axis=1
    )
    state_taps = jnp.concatenate([conv_state, conv_state_bias[None], jnp.zeros((3, 256), F32)], axis=0)

    token_f32 = ((chunk, LANES), F32)
    token_low = ((chunk, LANES), BF16)
    inner_low = ((chunk, DI), BF16)
    states = ((blocks, STATES, DI), F32)
    score_box = ((blocks, BLOCK, BLOCK), F32)
    turned = ((blocks, STATES, BLOCK), BF16)
    (
        normed, scpre, raw, step, cum, cum_t, bs, cs, cs_t, adv, gate, u, eloc, fin, dec,
    ) = grouped_call(
        front_kernel,
        (x_rows, gain_all, w_state, state_taps, head_rows, w_all, up_all, vectors),
        "aaaaaccc",
        [
            ((total_rows, D), BF16), ((chunk, 256), F32), token_f32, token_f32, token_f32,
            ((GROUPS, QUAD, chunk), F32), token_low, token_low, turned, ((total_rows, LANES), BF16),
            inner_low, inner_low, states, ((STATES, DI), BF16), ((8, DI), F32),
        ],
        "aaaaaaaaaalllll",
        [((total_rows, 512), F32), turned, ((total_rows, WIDTH), F32)],
    )
    decay = dec[0:1]
    entry = carry_in(fin, decay, row_count, col_count, seq_cols, True)
    out_rows, o, ent, aux, side_grad, out_up_grad = grouped_call(
        scan_kernel,
        (x_rows, g_rows, out_up_all, p_all, down_all, vectors, gate, u, eloc, entry, step, cum, cum_t, bs, cs),
        "aaacccllllaacaa",
        [
            ((row_count, chunk, part), BF16), inner_low, ((blocks, STATES, DI), BF16), token_f32, token_low,
            ((RANK, D), F32),
        ],
        "allaaa",
        [score_box, ((chunk, D), F32), token_f32, token_f32],
    )
    dgate, dy, gloc, gfin, out_down_grad = grouped_call(
        gate_kernel,
        (g_rows, p_all, side_grad, down_all, vectors, gate, o, aux, cum, cs_t),
        "acaccllaaa",
        [inner_low, inner_low, states, ((STATES, DI), BF16), ((RANK, DI), F32)],
        "lllll",
        [((blocks, RANK, BLOCK), BF16)],
    )
    exit_grad = carry_in(gfin, decay, row_count, col_count, seq_cols, False)
    corr, in_up_grad, in_down_grad = grouped_call(
        back_kernel,
        (
            x_rows, gain_all, normed, w_state, w_all, up_all, adv, vectors, state_taps, head_rows,
            u, o, dy, dgate, ent, gloc, exit_grad, step, cum, cum_t, raw, scpre, bs, cs,
        ),
        "aaaaccacaalllllllaacaaaa",
        [((row_count, total_rows, part), BF16), ((GROUPS, RANK, 2 * WIDTH), F32), ((RANK, D), F32)],
        "aca",
        [
            score_box, score_box, token_f32, token_f32, token_f32, token_f32, ((blocks, 8, LANES), F32),
            ((total_rows + HALO, WIDTH), F32), ((total_rows, 2 * WIDTH), BF16), ((total_rows, D), F32),
            ((total_rows, LANES), F32), ((blocks, RANK, BLOCK), BF16),
        ],
    )

    block_out = lax.all_to_all(out_rows, "row", 0, 0, tiled=True).reshape(col_tokens, part)
    corr = lax.all_to_all(corr, "row", 0, 0, tiled=True).astype(F32)
    early = corr[:, :HALO]
    input_grad = cotangent.astype(F32) + corr[:, HALO:].reshape(col_tokens, part)
    for r in range(1, row_count):
        input_grad = input_grad.at[r * chunk - HALO : r * chunk].add(early[r])
    if seq_cols > 1:
        pairs = [(i, (i - 1) % col_count) for i in range(col_count)]
        late = lax.ppermute(early[0].astype(BF16), "col", pairs).astype(F32)
        late = jnp.where(lax.rem(col, seq_cols) < seq_cols - 1, late, jnp.zeros_like(late))
        input_grad = input_grad.at[-HALO:].add(late)

    thin = jnp.concatenate([in_down_grad, out_up_grad], axis=0).astype(BF16)
    thin = lax.psum_scatter(thin, "row", scatter_dimension=1, tiled=True)
    thin = lax.all_gather(thin, "col").astype(F32)
    wide = in_up_grad.reshape(GROUPS, RANK, 2, WIDTH)
    wide = to_cols(wide, heads_here, col_count)
    tall = jnp.swapaxes(out_down_grad.reshape(RANK, GROUPS, WIDTH), 0, 1)
    tall = to_cols(tall, heads_here, col_count)
    wide = jnp.concatenate([wide.reshape(col_count, RANK, 2 * local), tall], axis=2).astype(BF16)
    wide = lax.all_to_all(wide, "col", 0, 0, tiled=True)
    wide = lax.psum(wide, "row").astype(F32)
    owner = jnp.repeat(adapter_id, seq_cols)
    adapters = rank_total // RANK
    chosen = owner[:, None] == jnp.arange(adapters, dtype=jnp.int32)[None, :]
    wide = jnp.sum(jnp.where(chosen[:, :, None, None], wide[:, None], 0.0), axis=0)
    wide = wide.reshape(rank_total, 3 * local)
    in_up = wide[:, : 2 * local].reshape(rank_total, 2, heads_here, P_SIZE)
    in_up = jnp.swapaxes(in_up, 1, 2).reshape(rank_total, heads_here, 2 * P_SIZE)
    out_down = wide[:, 2 * local :]
    thin = jnp.sum(jnp.where(chosen[:, :, None, None], thin[:, None], 0.0), axis=0)
    thin = thin.reshape(adapters, 2, RANK, part)
    thin = jnp.transpose(thin, (1, 3, 0, 2)).reshape(2, part, rank_total)
    thin = lax.dynamic_slice_in_dim(thin, col * rank_share, rank_share, 2)
    return block_out, input_grad, thin[0], in_up, out_down, thin[1]


def solution(mesh):
    placed = (
        P("col", "row"), P("row"), P("row", "col", None), P("row", None), P(None, "col"), P("col"), P(), P(),
        P("col"), P("col"), P("col"), P("col"), P("col", "row"), P("row", None), P(None, "col", None),
        P(None, "col"), P("row", None), P(), P("col", "row"),
    )
    return jax.shard_map(
        per_device,
        mesh=mesh,
        in_specs=placed,
        out_specs=(
            P("col", "row"), P("col", "row"), P("row", "col"), P(None, "col", None), P(None, "col"),
            P("row", "col"),
        ),
        check_vma=False,
    )
```

time: 2870 us -> 518 us (0.18)
  waiting for transfers between devices: 1510 us -> 101 us
  matrix products: 498 us -> 0 us
  other arithmetic: 375 us -> 17 us
  local copies, waits for them, and re-layouts: 296 us -> 27.6 us
  Pallas kernels: 0 us -> 195 us
    reduce_scatter x6 -> x1, waiting for transfers between devices: 1090 us -> 21.1 us  [per_device(): thin = lax.psum_scatter(thin, 'row', scatter_dimension=1, tiled=True)]
    dot_general x26 -> x0, matrix products: 498 us -> none  [the longest x3 152 us: scan_blocks(): jnp.einsum('chts,cshp->cthp', weights, value_block, precision=HIGHEST)]
    all_gather x6 -> x2, waiting for transfers between devices: 403 us -> 22.2 us  [the longest x1 20.2 us: per_device(): lax.all_gather(p_block, ('col', 'row'))]
    pallas_call x0 -> x4, Pallas kernels: none -> 195 us  [grouped_call(): pl.pallas_call(kernel, grid=(GROUPS,), in_specs=[KINDS[kind](value.shape)...]
    unnamed x1 -> x0, blocking collectives: 105 us -> none
    all_gather x0 -> x4, blocking collectives: none -> 103 us  [the longest x1 35.6 us: per_device(): lax.all_gather(jnp.concatenate([proj_state, in_down, out_up], axis=1), 'r...]
    slice x15 -> x12, local copies, waits for them, and re-layouts: 99.8 us -> 3.76 us  [the longest x1 1.3 us: per_device(): up_all = w_all[:, :, part:, :].reshape(GROUPS, rank_total, 2 * WIDTH)]
    convert_element_type x11 -> x5, other arithmetic: 76.7 us -> 4.72 us  [the longest x2 3.4 us: carry_in(): total = joined.astype(BF16)]
  transfers between devices with their start and end apart: 14 -> 12, of which waited for: 10 -> 7; matrix products, arithmetic and copies ran while one was open for 41% -> 6% of each run, Pallas kernels for 0% -> 9%
where the time goes in v1:
time: 518 us; the launch traced here: 517 us
  Pallas kernels  195 us (38%)
  blocking collectives  146 us (28%)
  waiting for transfers between devices  101 us (19%)
  local copies, waits for them, and re-layouts  27.6 us (5%)
  other arithmetic  17 us (3%)
  between operations  15 us (3%)
  starting transfers between devices  14.4 us (3%)
    pallas_call x4, Pallas kernels, grouped_call(): pl.pallas_call(kernel, grid=(GROUPS,), in_specs=[KINDS[kind](value.shape)...  195 us
    all_gather x1, blocking collectives, per_device(): lax.all_gather(jnp.concatenate([proj_state, in_down, out_up], axis=1), 'r...  35.6 us
    all_gather x1, blocking collectives, per_device(): vectors = lax.all_gather(vectors, 'col')  31.9 us
    psum x1, waiting for transfers between devices, per_device(): wide = lax.psum(wide, 'row').astype(F32)  31.1 us
    all_gather x1, blocking collectives, per_device(): thin = lax.all_gather(thin, 'col').astype(F32)  30.8 us
    all_to_all x1, blocking collectives, per_device(): lax.all_to_all(out_rows, 'row', 0, 0, tiled=True).reshape(col_tokens, part)  28.9 us
    ppermute x4, waiting for transfers between devices, carry_in(): other = lax.ppermute(total, 'row', pairs).astype(F32)  26.8 us
    reduce_scatter x1, waiting for transfers between devices, per_device(): thin = lax.psum_scatter(thin, 'row', scatter_dimension=1, tiled=True)  21.1 us
  transfers between devices with their start and end apart: 12, of which 7 were waited for; matrix products, arithmetic and copies ran while one was open for 6% of the time, Pallas kernels for 9%

profile of v1, /device:TPU:0, one launch (start us, length us, event | category | flops | bytes accessed | tf_op | source)
XLA Modules:
  0.0 516.9 jit_solution(18119653427470969860)
XLA Ops:
  7.3 0.8 copy-done
  8.3 1.1 copy.100
  9.5 0.9 copy.104
  12.2 1.6 pad_maximum_fusion
  13.8 4.4 all-to-all-start
  19.8 35.6 %all-gather = bf16[1024,320]{0,1:T(8,128)(2,1)} all-gather(bf16[256,320]{0,1:T(8,128)(2,1)S(1)} %pad_maximum_fusion.4), channel_id=2, replica_groups=mesh['row'=4,'col'=8] {'row'}, dimensions={0}, use_global_device_ids=true | all-gather | bytes 819200 | tf_op jit(solution)/shard_map/all_gather | solution.py:631
  55.4 1.5 copy.93
  57.0 31.9 %all-gather.5 = f32[8,7,256]{2,1,0:T(8,128)S(1)} all-gather(f32[1,7,256]{2,1,0:T(8,128)S(1)} %maximum_bitcast_fusion), channel_id=4, replica_groups=mesh['row'=4,'col'=8] {'col'}, dimensions={0}, use_global_device_ids=true | all-gather | bytes 64512 | tf_op jit(solution)/shard_map/all_gather | solution.py:646
  90.3 5.1 all-gather.6.gain_ref
  95.6 1.1 fusion.6.wst_ref
  98.1 2.1 all-gather.10.cloned.1.call-done
  100.1 1.3 slice.165
  101.4 1.1 pad.40.up_ref
  102.5 1.3 copy-done.2
  103.9 45.0 %shard_map.226 = (bf16[1040,1024]{1,0:T(8,128)(2,1)}, f32[1024,256]{1,0:T(8,128)}, f32[1024,128]{1,0:T(8,128)}, f32[1024,128]{1,0:T(8,128)}, f32[1024,128]{1,0:T...) custom-call(bf16[4,1040,256]{2,1,0:T(8,128)(2,1)} %copy-done.2, ...), custom_call_target="tpu_custom_call" | custom-call | tf_op jit(solution)/shard_map/pallas_call | solution.py:497
  149.2 3.8 all-to-all-start.1
  153.8 0.8 slice.145
  154.9 20.2 %all-gather.12.cloned.1.call-done = bf16[8192,288]{1,0:T(8,128)(2,1)} async-done(((bf16[256,288]{1,0:T(8,128)(2,1)}), bf16[8192,288]{1,0:T(8,128)(2,1)}) %all-gather.12.cloned.1.call-update) | async-done | bytes 4718608 | tf_op jit(solution)/shard_map/all_gather | solution.py:621
  175.1 3.1 slice_bitcast_fusion
  178.2 1.9 copy.95
  180.1 2.1 fusion.3
  182.2 0.8 collective-permute-start.2
  183.3 0.9 pad.35.down_ref
  184.2 12.4 %collective-permute-done.2 = bf16[128,2048]{1,0:T(8,128)(2,1)} collective-permute-done((bf16[128,2048]{1,0:T(8,128)(2,1)}, bf16[128,2048]{1,0:T(8,128)(2,1)}, u32[]{:S(2)}, u32[]{:S(2)}) %collective-permute-start.2) | collective-permute-done | bytes 524320 | tf_op jit(solution)/shard_map/ppermute | solution.py:553
  196.6 2.3 add_select_fusion.1.ein_ref
  198.9 1.3 copy-done.3
  200.2 46.7 %shard_map.227 = (bf16[4,1024,256]{2,1,0:T(8,128)(2,1)}, bf16[1024,2048]{1,0:T(8,128)(2,1)}, bf16[4,128,2048]{2,1,0:T(8,128)(2,1)}, f32[1024,128]{1,0:T(8,128)},...) custom-call(bf16[4,1040,256]{2,1,0:T(8,128)(2,1)} %copy-done.2, bf16[4,1024,256]{2,1,0:T(8,128)(2,1)} %copy-done.3, ...), custom_call_target="tpu_custom_call" | custom-call | tf_op jit(solution)/shard_map/pallas_call | solution.py:497
  246.9 25.1 %shard_map.228 = (bf16[1024,2048]{1,0:T(8,128)(2,1)}, bf16[1024,2048]{1,0:T(8,128)(2,1)}, f32[4,128,2048]{2,1,0:T(8,128)}, bf16[128,2048]{1,0:T(8,128)(2,1)}, f32[16,2048]{1,0:T(8,128)}) custom-call(bf16[4,1024,256]{2,1,0:T(8,128)(2,1)} %copy-done.3, bf16[8,4,256,288]{3,2,1,0:T(8,128)(2,1)} %bitcast.95, bf16[1024,128]{1,0:T(8,128)(2,1)} %get-tuple-element.85.sg_ref, ...), custom_call_target="tpu_custom_call" | custom-call | tf_op jit(solution)/shard_map/pallas_call | solution.py:497
  272.1 2.1 collective-permute-done.3
  274.2 1.3 fusion.5
  275.5 0.9 collective-permute-start.4
  276.4 0.9 convert.17
  277.3 12.3 %collective-permute-done.4 = bf16[128,2048]{1,0:T(8,128)(2,1)S(1)} collective-permute-done((bf16[128,2048]{1,0:T(8,128)(2,1)S(1)}, bf16[128,2048]{1,0:T(8,128)(2,1)S(1)}, u32[]{:S(2)}, u32[]{:S(2)}) %collective-permute-start.4) | collective-permute-done | bytes 524320 | tf_op jit(solution)/shard_map/ppermute | solution.py:553
  289.6 1.2 add_select_fusion.gin_ref
  290.8 78.2 %shard_map.229 = (bf16[4,1040,256]{2,1,0:T(8,128)(2,1)}, f32[8,16,512]{2,1,0:T(8,128)}, f32[16,1024]{1,0:T(8,128)}) custom-call(bf16[4,1040,256]{2,1,0:T(8,128)(2,1)} %copy-done.2, f32[4,1,256]{2,1,0:T(1,128)} %all-gather.6.gain_ref, bf16[1040,1024]{1,0:T(8,128)(2,1)} %get-tuple-element.82.normed_ref, bf16[4,256,512]{2,1,0:T(8,128)(2,1)} %fusion.6.wst_ref, ...), custom_call_target="tpu_custom_call" | custom-call | tf_op jit(solution)/shard_map/pallas_call | solution.py:497
  369.0 1.0 convert.16
  370.0 14.2 %all_to_all.25 = bf16[8,16,768]{2,1,0:T(8,128)(2,1)} all-to-all(bf16[8,16,768]{2,1,0:T(8,128)(2,1)S(1)} %pad_maximum_fusion.3), channel_id=1, replica_groups=mesh['row'=4,'col'=8] {'col'}, dimensions={0} | all-to-all | bytes 393216 | tf_op jit(solution)/shard_map/all_to_all | solution.py:734
  384.1 28.9 %all_to_all.26 = bf16[4,1024,256]{2,1,0:T(8,128)(2,1)} all-to-all(bf16[4,1024,256]{2,1,0:T(8,128)(2,1)S(1)} %copy-done.8), channel_id=1, replica_groups=mesh['row'=4,'col'=8] {'row'}, dimensions={0} | all-to-all | bytes 4194304 | tf_op jit(solution)/shard_map/all_to_all | solution.py:714
  413.1 3.7 all-to-all-start.3
  417.7 21.1 %reduce-scatter.2.cloned.1.call-done = bf16[32,256]{1,0:T(8,128)(2,1)} async-done(((bf16[32,1024]{1,0:T(8,128)(2,1)}), bf16[32,256]{1,0:T(8,128)(2,1)}) %reduce-scatter.2.cloned.1.call-update) | async-done | bytes 16400 | tf_op jit(solution)/shard_map/reduce_scatter | solution.py:727
  438.8 30.8 %all-gather.4 = bf16[256,256]{1,0:T(8,128)(2,1)S(1)} all-gather(bf16[32,256]{1,0:T(8,128)(2,1)} %reduce-scatter.2.cloned.1.call-done), channel_id=6, replica_groups=mesh['row'=4,'col'=8] {'col'}, dimensions={0}, use_global_device_ids=true | all-gather | bytes 147456 | tf_op jit(solution)/shard_map/all_gather | solution.py:728
  470.5 31.1 %all-reduce.10.cloned.1.call-done = bf16[8,16,768]{2,1,0:T(8,128)(2,1)} async-done(((bf16[8,16,768]{2,1,0:T(8,128)(2,1)}), bf16[8,16,768]{2,1,0:T(8,128)(2,1)}) %all-reduce.10.cloned.1.call-update) | async-done | bytes 196624 | tf_op jit(solution)/shard_map/psum | solution.py:735
  501.7 1.0 convert_element_type.62
  503.7 0.8 copy.109
  504.9 1.2 copy-done.4
  506.2 0.8 bitcast_add_fusion
  507.4 1.6 copy-done.5
  509.1 1.3 copy.119
  (120 shorter events, 11.3 us)
Async XLA Ops:
  7.2 0.9 copy-start
  7.2 4.2 copy-start.10
  7.2 4.9 copy-start.6
  7.2 92.9 %all-gather.10.cloned.1.call-start = ((), (), s32[]{:S(2)}) async-start(), calls=%async_computation.6 | async-start | bytes 9732096 | tf_op jit(solution)/shard_map/all_gather | solution.py:612
  10.4 164.6 %all-gather.12.cloned.1.call-start = ((), (), s32[]{:S(2)}) async-start(), calls=%async_computation.9 | async-start | bytes 6488064 | tf_op jit(solution)/shard_map/all_gather | solution.py:621
  13.8 4.5 copy-start.24
  13.8 5.7 %copy-start.13 = (bf16[256,128]{1,0:T(8,128)(2,1)S(1)}, bf16[256,128]{1,0:T(8,128)(2,1)}, u32[]{:S(2)}) copy-start(bf16[256,128]{1,0:T(8,128)(2,1)} %param.41) | copy-start | bytes 196612
  13.8 5.7 %copy-start.14 = (bf16[256,128]{1,0:T(8,128)(2,1)S(1)}, bf16[256,128]{1,0:T(8,128)(2,1)}, u32[]{:S(2)}) copy-start(bf16[256,128]{1,0:T(8,128)(2,1)} %param.38) | copy-start | bytes 196612
  13.8 6.0 %copy-start.9 = (bf16[256,288]{0,1:T(8,128)(2,1)S(1)}, bf16[256,288]{0,1:T(8,128)(2,1)}, u32[]{:S(2)}) copy-start(bf16[256,288]{0,1:T(8,128)(2,1)} %param.28) | copy-start | bytes 442372
  13.8 88.7 %all-to-all-start = ((bf16[4,1040,256]{2,1,0:T(8,128)(2,1)}), bf16[4,1040,256]{2,1,0:T(8,128)(2,1)S(1)}, u32[]{:S(2)}, u32[]{:S(2)}) async-start(bf16[4,1040,256]{2,1,0:T(8,128)(2,1)} %pad_maximum_fusion), calls=%async_computation | async-start | bytes 4259840 | tf_op jit(solution)/shard_map/all_to_all | solution.py:603
  18.2 38.7 %copy-start.21 = (f32[4]{0:T(128)S(1)}, f32[4]{0:T(128)}, u32[]{:S(2)}) copy-start(f32[4]{0:T(128)} %param.35) | copy-start | bytes 52
  18.2 38.7 %copy-start.22 = (f32[4]{0:T(128)S(1)}, f32[4]{0:T(128)}, u32[]{:S(2)}) copy-start(f32[4]{0:T(128)} %param.34) | copy-start | bytes 52
  18.2 38.7 %copy-start.23 = (f32[4]{0:T(128)S(1)}, f32[4]{0:T(128)}, u32[]{:S(2)}) copy-start(f32[4]{0:T(128)} %param.33) | copy-start | bytes 52
  18.2 38.8 %copy-start.16 = (f32[4,256]{1,0:T(4,128)S(1)}, f32[4,256]{1,0:T(4,128)}, u32[]{:S(2)}) copy-start(f32[4,256]{1,0:T(4,128)} %param.29) | copy-start | bytes 12292
  18.2 38.8 %copy-start.19 = (f32[256]{0:T(256)S(1)}, f32[256]{0:T(256)}, u32[]{:S(2)}) copy-start(f32[256]{0:T(256)} %param.36) | copy-start | bytes 3076
  18.2 38.8 %copy-start.20 = (f32[256]{0:T(256)S(1)}, f32[256]{0:T(256)}, u32[]{:S(2)}) copy-start(f32[256]{0:T(256)} %param.30) | copy-start | bytes 3076
  18.2 72.0 %copy-start.17 = (f32[256]{0:T(256)S(1)}, f32[256]{0:T(256)}, u32[]{:S(2)}) copy-start(f32[256]{0:T(256)} %param.26) | copy-start | bytes 3076
  55.4 41.3 %copy-start.15 = (f32[4,256]{1,0:T(4,128)S(1)}, f32[4,256]{1,0:T(4,128)}, u32[]{:S(2)}) copy-start(f32[4,256]{1,0:T(4,128)} %param.31) | copy-start | bytes 12292
  55.4 41.3 %copy-start.18 = (f32[256]{0:T(256)S(1)}, f32[256]{0:T(256)}, u32[]{:S(2)}) copy-start(f32[256]{0:T(256)} %param.32) | copy-start | bytes 3076
  102.5 1.3 copy-start.2
  148.9 31.2 %collective-permute-start = (bf16[128,2048]{1,0:T(8,128)(2,1)}, bf16[128,2048]{1,0:T(8,128)(2,1)S(1)}, u32[]{:S(2)}, u32[]{:S(2)}) collective-permute-start(bf16[128,2048]{1,0:T(8,128)(2,1)} %get-tuple-element.74), channel_id=1, source_target_pairs={{0,8},{8,0},{16,24},{24,16},{1,9},{9,1},{17,25},{25,17},{2,10},{10... | collective-permute-start | bytes 1572872 | tf_op jit(solution)/shard_map/ppermute | solution.py:553
  149.2 49.6 %all-to-all-start.1 = ((bf16[4,1024,256]{2,1,0:T(8,128)(2,1)}), bf16[4,1024,256]{2,1,0:T(8,128)(2,1)S(1)}, u32[]{:S(2)}, u32[]{:S(2)}) async-start(bf16[4,1024,256]{2,1,0:T(8,128)(2,1)} %bitcast.96), calls=%async_computation.1 | async-start | bytes 4194304 | tf_op jit(solution)/shard_map/all_to_all | solution.py:604
  154.6 25.4 %collective-permute-start.1 = (f32[1,2048]{1,0:T(1,128)S(1)}, f32[1,2048]{1,0:T(1,128)S(1)}, u32[]{:S(2)}, u32[]{:S(2)}) collective-permute-start(f32[1,2048]{1,0:T(1,128)S(1)} %slice.145), channel_id=1, source_target_pairs={{0,8},{8,0},{16,24},{24,16},{1,9},{9,1},{17,25},{25,17},{2,10},{10... | collective-permute-start | bytes 24584 | tf_op jit(solution)/shard_map/ppermute | solution.py:554
  182.2 14.4 %collective-permute-start.2 = (bf16[128,2048]{1,0:T(8,128)(2,1)}, bf16[128,2048]{1,0:T(8,128)(2,1)}, u32[]{:S(2)}, u32[]{:S(2)}) collective-permute-start(bf16[128,2048]{1,0:T(8,128)(2,1)} %fusion.3), channel_id=1, source_target_pairs={{0,16},{8,24},{16,0},{24,8},{1,17},{9,25},{17,1},{25,9},{2,18},{10... | collective-permute-start | bytes 1572872 | tf_op jit(solution)/shard_map/ppermute | solution.py:553
  198.9 1.3 copy-start.3
  272.1 2.2 collective-permute-start.3
  275.5 14.0 %collective-permute-start.4 = (bf16[128,2048]{1,0:T(8,128)(2,1)S(1)}, bf16[128,2048]{1,0:T(8,128)(2,1)S(1)}, u32[]{:S(2)}, u32[]{:S(2)}) collective-permute-start(bf16[128,2048]{1,0:T(8,128)(2,1)S(1)} %fusion.5), channel_id=1, source_target_pairs={{0,16},{8,24},{16,0},{24,8},{1,17},{9,25},{17,1},{25,9},{2,18},{10... | collective-permute-start | bytes 1572872 | tf_op jit(solution)/shard_map/ppermute | solution.py:553
  290.8 93.4 %copy-start.8 = (bf16[4,1024,256]{2,1,0:T(8,128)(2,1)S(1)}, bf16[4,1024,256]{2,1,0:T(8,128)(2,1)}, u32[]{:S(2)}) copy-start(bf16[4,1024,256]{2,1,0:T(8,128)(2,1)} %get-tuple-element.81) | copy-start | bytes 6291460
  413.0 3.8 copy-start.11
  413.1 3.8 copy-start.12
  413.1 91.5 %all-to-all-start.3 = ((bf16[4,1040,256]{2,1,0:T(8,128)(2,1)}), bf16[4,1040,256]{2,1,0:T(8,128)(2,1)S(1)}, u32[]{:S(2)}, u32[]{:S(2)}) async-start(bf16[4,1040,256]{2,1,0:T(8,128)(2,1)} %get-tuple-element.95), calls=%async_computation.3 | async-start | bytes 4259840 | tf_op jit(solution)/shard_map/all_to_all | solution.py:715
  416.8 22.0 %reduce-scatter.2.cloned.1.call-start = ((), (), s32[]{:S(2)}) async-start(), calls=%async_computation.7 | async-start | bytes 81920 | tf_op jit(solution)/shard_map/reduce_scatter | solution.py:727
  417.6 84.1 %all-reduce.10.cloned.1.call-start = ((), (), s32[]{:S(2)}) async-start(), calls=%async_computation.8 | async-start | bytes 393216 | tf_op jit(solution)/shard_map/psum | solution.py:735
  504.6 1.6 copy-start.4
  507.0 2.1 copy-start.5
  507.4 3.0 copy-start.1
  507.4 3.0 copy-start.7
Sparse Core Ops, SparseCore 0:
  11.5 88.5 all-gather.9
  103.0 72.0 all-gather.11
  420.6 18.1 reduce-scatter.1
  470.0 31.6 all-reduce.9

commit v2 on v1

--- a/solution.py
+++ b/solution.py
@@ -26,6 +26,7 @@
 VMEM_BYTES = 60 * 1024 * 1024
 F32 = jnp.float32
 BF16 = jnp.bfloat16
+MESH = pl.DeviceIdType.MESH
 
 
 def mm(left, right):
@@ -295,7 +296,7 @@
             sg_t_scr[k] = sg_ref[at_block(k), :].astype(F32).T[:RANK].astype(BF16)
 
     taps = vp_ref[0]
-    gdown_ref[...] = jnp.zeros_like(gdown_ref)
+    gdown_ref[0] = jnp.zeros((RANK, WIDTH), F32)
 
     def one_block(i, state):
         k = blocks - 1 - i
@@ -312,7 +313,7 @@
         coefficient = aux_ref[rows, 1:2]
         scale = rms * taps[5:6]
         mixed = (gated * scale).astype(BF16)
-        gdown_ref[...] += mm(sg_t_scr[k], mixed)
+        gdown_ref[0] += mm(sg_t_scr[k], mixed)
         gated_grad = scale * dmix - gated * coefficient
         dy = gated_grad * act
         dgate = gated_grad * output * (sig + act * (1.0 - sig))
@@ -330,9 +331,9 @@
 def back_kernel(
     x_ref, gain_ref, normed_ref, wst_ref, w_ref, up_ref, adv_ref, vp_ref, sp_ref, hp_ref,
     u_ref, o_ref, dy_ref, dgate_ref, ent_ref, gloc_ref, gin_ref,
-    step_ref, cum_ref, cum_t_ref, raw_ref, scpre_ref, bs_ref, cs_ref,
-    corr_ref, gup_ref, gdown_ref,
-    score_scr, dscore_scr, db_scr, dc_scr, dcum_scr, dstep_scr, dlast_scr, du_scr, ig_scr, ng_scr, adg_scr, adv_t_scr,
+    step_ref, cum_ref, cum_t_ref, raw_ref, scpre_ref, bs_ref, cs_ref, out_down_ref, out_up_ref,
+    corr_ref, wide_ref, thin_ref,
+    score_scr, dscore_scr, db_scr, dc_scr, dcum_scr, dstep_scr, dlast_scr, du_scr, ig_scr, ng_scr, adg_scr, adv_t_scr, up_scr, in_scr,
 ):
     group = pl.program_id(0)
     row_count, _, part = x_ref.shape
@@ -415,14 +416,19 @@
 
     ig_scr[0:HALO, :WIDTH] = jnp.zeros((HALO, WIDTH), BF16)
     first = spread_back(pl.ds(0, HALO), du_scr[0 : HALO + 8, :], HALO)
-    gup_ref[0] = mm_tn(adv_ref[0:HALO, :], first)[:RANK]
+    up_scr[...] = mm_tn(adv_ref[0:HALO, :], first)[:RANK]
 
     @pl.loop(0, blocks)
     def _(k):
         ig_scr[at_rows(k), :WIDTH] = dgate_ref[at_block(k), :]
         window = du_scr[pl.ds(pl.multiple_of(HALO + k * BLOCK, 8), BLOCK + 8), :]
         grad = spread_back(at_rows(k), window, BLOCK)
-        gup_ref[0] += mm(adv_t_scr[k], grad)
+        up_scr[...] += mm(adv_t_scr[k], grad)
+
+    share = RANK // row_count
+    for r in range(row_count):
+        wide_ref[r, 0, :, : 2 * WIDTH] = up_scr[r * share : (r + 1) * share, :]
+        wide_ref[r, 0, :, 2 * WIDTH :] = out_down_ref[0, r * share : (r + 1) * share, :]
 
     @pl.when(group == pl.num_programs(0) - 1)
     def _():
@@ -461,14 +467,14 @@
                 total = total + jnp.sum(piece * grad, axis=1, keepdims=True)
                 square = square + jnp.sum(piece * piece, axis=1, keepdims=True)
                 grads.append(grad)
-                gdown_ref[:, cols] += mm_tn(adapt, normed_ref[rows, cols])[:RANK]
+                in_scr[:, cols] += mm_tn(adapt, normed_ref[rows, cols])[:RANK]
             inv = lax.rsqrt(square / D + EPS)
             factor = inv * inv * inv * total / D
             for r in range(row_count):
                 piece = x_ref[r, rows, :].astype(F32)
                 corr_ref[r, rows, :] = (inv * grads[r] - factor * piece).astype(BF16)
 
-        gdown_ref[...] = jnp.zeros_like(gdown_ref)
+        in_scr[...] = jnp.zeros_like(in_scr)
         finish(pl.ds(0, HALO), du_scr[0 : HALO + 8, :], HALO, None)
 
         @pl.loop(0, blocks)
@@ -476,6 +482,113 @@
             window = du_scr[pl.ds(pl.multiple_of(HALO + k * BLOCK, 8), BLOCK + 8), :]
             finish(at_rows(k), window, BLOCK, dstep_scr[at_block(k), :].astype(BF16))
 
+        for r in range(row_count):
+            thin_ref[r, 0:RANK, :] = in_scr[:, r * part : (r + 1) * part]
+            thin_ref[r, RANK:, :] = out_up_ref[:, r * part : (r + 1) * part]
+
+
+def on_row(row):
+    return {"row": row}
+
+
+def on_col(col):
+    return {"col": col}
+
+
+def tail_kernel(
+    corr_ref, wide_ref, thin_ref,
+    corr_out, wide_out, thin_out,
+    wide_scr, thin_scr, wide_sum, thin_sum, wide_col,
+    own_sem, corr_send, corr_recv, row_send, row_recv, col_send, col_recv, last_send, last_recv,
+):
+    row_count = corr_ref.shape[0]
+    col_count = thin_out.shape[0]
+    row = lax.axis_index("row")
+    col = lax.axis_index("col")
+    barrier = pltpu.get_barrier_semaphore()
+    for d in range(1, row_count):
+        pl.semaphore_signal(barrier, inc=1, device_id=on_row(lax.rem(row + d, row_count)), device_id_type=MESH)
+    for d in range(1, col_count):
+        pl.semaphore_signal(barrier, inc=1, device_id=on_col(lax.rem(col + d, col_count)), device_id_type=MESH)
+    pl.semaphore_wait(barrier, row_count + col_count - 2)
+
+    def send(source, target, sends, recvs, index, device):
+        copy = pltpu.make_async_remote_copy(
+            src_ref=source, dst_ref=target, send_sem=sends.at[index], recv_sem=recvs.at[index],
+            device_id=device, device_id_type=MESH,
+        )
+        copy.start()
+        return copy
+
+    first = []
+    for d in range(1, row_count):
+        peer = lax.rem(row + d, row_count)
+        first.append(send(wide_ref.at[peer], wide_scr.at[row], row_send, row_recv, d, on_row(peer)))
+        first.append(send(thin_ref.at[peer], thin_scr.at[row], row_send, row_recv, row_count + d, on_row(peer)))
+    moved = []
+    for d in range(1, row_count):
+        peer = lax.rem(row + d, row_count)
+        moved.append(send(corr_ref.at[peer], corr_out.at[row], corr_send, corr_recv, d, on_row(peer)))
+    own = pltpu.make_async_copy(corr_ref.at[row], corr_out.at[row], own_sem.at[0])
+    own.start()
+    for copy in first:
+        copy.wait()
+    wide = wide_ref[row]
+    thin = thin_ref[row]
+    for d in range(1, row_count):
+        peer = lax.rem(row + d, row_count)
+        wide = wide + wide_scr[peer]
+        thin = thin + thin_scr[peer]
+    wide_sum[...] = wide
+    thin_sum[...] = thin
+    second = []
+    for d in range(1, col_count):
+        peer = lax.rem(col + d, col_count)
+        second.append(send(wide_sum.at[peer], wide_col.at[col], col_send, col_recv, d, on_col(peer)))
+        second.append(send(thin_sum, thin_out.at[col], col_send, col_recv, col_count + d, on_col(peer)))
+    wide_col[col] = wide_sum[col]
+    thin_out[col] = thin
+    for copy in second:
+        copy.wait()
+    third = []
+    for d in range(1, row_count):
+        peer = lax.rem(row + d, row_count)
+        third.append(send(wide_col, wide_out.at[row], last_send, last_recv, d, on_row(peer)))
+    wide_out[row] = wide_col[...]
+    for copy in third:
+        copy.wait()
+    for copy in moved:
+        copy.wait()
+    own.wait()
+
+
+def finish_exchange(corr, wide, thin):
+    row_count = corr.shape[0]
+    col_count = wide.shape[1]
+    share, width = wide.shape[2:]
+    vmem = pl.BlockSpec(memory_space=pltpu.VMEM)
+    anywhere = pl.BlockSpec(memory_space=pl.ANY)
+    dma = pltpu.SemaphoreType.DMA
+    return pl.pallas_call(
+        tail_kernel,
+        in_specs=[anywhere, vmem, vmem],
+        out_specs=[anywhere, vmem, vmem],
+        out_shape=[
+            jax.ShapeDtypeStruct(corr.shape, corr.dtype),
+            jax.ShapeDtypeStruct((row_count, col_count, share, width), F32),
+            jax.ShapeDtypeStruct((col_count,) + thin.shape[1:], F32),
+        ],
+        scratch_shapes=[
+            pltpu.VMEM(wide.shape, F32), pltpu.VMEM(thin.shape, F32), pltpu.VMEM(wide.shape[1:], F32),
+            pltpu.VMEM(thin.shape[1:], F32), pltpu.VMEM(wide.shape[1:], F32),
+            dma((1,)), dma((row_count,)), dma((row_count,)), dma((2 * row_count,)), dma((2 * row_count,)),
+            dma((2 * col_count,)), dma((2 * col_count,)), dma((row_count,)), dma((row_count,)),
+        ],
+        compiler_params=pltpu.CompilerParams(
+            collective_id=0, has_side_effects=True, vmem_limit_bytes=VMEM_BYTES // 2
+        ),
+    )(corr, wide, thin)
+
 
 def whole_spec(shape):
     return pl.BlockSpec(shape, lambda c: (0,) * len(shape))
@@ -490,10 +603,15 @@
     return pl.BlockSpec(block, lambda c: (0,) * (len(shape) - 1) + (c,))
 
 
-KINDS = {"a": whole_spec, "c": lead_spec, "l": lane_spec}
-
-
-def grouped_call(kernel, inputs, kinds, outputs, out_kinds, scratch):
+def second_spec(shape):
+    block = (shape[0], 1) + tuple(shape[2:])
+    return pl.BlockSpec(block, lambda c: (0, c) + (0,) * (len(shape) - 2))
+
+
+KINDS = {"s": second_spec, "a": whole_spec, "c": lead_spec, "l": lane_spec}
+
+
+def grouped_call(kernel, inputs, kinds, outputs, out_kinds, scratch, flops=0):
     return pl.pallas_call(
         kernel,
         grid=(GROUPS,),
@@ -502,6 +620,7 @@
         out_shape=[jax.ShapeDtypeStruct(shape, dtype) for shape, dtype in outputs],
         scratch_shapes=[pltpu.VMEM(shape, dtype) for shape, dtype in scratch],
         compiler_params=pltpu.CompilerParams(vmem_limit_bytes=VMEM_BYTES),
+        cost_estimate=pl.CostEstimate(flops=flops, bytes_accessed=40_000_000, transcendentals=0),
     )(*inputs)
 
 
@@ -572,6 +691,19 @@
     return before
 
 
+def rows_to_parts(value):
+    row_count = value.shape[0]
+    row = lax.axis_index("row")
+    result = value
+    for d in range(1, row_count):
+        peer = lax.rem(row + d, row_count)
+        pairs = [(i, (i + d) % row_count) for i in range(row_count)]
+        piece = lax.ppermute(lax.dynamic_index_in_dim(value, peer), "row", pairs)
+        source = lax.rem(row + row_count - d, row_count)
+        result = lax.dynamic_update_slice_in_dim(result, piece, source, 0)
+    return result
+
+
 def per_device(
     block_in, norm_gain, proj_inner, proj_state, conv_inner, conv_inner_bias, conv_state, conv_state_bias,
     step_bias, decay_log, skip_gain, gate_gain, proj_out, adapt_in_down, adapt_in_up, adapt_out_down,
@@ -672,6 +804,7 @@
         ],
         "aaaaaaaaaalllll",
         [((total_rows, 512), F32), turned, ((total_rows, WIDTH), F32)],
+        flops=int(45e9),
     )
     decay = dec[0:1]
     entry = carry_in(fin, decay, row_count, col_count, seq_cols, True)
@@ -685,54 +818,57 @@
         ],
         "allaaa",
         [score_box, ((chunk, D), F32), token_f32, token_f32],
+        flops=int(45e9),
     )
+    block_out = rows_to_parts(out_rows).reshape(col_tokens, part)
     dgate, dy, gloc, gfin, out_down_grad = grouped_call(
         gate_kernel,
         (g_rows, p_all, side_grad, down_all, vectors, gate, o, aux, cum, cs_t),
         "acaccllaaa",
-        [inner_low, inner_low, states, ((STATES, DI), BF16), ((RANK, DI), F32)],
-        "lllll",
+        [inner_low, inner_low, states, ((STATES, DI), BF16), ((GROUPS, RANK, WIDTH), F32)],
+        "llllc",
         [((blocks, RANK, BLOCK), BF16)],
+        flops=int(25e9),
     )
     exit_grad = carry_in(gfin, decay, row_count, col_count, seq_cols, False)
-    corr, in_up_grad, in_down_grad = grouped_call(
+    corr, wide, thin = grouped_call(
         back_kernel,
         (
             x_rows, gain_all, normed, w_state, w_all, up_all, adv, vectors, state_taps, head_rows,
             u, o, dy, dgate, ent, gloc, exit_grad, step, cum, cum_t, raw, scpre, bs, cs,
+            out_down_grad, out_up_grad,
         ),
-        "aaaaccacaalllllllaacaaaa",
-        [((row_count, total_rows, part), BF16), ((GROUPS, RANK, 2 * WIDTH), F32), ((RANK, D), F32)],
-        "aca",
+        "aaaaccacaalllllllaacaaaaca",
+        [
+            ((row_count, total_rows, part), BF16), ((row_count, GROUPS, RANK // row_count, 3 * WIDTH), F32),
+            ((row_count, 2 * RANK, part), F32),
+        ],
+        "asa",
         [
             score_box, score_box, token_f32, token_f32, token_f32, token_f32, ((blocks, 8, LANES), F32),
             ((total_rows + HALO, WIDTH), F32), ((total_rows, 2 * WIDTH), BF16), ((total_rows, D), F32),
             ((total_rows, LANES), F32), ((blocks, RANK, BLOCK), BF16),
+            ((RANK, 2 * WIDTH), F32), ((RANK, D), F32),
         ],
+        flops=int(75e9),
     )
 
-    block_out = lax.all_to_all(out_rows, "row", 0, 0, tiled=True).reshape(col_tokens, part)
-    corr = lax.all_to_all(corr, "row", 0, 0, tiled=True).astype(F32)
-    early = corr[:, :HALO]
-    input_grad = cotangent.astype(F32) + corr[:, HALO:].reshape(col_tokens, part)
+    if heads_here != QUAD:
+        share = RANK // row_count
+        wide = jnp.swapaxes(wide.reshape(row_count, GROUPS, share, 3, WIDTH), 0, 1)
+        wide = to_cols(wide, heads_here, col_count)
+        wide = jnp.swapaxes(wide, 0, 1).reshape(row_count, col_count, share, 3 * local)
+    corr, wide, thin = finish_exchange(corr, wide, thin)
+    input_grad = cotangent.astype(F32) + corr[:, HALO:].reshape(col_tokens, part).astype(F32)
+    early = corr[:, :HALO].astype(F32)
     for r in range(1, row_count):
         input_grad = input_grad.at[r * chunk - HALO : r * chunk].add(early[r])
     if seq_cols > 1:
         pairs = [(i, (i - 1) % col_count) for i in range(col_count)]
-        late = lax.ppermute(early[0].astype(BF16), "col", pairs).astype(F32)
+        late = lax.ppermute(corr[0, :HALO], "col", pairs).astype(F32)
         late = jnp.where(lax.rem(col, seq_cols) < seq_cols - 1, late, jnp.zeros_like(late))
         input_grad = input_grad.at[-HALO:].add(late)
-
-    thin = jnp.concatenate([in_down_grad, out_up_grad], axis=0).astype(BF16)
-    thin = lax.psum_scatter(thin, "row", scatter_dimension=1, tiled=True)
-    thin = lax.all_gather(thin, "col").astype(F32)
-    wide = in_up_grad.reshape(GROUPS, RANK, 2, WIDTH)
-    wide = to_cols(wide, heads_here, col_count)
-    tall = jnp.swapaxes(out_down_grad.reshape(RANK, GROUPS, WIDTH), 0, 1)
-    tall = to_cols(tall, heads_here, col_count)
-    wide = jnp.concatenate([wide.reshape(col_count, RANK, 2 * local), tall], axis=2).astype(BF16)
-    wide = lax.all_to_all(wide, "col", 0, 0, tiled=True)
-    wide = lax.psum(wide, "row").astype(F32)
+    wide = jnp.swapaxes(wide, 0, 1).reshape(col_count, RANK, 3 * local)
     owner = jnp.repeat(adapter_id, seq_cols)
     adapters = rank_total // RANK
     chosen = owner[:, None] == jnp.arange(adapters, dtype=jnp.int32)[None, :]

time: 518 us -> 434 us (0.84)
  blocking collectives: 146 us -> 72.9 us
  waiting for transfers between devices: 101 us -> 49.4 us
  Pallas kernels: 195 us -> 236 us
    all_to_all x2 -> x0, blocking collectives: 43.1 us -> none  [the longest x1 28.9 us: per_device(): lax.all_to_all(out_rows, 'row', 0, 0, tiled=True).reshape(col_tokens, part)]
    pallas_call x0 -> x1, Pallas kernels: none -> 40.6 us  [finish_exchange(): pl.pallas_call(tail_kernel, in_specs=[anywhere, vmem, vmem], out_specs=[a...]
    psum x1 -> x0, waiting for transfers between devices: 31.1 us -> none  [per_device(): wide = lax.psum(wide, 'row').astype(F32)]
    all_gather x1 -> x0, blocking collectives: 30.8 us -> none  [per_device(): thin = lax.all_gather(thin, 'col').astype(F32)]
    reduce_scatter x1 -> x0, waiting for transfers between devices: 21.1 us -> none  [per_device(): thin = lax.psum_scatter(thin, 'row', scatter_dimension=1, tiled=True)]
    ppermute x4, waiting for transfers between devices: 26.8 us -> 17 us  [carry_in(): other = lax.ppermute(total, 'row', pairs).astype(F32)]
    ppermute x0 -> x3, waiting for transfers between devices: none -> 8.48 us  [rows_to_parts(): piece = lax.ppermute(lax.dynamic_index_in_dim(value, peer), 'row', pairs)]
  transfers between devices with their start and end apart: 12 -> 12, of which waited for: 7 -> 6; matrix products, arithmetic and copies ran while one was open for 6% -> 9% of each run, Pallas kernels for 9% -> 38%
where the time goes in v2:
time: 434 us; the launch traced here: 432 us
  Pallas kernels  236 us (54%)
  blocking collectives  72.9 us (17%)
  waiting for transfers between devices  49.4 us (11%)
  local copies, waits for them, and re-layouts  27.4 us (6%)
  other arithmetic  19.6 us (5%)
  between operations  15.2 us (4%)
  starting transfers between devices  12.2 us (3%)
    pallas_call x4, Pallas kernels, grouped_call(): pl.pallas_call(kernel, grid=(GROUPS,), in_specs=[KINDS[kind](value.shape)...  195 us
    pallas_call x1, Pallas kernels, finish_exchange(): pl.pallas_call(tail_kernel, in_specs=[anywhere, vmem, vmem], out_specs=[a...  40.6 us
    all_gather x1, blocking collectives, per_device(): lax.all_gather(jnp.concatenate([proj_state, in_down, out_up], axis=1), 'r...  35.7 us
    all_gather x1, blocking collectives, per_device(): vectors = lax.all_gather(vectors, 'col')  32.1 us
    all_gather x1, waiting for transfers between devices, per_device(): lax.all_gather(p_block, ('col', 'row'))  21.4 us
    ppermute x4, waiting for transfers between devices, carry_in(): other = lax.ppermute(total, 'row', pairs).astype(F32)  17 us
  transfers between devices with their start and end apart: 12, of which 6 were waited for; matrix products, arithmetic and copies ran while one was open for 9% of the time, Pallas kernels for 38%

profile of v2, /device:TPU:0, one launch (start us, length us, event | category | flops | bytes accessed | tf_op | source)
XLA Modules:
  0.0 432.3 jit_solution(15016529239224727160)
XLA Ops:
  7.3 0.8 copy-done
  8.3 1.1 copy.103
  9.5 0.9 copy.107
  10.5 0.7 dynamic-slice_bitcast_fusion.2
  11.3 0.7 pad_maximum_fusion.2
  12.2 1.6 pad_maximum_fusion
  13.8 4.6 %all-to-all-start = ((bf16[4,1040,256]{2,1,0:T(8,128)(2,1)}), bf16[4,1040,256]{2,1,0:T(8,128)(2,1)}, u32[]{:S(2)}, u32[]{:S(2)}) async-start(bf16[4,1040,256]{2,1,0:T(8,128)(2,1)} %pad_maximum_fusion), calls=%async_computation | async-start | bytes 4259840 | tf_op jit(solution)/shard_map/all_to_all | solution.py:735
  20.1 35.7 %all-gather = bf16[1024,320]{0,1:T(8,128)(2,1)S(1)} all-gather(bf16[256,320]{0,1:T(8,128)(2,1)S(1)} %pad_maximum_fusion.3), channel_id=2, replica_groups=mesh['row'=4,'col'=8] {'row'}, dimensions={0}, use_global_device_ids=true | all-gather | bytes 819200 | tf_op jit(solution)/shard_map/all_gather | solution.py:763
  56.3 32.1 %all-gather.4 = f32[8,7,256]{2,1,0:T(8,128)S(1)} all-gather(f32[1,7,256]{2,1,0:T(8,128)S(1)} %maximum_bitcast_fusion), channel_id=4, replica_groups=mesh['row'=4,'col'=8] {'col'}, dimensions={0}, use_global_device_ids=true | all-gather | bytes 64512 | tf_op jit(solution)/shard_map/all_gather | solution.py:778
  89.7 5.1 %all-gather.5.gain_ref = f32[4,1,256]{2,1,0:T(1,128)} all-gather(f32[1,1,256]{2,1,0:T(1,128)S(1)} %bitcast.116), channel_id=5, replica_groups=mesh['row'=4,'col'=8] {'row'}, dimensions={0}, use_global_device_ids=true | all-gather | bytes 5120 | tf_op jit(solution)/shard_map/all_gather | solution.py:772
  95.0 1.1 fusion.6.wst_ref
  96.8 0.7 maximum_maximum_fusion.vp_ref
  97.5 2.5 all-gather.9.cloned.1.call-done
  100.0 1.3 slice.165
  101.4 1.1 pad.40.up_ref
  102.5 44.8 %shard_map.226 = (bf16[1040,1024]{1,0:T(8,128)(2,1)}, f32[1024,256]{1,0:T(8,128)}, f32[1024,128]{1,0:T(8,128)}, f32[1024,128]{1,0:T(8,128)}, f32[1024,128]{1,0:T...) custom-call(bf16[4,1040,256]{2,1,0:T(8,128)(2,1)} %all-to-all-done.x, ...), custom_call_target="tpu_custom_call" | custom-call | flops 44999999488 | bytes 40000000 | tf_op jit(solution)/shard_map/pallas_call | solution.py:615
  147.6 4.5 %all-to-all-start.1 = ((bf16[4,1024,256]{2,1,0:T(8,128)(2,1)}), bf16[4,1024,256]{2,1,0:T(8,128)(2,1)}, u32[]{:S(2)}, u32[]{:S(2)}) async-start(bf16[4,1024,256]{2,1,0:T(8,128)(2,1)} %bitcast.4), calls=%async_computation.1 | async-start | bytes 4194304 | tf_op jit(solution)/shard_map/all_to_all | solution.py:736
  152.1 0.8 pad.34.oup_ref
  152.9 0.8 slice.144
  154.2 21.4 %all-gather.11.cloned.1.call-done = bf16[8192,288]{1,0:T(8,128)(2,1)} async-done(((bf16[256,288]{1,0:T(8,128)(2,1)}), bf16[8192,288]{1,0:T(8,128)(2,1)}) %all-gather.11.cloned.1.call-update) | async-done | bytes 4718608 | tf_op jit(solution)/shard_map/all_gather | solution.py:753
  175.5 1.7 slice_bitcast_fusion
  177.3 0.8 copy.98
  178.1 1.3 fusion.3
  179.4 0.9 collective-permute-start.2
  180.6 0.9 pad.35.down_ref
  181.5 12.7 %collective-permute-done.2 = bf16[128,2048]{1,0:T(8,128)(2,1)S(1)} collective-permute-done((bf16[128,2048]{1,0:T(8,128)(2,1)S(1)}, bf16[128,2048]{1,0:T(8,128)(2,1)S(1)}, u32[]{:S(2)}, u32[]{:S(2)}) %collective-permute-start.2) | collective-permute-done | bytes 524320 | tf_op jit(solution)/shard_map/ppermute | solution.py:672
  194.2 1.2 add_select_fusion.1.ein_ref
  195.4 46.6 %shard_map.227 = (bf16[4,1024,256]{2,1,0:T(8,128)(2,1)}, bf16[1024,2048]{1,0:T(8,128)(2,1)}, bf16[4,128,2048]{2,1,0:T(8,128)(2,1)}, f32[1024,128]{1,0:T(8,128)},...) custom-call(bf16[4,1040,256]{2,1,0:T(8,128)(2,1)} %all-to-all-done.x_ref, bf16[4,1024,256]{2,1,0:T(8,128)(2,1)} %all-to-all-done.1.g_ref, ...), custom_call_target="tpu_custom_call" | custom-call | flops 44999999488 | bytes 40000000 | tf_op jit(solution)/shard_map/pallas_call | solution.py:615
  242.1 25.3 %shard_map.228 = (bf16[1024,2048]{1,0:T(8,128)(2,1)}, bf16[1024,2048]{1,0:T(8,128)(2,1)}, f32[4,128,2048]{2,1,0:T(8,128)}, bf16[128,2048]{1,0:T(8,128)(2,1)}, f32[8,16,256]{2,1,0:T(8,128)}) custom-call(bf16[4,1024,256]{2,1,0:T(8,128)(2,1)} %all-to-all-done.1.g_ref, bf16[8,4,256,288]{3,2,1,0:T(8,128)(2,1)} %bitcast.98, ...), custom_call_target="tpu_custom_call" | custom-call | flops 24999999488 | bytes 40000000 | tf_op jit(solution)/shard_map/pallas_call | solution.py:615
  267.5 0.8 constant_dynamic-slice_fusion.2
  268.8 0.8 collective-permute-done.6
  269.6 1.3 fusion.5
  271.3 8.5 %collective-permute-done.3 = bf16[1,1024,256]{2,1,0:T(8,128)(2,1)} collective-permute-done((bf16[1,1024,256]{2,1,0:T(8,128)(2,1)}, bf16[1,1024,256]{2,1,0:T(8,128)(2,1)}, u32[]{:S(2)}, u32[]{:S(2)}) %collective-permute-start.3) | collective-permute-done | bytes 524320 | tf_op jit(solution)/shard_map/ppermute | solution.py:701
  279.8 2.2 constant_dynamic-slice_fusion
  282.4 3.5 collective-permute-done.7
  285.9 2.2 add_select_fusion.gin_ref
  288.1 78.2 %shard_map.229 = (bf16[4,1040,256]{2,1,0:T(8,128)(2,1)}, f32[4,8,4,768]{3,2,1,0:T(4,128)}, f32[4,32,256]{2,1,0:T(8,128)}) custom-call(bf16[4,1040,256]{2,1,0:T(8,128)(2,1)} %all-to-all-done.x_ref, f32[4,1,256]{2,1,0:T(1,128)} %all-gather.5.gain_ref, bf16[1040,1024]{1,0:T(8,128)(2,1)} %get-tuple-element.85.normed_ref, bf16[4,256,512]{2,1,0:T(8,128)(2,1)} %fusion.6.wst_ref, ...), custom_call_target="tpu_custom_call" | custom-call | flops 74999996416 | bytes 40000000 | tf_op jit(solution)/shard_map/pallas_call | solution.py:615
  366.3 1.6 copy-done.2
  367.9 1.0 copy-done.3
  368.9 0.9 copy-done.4
  369.8 40.6 %shard_map.230 = (bf16[4,1040,256]{2,1,0:T(8,128)(2,1)S(1)}, f32[4,8,4,768]{3,2,1,0:T(4,128)S(1)}, f32[8,32,256]{2,1,0:T(8,128)S(1)}) custom-call(bf16[4,1040,256]{2,1,0:T(8,128)(2,1)S(1)} %copy-done.2, f32[4,8,4,768]{3,2,1,0:T(4,128)S(1)} %copy-done.3, f32[4,32,256]{2,1,0:T(8,128)S(1)} %copy-done.4), custom_call_target="tpu_custom_call" | custom-call | tf_op jit(solution)/shard_map/pallas_call | solution.py:572
  410.6 4.1 convert_add_fusion
  416.2 0.8 copy.113
  417.1 1.3 fusion.13
  418.4 1.9 constant_dynamic-update-slice_fusion.1
  420.9 1.3 fusion.11
  422.2 1.3 fusion.9
  423.6 1.9 constant_dynamic-update-slice_fusion
  (106 shorter events, 9.1 us)
Async XLA Ops:
  7.2 0.9 copy-start
  7.2 4.2 copy-start.9
  7.2 4.9 %copy-start.5 = (bf16[4096,256]{1,0:T(8,128)(2,1)S(1)}, bf16[4096,256]{1,0:T(8,128)(2,1)}, u32[]{:S(2)}) copy-start(bf16[4096,256]{1,0:T(8,128)(2,1)} %param.25) | copy-start | bytes 6291460
  7.2 92.8 %all-gather.9.cloned.1.call-start = ((), (), s32[]{:S(2)}) async-start(), calls=%async_computation.2 | async-start | bytes 9732096 | tf_op jit(solution)/shard_map/all_gather | solution.py:744
  10.4 165.1 %all-gather.11.cloned.1.call-start = ((), (), s32[]{:S(2)}) async-start(), calls=%async_computation.3 | async-start | bytes 6488064 | tf_op jit(solution)/shard_map/all_gather | solution.py:753
  13.8 4.7 %copy-start.21 = (s32[8]{0:T(128)S(1)}, s32[8]{0:T(128)}, u32[]{:S(2)}) copy-start(s32[8]{0:T(128)} %param.42) | copy-start | bytes 100
  13.8 6.0 %copy-start.10 = (bf16[256,128]{1,0:T(8,128)(2,1)S(1)}, bf16[256,128]{1,0:T(8,128)(2,1)}, u32[]{:S(2)}) copy-start(bf16[256,128]{1,0:T(8,128)(2,1)} %param.41) | copy-start | bytes 196612
  13.8 6.0 %copy-start.11 = (bf16[256,128]{1,0:T(8,128)(2,1)S(1)}, bf16[256,128]{1,0:T(8,128)(2,1)}, u32[]{:S(2)}) copy-start(bf16[256,128]{1,0:T(8,128)(2,1)} %param.38) | copy-start | bytes 196612
  13.8 6.2 %copy-start.8 = (bf16[256,288]{0,1:T(8,128)(2,1)S(1)}, bf16[256,288]{0,1:T(8,128)(2,1)}, u32[]{:S(2)}) copy-start(bf16[256,288]{0,1:T(8,128)(2,1)} %param.28) | copy-start | bytes 442372
  13.8 88.6 %all-to-all-start = ((bf16[4,1040,256]{2,1,0:T(8,128)(2,1)}), bf16[4,1040,256]{2,1,0:T(8,128)(2,1)}, u32[]{:S(2)}, u32[]{:S(2)}) async-start(bf16[4,1040,256]{2,1,0:T(8,128)(2,1)} %pad_maximum_fusion), calls=%async_computation | async-start | bytes 4259840 | tf_op jit(solution)/shard_map/all_to_all | solution.py:735
  18.4 37.7 %copy-start.18 = (f32[4]{0:T(128)S(1)}, f32[4]{0:T(128)}, u32[]{:S(2)}) copy-start(f32[4]{0:T(128)} %param.35) | copy-start | bytes 52
  18.4 37.7 %copy-start.19 = (f32[4]{0:T(128)S(1)}, f32[4]{0:T(128)}, u32[]{:S(2)}) copy-start(f32[4]{0:T(128)} %param.34) | copy-start | bytes 52
  18.4 37.7 %copy-start.20 = (f32[4]{0:T(128)S(1)}, f32[4]{0:T(128)}, u32[]{:S(2)}) copy-start(f32[4]{0:T(128)} %param.33) | copy-start | bytes 52
  18.5 37.8 %copy-start.13 = (f32[4,256]{1,0:T(4,128)S(1)}, f32[4,256]{1,0:T(4,128)}, u32[]{:S(2)}) copy-start(f32[4,256]{1,0:T(4,128)} %param.29) | copy-start | bytes 12292
  18.5 37.8 %copy-start.16 = (f32[256]{0:T(256)S(1)}, f32[256]{0:T(256)}, u32[]{:S(2)}) copy-start(f32[256]{0:T(256)} %param.36) | copy-start | bytes 3076
  18.5 37.8 %copy-start.17 = (f32[256]{0:T(256)S(1)}, f32[256]{0:T(256)}, u32[]{:S(2)}) copy-start(f32[256]{0:T(256)} %param.30) | copy-start | bytes 3076
  18.5 71.2 %copy-start.14 = (f32[256]{0:T(256)S(1)}, f32[256]{0:T(256)}, u32[]{:S(2)}) copy-start(f32[256]{0:T(256)} %param.26) | copy-start | bytes 3076
  55.8 40.4 %copy-start.12 = (f32[4,256]{1,0:T(4,128)S(1)}, f32[4,256]{1,0:T(4,128)}, u32[]{:S(2)}) copy-start(f32[4,256]{1,0:T(4,128)} %param.31) | copy-start | bytes 12292
  55.8 40.4 %copy-start.15 = (f32[256]{0:T(256)S(1)}, f32[256]{0:T(256)}, u32[]{:S(2)}) copy-start(f32[256]{0:T(256)} %param.32) | copy-start | bytes 3076
  147.3 30.8 %collective-permute-start = (bf16[128,2048]{1,0:T(8,128)(2,1)}, bf16[128,2048]{1,0:T(8,128)(2,1)S(1)}, u32[]{:S(2)}, u32[]{:S(2)}) collective-permute-start(bf16[128,2048]{1,0:T(8,128)(2,1)} %get-tuple-element.77), channel_id=1, source_target_pairs={{0,8},{8,0},{16,24},{24,16},{1,9},{9,1},{17,25},{25,17},{2,10},{10... | collective-permute-start | bytes 1572872 | tf_op jit(solution)/shard_map/ppermute | solution.py:672
  147.6 47.8 %all-to-all-start.1 = ((bf16[4,1024,256]{2,1,0:T(8,128)(2,1)}), bf16[4,1024,256]{2,1,0:T(8,128)(2,1)}, u32[]{:S(2)}, u32[]{:S(2)}) async-start(bf16[4,1024,256]{2,1,0:T(8,128)(2,1)} %bitcast.4), calls=%async_computation.1 | async-start | bytes 4194304 | tf_op jit(solution)/shard_map/all_to_all | solution.py:736
  153.7 24.3 %collective-permute-start.1 = (f32[1,2048]{1,0:T(1,128)S(1)}, f32[1,2048]{1,0:T(1,128)S(1)}, u32[]{:S(2)}, u32[]{:S(2)}) collective-permute-start(f32[1,2048]{1,0:T(1,128)S(1)} %slice.144), channel_id=1, source_target_pairs={{0,8},{8,0},{16,24},{24,16},{1,9},{9,1},{17,25},{25,17},{2,10},{10... | collective-permute-start | bytes 24584 | tf_op jit(solution)/shard_map/ppermute | solution.py:673
  179.4 14.8 %collective-permute-start.2 = (bf16[128,2048]{1,0:T(8,128)(2,1)S(1)}, bf16[128,2048]{1,0:T(8,128)(2,1)S(1)}, u32[]{:S(2)}, u32[]{:S(2)}) collective-permute-start(bf16[128,2048]{1,0:T(8,128)(2,1)S(1)} %fusion.3), channel_id=1, source_target_pairs={{0,16},{8,24},{16,0},{24,8},{1,17},{9,25},{17,1},{25,9},{2,18},{10... | collective-permute-start | bytes 1572872 | tf_op jit(solution)/shard_map/ppermute | solution.py:672
  242.1 25.4 %copy-start.6 = (bf16[4,1024,256]{2,1,0:T(8,128)(2,1)S(1)}, bf16[4,1024,256]{2,1,0:T(8,128)(2,1)}, u32[]{:S(2)}) copy-start(bf16[4,1024,256]{2,1,0:T(8,128)(2,1)} %get-tuple-element.84) | copy-start | bytes 6291460
  267.4 2.2 collective-permute-start.6
  268.3 11.5 %collective-permute-start.3 = (bf16[1,1024,256]{2,1,0:T(8,128)(2,1)}, bf16[1,1024,256]{2,1,0:T(8,128)(2,1)}, u32[]{:S(2)}, u32[]{:S(2)}) collective-permute-start(bf16[1,1024,256]{2,1,0:T(8,128)(2,1)} %constant_dynamic-slice_fusion.2), channel_id=1, source_target_pairs={{0,8},{8,16},{16,24},{24,0},{1,9},{9,17},{17,25},{25,1},{2,10},{10... | collective-permute-start | bytes 1572872 | tf_op jit(solution)/shard_map/ppermute | solution.py:701
  270.9 15.0 %collective-permute-start.7 = (bf16[128,2048]{1,0:T(8,128)(2,1)S(1)}, bf16[128,2048]{1,0:T(8,128)(2,1)}, u32[]{:S(2)}, u32[]{:S(2)}) collective-permute-start(bf16[128,2048]{1,0:T(8,128)(2,1)S(1)} %fusion.5), channel_id=1, source_target_pairs={{0,16},{8,24},{16,0},{24,8},{1,17},{9,25},{17,1},{25,9},{2,18},{10... | collective-permute-start | bytes 1572872 | tf_op jit(solution)/shard_map/ppermute | solution.py:672
  282.0 84.3 %copy-start.7 = (bf16[4,1024,256]{2,1,0:T(8,128)(2,1)}, bf16[4,1024,256]{2,1,0:T(8,128)(2,1)S(1)}, u32[]{:S(2)}) copy-start(bf16[4,1024,256]{2,1,0:T(8,128)(2,1)S(1)} %get-tuple-element.132) | copy-start | bytes 6291460
  282.0 136.4 %collective-permute-start.4 = (bf16[1,1024,256]{2,1,0:T(8,128)(2,1)}, bf16[1,1024,256]{2,1,0:T(8,128)(2,1)}, u32[]{:S(2)}, u32[]{:S(2)}) collective-permute-start(bf16[1,1024,256]{2,1,0:T(8,128)(2,1)} %get-tuple-element.131), channel_id=1, source_target_pairs={{0,16},{8,24},{16,0},{24,8},{1,17},{9,25},{17,1},{25,9},{2,18},{10... | collective-permute-start | bytes 1572872 | tf_op jit(solution)/shard_map/ppermute | solution.py:701
  282.4 141.2 %collective-permute-start.5 = (bf16[1,1024,256]{2,1,0:T(8,128)(2,1)}, bf16[1,1024,256]{2,1,0:T(8,128)(2,1)}, u32[]{:S(2)}, u32[]{:S(2)}) collective-permute-start(bf16[1,1024,256]{2,1,0:T(8,128)(2,1)} %get-tuple-element.130), channel_id=1, source_target_pairs={{0,24},{8,0},{16,8},{24,16},{1,25},{9,1},{17,9},{25,17},{2,26},{10... | collective-permute-start | bytes 1572872 | tf_op jit(solution)/shard_map/ppermute | solution.py:701
  366.3 1.6 copy-start.2
  367.9 1.0 copy-start.3
  368.9 0.9 copy-start.4
  416.1 9.4 %copy-start.1 = (bf16[128,4,128]{2,1,0:T(4,128)(2,1)S(1)}, bf16[128,4,128]{2,1,0:T(4,128)(2,1)}, u32[]{:S(2)}) copy-start(bf16[128,4,128]{2,1,0:T(4,128)(2,1)} %param.39) | copy-start | bytes 393220
Sparse Core Ops, SparseCore 0:
  11.5 88.4 all-gather.8
  102.9 72.5 all-gather.10

commit v3 on v2

--- a/solution.py
+++ b/solution.py
@@ -19,6 +19,8 @@
 LOG2E = 1.4426950408889634
 
 HALO = 16
+IN_LANE = 32
+OUT_LANE = 48
 QUAD = 4
 WIDTH = QUAD * P_SIZE
 GROUPS = HEADS // QUAD
@@ -72,6 +74,18 @@
 
 def to_front(cols, group):
     return pltpu.roll(cols, lax.rem(LANES - QUAD * group, LANES), 1)
+
+
+def lane_range(values, first):
+    lane = iota(values.shape, 1)
+    return jnp.where((lane >= first) & (lane < first + RANK), values, 0.0)
+
+
+def out_block(w_ref, row, part):
+    if w_ref.shape[2] == WIDTH:
+        return w_ref[0, row, :, :part]
+    rows = WIDTH // 2
+    return jnp.concatenate([w_ref[0, row, :rows, :part], w_ref[0, row, :rows, part:]], axis=0)
 
 
 def head_only(values, head):
@@ -125,7 +139,7 @@
                 term = mm(normed, wst_ref[r])
                 total = term if total is None else total + term
             st_scr[rows, :] = total
-            adv_ref[rows, :] = total[:, 384:512].astype(BF16)
+            adv_ref[rows, :] = lane_range(total[:, 256:384], IN_LANE).astype(BF16)
 
         project(pl.ds(0, HALO))
 
@@ -196,7 +210,7 @@
 
 
 def scan_kernel(
-    x_ref, g_ref, oup_ref, w_ref, down_ref, vp_ref, gate_ref, u_ref, eloc_ref, ein_ref,
+    x_ref, g_ref, wst_ref, w_ref, down_ref, vp_ref, gate_ref, u_ref, eloc_ref, ein_ref,
     step_ref, cum_ref, cum_t_ref, bs_ref, cs_ref,
     out_ref, o_ref, ent_ref, aux_ref, sg_ref, gup_ref,
     score_scr, acc_scr, side_scr, square_scr,
@@ -243,8 +257,8 @@
         gained = (gated * taps[5:6]).astype(BF16)
         for r in range(row_count):
             cols = slice(r * part, (r + 1) * part)
-            acc_scr[rows, cols] += mm(gained, w_ref[0, r, :, :part])
-        side_scr[rows, :] += mm(gained, down_ref[0])
+            acc_scr[rows, cols] += mm(gained, out_block(w_ref, r, part))
+        side_scr[rows, :] += mm_nt(gained, down_ref[0])
         return before * widen(jnp.exp2(cum[BLOCK - 8 :]))[7:8]
 
     lax.fori_loop(0, blocks, one_block, jnp.ones((1, WIDTH), F32))
@@ -262,18 +276,18 @@
             side = (side_raw * rms).astype(BF16)
             side_grad = None
             for r in range(row_count):
-                term = mm(g_ref[r, rows, :], oup_ref[r])
+                term = mm(g_ref[r, rows, :], wst_ref[r, :, 256:384])
                 side_grad = term if side_grad is None else side_grad + term
-            side_grad = side_grad.astype(BF16)
+            side_grad = lane_range(side_grad, OUT_LANE).astype(BF16)
             product = jnp.sum(side_grad.astype(F32) * side_raw, axis=1, keepdims=True)
             for r in range(row_count):
                 cols = slice(r * part, (r + 1) * part)
                 raw = acc_scr[rows, cols]
                 cot = g_ref[r, rows, :]
                 product = product + jnp.sum(raw * cot.astype(F32), axis=1, keepdims=True)
-                total = x_ref[r, at_rows(k), :].astype(F32) + raw * rms + mm_nt(side, oup_ref[r])
+                total = x_ref[r, at_rows(k), :].astype(F32) + raw * rms + mm_nt(side, wst_ref[r, :, 256:384])
                 out_ref[r, rows, :] = total.astype(BF16)
-                gup_ref[:, cols] += mm_tn(side, cot)[:RANK]
+                gup_ref[:, cols] += mm_tn(side, cot)[OUT_LANE : OUT_LANE + RANK]
             coefficient = rms * rms * rms * product / DI
             lane = iota((BLOCK, LANES), 1)
             aux_ref[rows, :] = jnp.where(lane == 0, rms, coefficient)
@@ -293,7 +307,7 @@
     def _():
         @pl.loop(0, blocks)
         def _(k):
-            sg_t_scr[k] = sg_ref[at_block(k), :].astype(F32).T[:RANK].astype(BF16)
+            sg_t_scr[k] = sg_ref[at_block(k), :].astype(F32).T[OUT_LANE : OUT_LANE + RANK].astype(BF16)
 
     taps = vp_ref[0]
     gdown_ref[0] = jnp.zeros((RANK, WIDTH), F32)
@@ -301,9 +315,9 @@
     def one_block(i, state):
         k = blocks - 1 - i
         rows = at_block(k)
-        dmix = mm_nt(sg_ref[rows, :], down_ref[0])
+        dmix = mm(sg_ref[rows, :], down_ref[0])
         for r in range(row_count):
-            dmix = dmix + mm_nt(g_ref[r, rows, :], w_ref[0, r, :, :part])
+            dmix = dmix + mm_nt(g_ref[r, rows, :], out_block(w_ref, r, part))
         gate = gate_ref[rows, :].astype(F32)
         output = o_ref[rows, :].astype(F32)
         sig = sigmoid(gate)
@@ -350,7 +364,7 @@
         @pl.loop(0, blocks)
         def _(k):
             score_scr[k] = mm_nt(bs_ref[at_block(k), :], cs_ref[at_block(k), :])
-            adv_t_scr[k] = adv_ref[at_rows(k), :].astype(F32).T[:RANK].astype(BF16)
+            adv_t_scr[k] = adv_ref[at_rows(k), :].astype(F32).T[IN_LANE : IN_LANE + RANK].astype(BF16)
 
     keep = iota((BLOCK, BLOCK), 0) <= iota((BLOCK, BLOCK), 1)
     taps = vp_ref[0]
@@ -416,7 +430,7 @@
 
     ig_scr[0:HALO, :WIDTH] = jnp.zeros((HALO, WIDTH), BF16)
     first = spread_back(pl.ds(0, HALO), du_scr[0 : HALO + 8, :], HALO)
-    up_scr[...] = mm_tn(adv_ref[0:HALO, :], first)[:RANK]
+    up_scr[...] = mm_tn(adv_ref[0:HALO, :], first)[IN_LANE : IN_LANE + RANK]
 
     @pl.loop(0, blocks)
     def _(k):
@@ -453,21 +467,20 @@
         def finish(rows, window, count, draw):
             dstate = advances(window, sp_ref[0:4], count).astype(BF16)
             adapt = adg_scr[rows, :].astype(BF16)
+            mixed = adapt if draw is None else adapt + draw
             total = jnp.zeros((count, 1), F32)
             square = jnp.zeros((count, 1), F32)
             grads = []
             for r in range(row_count):
                 cols = slice(r * part, (r + 1) * part)
                 grad = ng_scr[rows, cols] + mm_nt(dstate, wst_ref[r, :, 0:256])
-                grad = grad + mm_nt(adapt, wst_ref[r, :, 384:512])
-                if draw is not None:
-                    grad = grad + mm_nt(draw, wst_ref[r, :, 256:384])
+                grad = grad + mm_nt(mixed, wst_ref[r, :, 256:384])
                 grad = grad * gain_ref[r]
                 piece = x_ref[r, rows, :].astype(F32)
                 total = total + jnp.sum(piece * grad, axis=1, keepdims=True)
                 square = square + jnp.sum(piece * piece, axis=1, keepdims=True)
                 grads.append(grad)
-                in_scr[:, cols] += mm_tn(adapt, normed_ref[rows, cols])[:RANK]
+                in_scr[:, cols] += mm_tn(adapt, normed_ref[rows, cols])[IN_LANE : IN_LANE + RANK]
             inv = lax.rsqrt(square / D + EPS)
             factor = inv * inv * inv * total / D
             for r in range(row_count):
@@ -562,6 +575,283 @@
     own.wait()
 
 
+def start_kernel(
+    x_ref, w_ref, up_ref, p_ref, down_ref, shared_ref, gain_ref, conv_ref, bias_ref, gate_ref, step_ref, rate_ref,
+    skip_ref,
+    x_out, w_out, shared_out, gain_out, vec_out, head_out,
+    block_scr, zero_scr,
+    own_sem, send_sem, recv_sem, row_send, row_recv, col_send, col_recv,
+):
+    col_count, row_count = w_out.shape[:2]
+    high_count = col_count // 2
+    part = x_ref.shape[1]
+    chunk = x_ref.shape[0] // row_count
+    rank_part = up_ref.shape[0] // row_count
+    row = lax.axis_index("row")
+    col = lax.axis_index("col")
+    low = lax.rem(col, 2)
+    high = col // 2
+    core = row + 1 - 2 * lax.rem(row, 2)
+    across = lax.rem(row + 2, row_count)
+    side = col + 1 - 2 * low
+    barrier = pltpu.get_barrier_semaphore()
+    for d in range(1, row_count):
+        pl.semaphore_signal(barrier, inc=1, device_id=on_row(lax.rem(row + d, row_count)), device_id_type=MESH)
+    for d in range(1, col_count):
+        pl.semaphore_signal(barrier, inc=1, device_id=on_col(lax.rem(col + d, col_count)), device_id_type=MESH)
+
+    def paired(value):
+        lane = iota((value.shape[0], LANES), 1) < P_SIZE
+        tiles = [value[:, h * LANES : (h + 1) * LANES].astype(F32) for h in range(QUAD)]
+        turned = [pltpu.roll(tile, P_SIZE, 1) for tile in tiles]
+        gates = [jnp.where(lane, tiles[h], turned[h + 1]) for h in (0, 2)]
+        values = [jnp.where(lane, turned[h], tiles[h + 1]) for h in (0, 2)]
+        return jnp.concatenate(gates + values, axis=1).astype(BF16)
+
+    block_scr[0:part, :] = paired(w_ref[...])
+    ranks = pl.ds(pl.multiple_of(row * rank_part, rank_part), rank_part)
+    block_scr[part : part + rank_part, :] = paired(up_ref[ranks, :])
+    first = part + rank_part
+    half = WIDTH // 2
+    block_scr[first : first + half, :WIDTH] = p_ref[:half, :]
+    block_scr[first : first + half, WIDTH:] = p_ref[half:, :]
+    first = first + half
+    downs = down_ref[ranks, :]
+    block_scr[first : first + rank_part // 2, :WIDTH] = downs[: rank_part // 2]
+    block_scr[first : first + rank_part // 2, WIDTH:] = downs[rank_part // 2 :]
+    zero_scr[...] = jnp.zeros_like(zero_scr)
+    vec_out[col, 0:4, :] = conv_ref[...]
+    vec_out[col, 4:5, :] = bias_ref[...]
+    vec_out[col, 5:6, :] = gate_ref[...]
+    vec_out[col, 6:7, :] = widen(skip_ref[...])
+    lane = iota((1, WIDTH), 1)
+    scalars = jnp.zeros((1, WIDTH), F32)
+    for h in range(QUAD):
+        scalars = jnp.where(lane == h, step_ref[:, h : h + 1], scalars)
+        scalars = jnp.where(lane == QUAD + h, rate_ref[:, h : h + 1], scalars)
+    vec_out[col, 7:8, :] = scalars
+    gain_out[row] = gain_ref[...]
+    pl.semaphore_wait(barrier, row_count + col_count - 2)
+
+    def remote(source, target, sends, recvs, index, device):
+        return pltpu.make_async_remote_copy(
+            src_ref=source, dst_ref=target, send_sem=sends.at[index], recv_sem=recvs.at[index],
+            device_id=device, device_id_type=MESH,
+        )
+
+    own_block = pltpu.make_async_copy(block_scr, w_out.at[col, row], own_sem.at[0])
+    own_block.start()
+
+    def whole_window(target, slot, index, peer):
+        source = x_ref.at[pl.ds(pl.multiple_of(target * chunk - HALO, HALO), chunk + HALO)]
+        return remote(source, x_out.at[slot], row_send, row_recv, index, on_row(peer))
+
+    def first_window(slot, index, peer):
+        source = x_ref.at[pl.ds(0, chunk)]
+        return remote(source, x_out.at[slot, pl.ds(HALO, chunk)], row_send, row_recv, index, on_row(peer))
+
+    def each_window(sending, act):
+        for d in range(1, row_count):
+            peer = lax.rem(row + d, row_count)
+            chosen = peer if sending else row
+            slot = row if sending else lax.rem(row + row_count - d, row_count)
+
+            @pl.when(chosen > 0)
+            def _():
+                act(whole_window(jnp.maximum(chosen, 1), slot, d, peer))
+
+            @pl.when(chosen == 0)
+            def _():
+                act(first_window(slot, d, peer))
+
+    @pl.when(row > 0)
+    def _():
+        source = x_ref.at[pl.ds(pl.multiple_of(jnp.maximum(row, 1) * chunk - HALO, HALO), chunk + HALO)]
+        pltpu.make_async_copy(source, x_out.at[row], own_sem.at[1]).start()
+
+    @pl.when(row == 0)
+    def _():
+        pltpu.make_async_copy(x_ref.at[pl.ds(0, chunk)], x_out.at[row, pl.ds(HALO, chunk)], own_sem.at[1]).start()
+        for r in range(row_count):
+            pltpu.make_async_copy(zero_scr, x_out.at[r, pl.ds(0, HALO)], own_sem.at[3 + r]).start()
+
+    own_shared = pltpu.make_async_copy(shared_ref, shared_out.at[row], own_sem.at[2])
+    own_shared.start()
+    small = []
+    for d in range(1, col_count):
+        peer = lax.rem(col + d, col_count)
+        small.append(remote(vec_out.at[col], vec_out.at[col], col_send, col_recv, d, on_col(peer)))
+    for d in range(1, row_count):
+        peer = lax.rem(row + d, row_count)
+        small.append(remote(shared_ref, shared_out.at[row], row_send, row_recv, row_count + d, on_row(peer)))
+        small.append(
+            remote(gain_out.at[row], gain_out.at[row], row_send, row_recv, 2 * row_count + d, on_row(peer))
+        )
+    for copy in small:
+        copy.start()
+
+    cut = (w_out.shape[2] * 60 // 100 + 8) // 16 * 16
+    spans = (pl.ds(0, cut), pl.ds(cut, w_out.shape[2] - cut))
+    has_up = high < high_count - 1
+    has_down = high > 0
+    routes = {
+        "up": (0, has_up, on_col(lax.rem(col + 2, col_count))),
+        "down": (1, has_down, on_col(lax.rem(col + col_count - 2, col_count))),
+        "x": (2, None, on_col(side)),
+        "y": (3, None, on_row(across)),
+        "core": (4, None, on_row(core)),
+    }
+
+    def piece(section, c, r, kind, device):
+        ref = w_out.at[c, r, spans[section]]
+        return pltpu.make_async_remote_copy(
+            src_ref=ref, dst_ref=ref, send_sem=send_sem.at[section, c, r, kind],
+            recv_sem=recv_sem.at[section, c, r], device_id=device, device_id_type=MESH,
+        )
+
+    def event(starting, section, c, r, names, arrives=True, valid=None):
+        def act():
+            if starting and arrives:
+                piece(section, c, r, 4, on_row(core)).wait_recv()
+            for name in names:
+                kind, allowed, device = routes[name]
+                copy = piece(section, c, r, kind, device)
+                if allowed is None:
+                    copy.start() if starting else copy.wait_send()
+                else:
+
+                    @pl.when(allowed)
+                    def _():
+                        copy.start() if starting else copy.wait_send()
+
+        if valid is None:
+            act()
+        else:
+            pl.when(valid)(act)
+
+    def far(column, step, distance):
+        return lax.rem(column + step * distance + 4 * col_count, col_count)
+
+    def within(step, distance):
+        return high >= distance if step < 0 else high + distance < high_count
+
+    onward = {-2: "up", 2: "down"}
+
+    def along(starting, section, distance):
+        for step in (-2, 2):
+            valid = within(step, distance)
+            if section == 0:
+                names = (onward[step], "y", "x", "core")
+                event(starting, 0, far(col, step, distance), row, names, valid=valid)
+            else:
+                for column, r in ((col, row), (side, row), (col, across), (side, across)):
+                    event(starting, 1, far(column, step, distance), r, (onward[step], "core"), valid=valid)
+
+    def over(starting, distance):
+        for step in (-2, 2):
+            valid = within(step, distance)
+            event(starting, 0, far(side, step, distance), row, ("core",), valid=valid)
+            event(starting, 0, far(col, step, distance), across, ("x", "core"), valid=valid)
+
+    def last(starting, distance):
+        for step in (-2, 2):
+            event(starting, 0, far(side, step, distance), across, ("core",), valid=within(step, distance))
+
+    def relay(starting):
+        event(starting, 1, col, row, ("x", "y"), arrives=False)
+        event(starting, 0, col, row, ("up", "down", "y", "x"), arrives=False)
+        event(starting, 1, col, row, ("up", "down", "core"), arrives=False)
+        event(starting, 0, col, row, ("core",), arrives=False)
+        event(starting, 1, side, row, ("y", "up", "down", "core"))
+        event(starting, 1, col, across, ("up", "down", "core"))
+        along(starting, 0, 1)
+        event(starting, 1, side, across, ("up", "down", "core"))
+        if starting:
+            each_window(True, lambda copy: copy.start())
+        event(starting, 0, col, across, ("x", "core"))
+        for d in range(2, high_count):
+            along(starting, 0, d)
+            along(starting, 1, d - 1)
+            if d == 2:
+                event(starting, 0, side, row, ("core",))
+                over(starting, 1)
+                event(starting, 0, side, across, ("core",))
+            else:
+                over(starting, d - 1)
+                last(starting, d - 2)
+        along(starting, 1, high_count - 1)
+        over(starting, high_count - 1)
+        if high_count > 2:
+            last(starting, high_count - 2)
+        last(starting, high_count - 1)
+
+    own_block.wait()
+    relay(True)
+    for copy in small:
+        copy.wait()
+    lane = iota((1, LANES), 1) < QUAD
+    steps = jnp.zeros((1, LANES), F32)
+    rates = jnp.zeros((1, LANES), F32)
+    for c in range(col_count):
+        values = vec_out[c, 7:8, :LANES]
+        steps = steps + pltpu.roll(jnp.where(lane, values, 0.0), (QUAD * c) % LANES, 1)
+        values = pltpu.roll(values, LANES - QUAD, 1)
+        rates = rates + pltpu.roll(jnp.where(lane, values, 0.0), (QUAD * c) % LANES, 1)
+    head_out[...] = jnp.concatenate([steps, rates, jnp.zeros((6, LANES), F32)], axis=0)
+    own_shared.wait()
+    each_window(True, lambda copy: copy.wait_send())
+    each_window(False, lambda copy: copy.wait_recv())
+
+    @pl.when(row > 0)
+    def _():
+        source = x_ref.at[pl.ds(0, chunk + HALO)]
+        pltpu.make_async_copy(source, x_out.at[row], own_sem.at[1]).wait()
+
+    @pl.when(row == 0)
+    def _():
+        pltpu.make_async_copy(x_ref.at[pl.ds(0, chunk)], x_out.at[row, pl.ds(HALO, chunk)], own_sem.at[1]).wait()
+        for r in range(row_count):
+            pltpu.make_async_copy(zero_scr, x_out.at[r, pl.ds(0, HALO)], own_sem.at[3 + r]).wait()
+
+    core_across = lax.rem(core + 2, row_count)
+    for c in range(col_count):
+        for r in (core, core_across):
+            for section in range(2):
+                piece(section, c, r, 4, on_row(core)).wait_recv()
+    relay(False)
+
+
+def start_exchange(x, w, up, p, down, shared, vectors, row_count, col_count):
+    part = x.shape[1]
+    rank_part = up.shape[0] // row_count
+    block_rows = part + rank_part + WIDTH // 2 + rank_part // 2
+    chunk = x.shape[0] // row_count
+    vmem = pl.BlockSpec(memory_space=pltpu.VMEM)
+    anywhere = pl.BlockSpec(memory_space=pl.ANY)
+    dma = pltpu.SemaphoreType.DMA
+    return pl.pallas_call(
+        start_kernel,
+        in_specs=[anywhere] + [vmem] * (5 + len(vectors)),
+        out_specs=[anywhere] * 3 + [vmem] * 3,
+        out_shape=[
+            jax.ShapeDtypeStruct((row_count, chunk + HALO, part), BF16),
+            jax.ShapeDtypeStruct((col_count, row_count, block_rows, 2 * WIDTH), BF16),
+            jax.ShapeDtypeStruct((row_count,) + shared.shape, BF16),
+            jax.ShapeDtypeStruct((row_count, 1, part), F32),
+            jax.ShapeDtypeStruct((col_count, 8, WIDTH), F32),
+            jax.ShapeDtypeStruct((8, LANES), F32),
+        ],
+        scratch_shapes=[
+            pltpu.VMEM((block_rows, 2 * WIDTH), BF16), pltpu.VMEM((HALO, part), BF16),
+            dma((3 + row_count,)), dma((2, col_count, row_count, 5)), dma((2, col_count, row_count)),
+            dma((3 * row_count,)), dma((3 * row_count,)), dma((col_count,)), dma((col_count,)),
+        ],
+        compiler_params=pltpu.CompilerParams(
+            collective_id=1, has_side_effects=True, vmem_limit_bytes=VMEM_BYTES
+        ),
+    )(x, w, up, p, down, shared, *vectors)
+
+
 def finish_exchange(corr, wide, thin):
     row_count = corr.shape[0]
     col_count = wide.shape[1]
@@ -585,7 +875,7 @@
             dma((2 * col_count,)), dma((2 * col_count,)), dma((row_count,)), dma((row_count,)),
         ],
         compiler_params=pltpu.CompilerParams(
-            collective_id=0, has_side_effects=True, vmem_limit_bytes=VMEM_BYTES // 2
+            collective_id=0, has_side_effects=True, vmem_limit_bytes=VMEM_BYTES
         ),
     )(corr, wide, thin)
 
@@ -608,7 +898,19 @@
     return pl.BlockSpec(block, lambda c: (0, c) + (0,) * (len(shape) - 2))
 
 
-KINDS = {"s": second_spec, "a": whole_spec, "c": lead_spec, "l": lane_spec}
+def front_spec(shape):
+    if shape[2] % 3 == 0 and shape[2] // 3 * 2 >= WIDTH and shape[3] == 2 * WIDTH and shape[1] == 4:
+        return pl.BlockSpec((1, shape[1], shape[2] // 3 * 2, shape[3]), lambda c: (c, 0, 0, 0))
+    return lead_spec(shape)
+
+
+def back_spec(shape):
+    if shape[2] > WIDTH:
+        return pl.BlockSpec((1, shape[1], shape[2] // 3, shape[3]), lambda c: (c, 0, 2, 0))
+    return lead_spec(shape)
+
+
+KINDS = {"w": front_spec, "p": back_spec, "s": second_spec, "a": whole_spec, "c": lead_spec, "l": lane_spec}
 
 
 def grouped_call(kernel, inputs, kinds, outputs, out_kinds, scratch, flops=0):
@@ -725,64 +1027,81 @@
     rank_share = rank_total // col_count
     adapter = lax.dynamic_index_in_dim(adapter_id, col // seq_cols, keepdims=False)
 
-    head = jnp.zeros((HALO, part), BF16)
-    if seq_cols > 1:
-        pairs = [(i, (i + 1) % col_count) for i in range(col_count)]
-        head = lax.ppermute(block_in[-HALO:], "col", pairs)
-        head = jnp.where(lax.rem(col, seq_cols) > 0, head, jnp.zeros_like(head))
-    padded = jnp.concatenate([head, block_in], axis=0)
-    windows = jnp.stack([padded[r * chunk : r * chunk + total_rows] for r in range(row_count)])
-    x_rows = lax.all_to_all(windows, "row", 0, 0, tiled=True)
-    g_rows = lax.all_to_all(cotangent.reshape(row_count, chunk, part), "row", 0, 0, tiled=True)
-
-    def split_pairs(value):
-        value = value.reshape(value.shape[0], heads_here, 2, P_SIZE)
-        return jnp.swapaxes(value, 1, 2).reshape(value.shape[0], 2, local)
-
-    up_part = lax.dynamic_slice_in_dim(adapt_in_up, row * rank_part, rank_part, 0)
-    w_block = jnp.concatenate([split_pairs(proj_inner), split_pairs(up_part)], axis=0)
-    w_all = lax.all_gather(w_block.reshape(part + rank_part, 2 * local), ("col", "row"))
-    w_all = w_all.reshape(col_count, row_count, part + rank_part, 2, local)
-    w_all = to_groups(w_all, heads_here).reshape(GROUPS, row_count, part + rank_part, 2 * WIDTH)
-    up_all = w_all[:, :, part:, :].reshape(GROUPS, rank_total, 2 * WIDTH)
-    up_all = lax.dynamic_slice_in_dim(up_all, adapter * RANK, RANK, 1)
-    up_all = jnp.pad(up_all, ((0, 0), (0, LANES - RANK), (0, 0)))
-
-    down_part = lax.dynamic_slice_in_dim(adapt_out_down, row * rank_part, rank_part, 0)
-    p_block = jnp.concatenate([proj_out, down_part.T], axis=1)
-    p_all = lax.all_gather(p_block, ("col", "row")).reshape(col_count, row_count, local, part + rank_part)
-    if heads_here != QUAD:
-        p_all = jnp.moveaxis(p_all, 1, 0).reshape(row_count, GROUPS, WIDTH, part + rank_part)
-        p_all = jnp.moveaxis(p_all, 0, 1)
-    down_all = jnp.swapaxes(p_all[..., part:], 1, 2).reshape(GROUPS, WIDTH, rank_total)
-    down_all = pad_lanes(lax.dynamic_slice_in_dim(down_all, adapter * RANK, RANK, 2), LANES)
-
     in_down = lax.dynamic_slice_in_dim(adapt_in_down, adapter * RANK, RANK, 1)
     out_up = lax.dynamic_slice_in_dim(adapt_out_up, adapter * RANK, RANK, 1)
-    state_width = proj_state.shape[1]
-    shared = lax.all_gather(jnp.concatenate([proj_state, in_down, out_up], axis=1), "row")
-    w_state = jnp.concatenate(
-        [
-            pad_lanes(shared[..., :state_width], 384),
-            pad_lanes(shared[..., state_width : state_width + RANK], LANES),
-        ],
-        axis=2,
-    )
-    out_up_all = pad_lanes(shared[..., state_width + RANK :], LANES)
-    gain_all = lax.all_gather(norm_gain, "row").reshape(row_count, 1, part)
-
-    scalars = jnp.concatenate([step_bias, decay_log, skip_gain])
-    vectors = jnp.concatenate(
-        [conv_inner, conv_inner_bias[None], gate_gain[None], pad_lanes(scalars, local)[None]], axis=0
-    )
-    vectors = lax.all_gather(vectors, "col")
-    scalars = vectors[:, 6, : 3 * heads_here].reshape(col_count, 3, heads_here)
-    scalars = jnp.swapaxes(scalars, 0, 1).reshape(3, HEADS)
-    head_rows = jnp.pad(scalars[:2], ((0, 6), (0, LANES - HEADS)))
-    skip_wide = jnp.repeat(scalars[2], P_SIZE).reshape(GROUPS, 1, WIDTH)
-    vectors = jnp.concatenate(
-        [to_groups(vectors[:, :6], heads_here), skip_wide, jnp.zeros_like(skip_wide)], axis=1
-    )
+    shared = pad_lanes(jnp.concatenate([proj_state, in_down, out_up], axis=1), 384)
+    relayed = row_count == 4 and heads_here == QUAD and seq_cols == 1 and part == WIDTH
+    if relayed:
+        x_rows, w_all, w_state, gain_all, vectors, head_rows = start_exchange(
+            block_in, proj_inner.reshape(part, 2 * local), adapt_in_up.reshape(rank_total, 2 * local), proj_out,
+            adapt_out_down, shared,
+            (
+                norm_gain[None], conv_inner, conv_inner_bias[None], gate_gain[None], step_bias[None],
+                decay_log[None], skip_gain[None],
+            ),
+            row_count, col_count,
+        )
+        per_part = rank_part // RANK
+        source = adapter // per_part
+        place = lax.rem(adapter, per_part)
+        zero = jnp.int32(0)
+        up_all = lax.dynamic_slice(
+            w_all, (zero, source, part + place * RANK, zero), (GROUPS, 1, RANK, 2 * WIDTH)
+        )[:, 0]
+        down_all = lax.dynamic_slice(
+            w_all, (zero, source, jnp.int32(part + rank_part + WIDTH // 2), place * WIDTH), (GROUPS, 1, RANK, WIDTH)
+        )[:, 0]
+        p_all = w_all
+        g_rows = lax.all_to_all(cotangent.reshape(row_count, chunk, part), "row", 0, 0, tiled=True)
+    else:
+        head = jnp.zeros((HALO, part), BF16)
+        if seq_cols > 1:
+            pairs = [(i, (i + 1) % col_count) for i in range(col_count)]
+            head = lax.ppermute(block_in[-HALO:], "col", pairs)
+            head = jnp.where(lax.rem(col, seq_cols) > 0, head, jnp.zeros_like(head))
+        padded = jnp.concatenate([head, block_in], axis=0)
+        windows = jnp.stack([padded[r * chunk : r * chunk + total_rows] for r in range(row_count)])
+        x_rows = lax.all_to_all(windows, "row", 0, 0, tiled=True)
+        g_rows = lax.all_to_all(cotangent.reshape(row_count, chunk, part), "row", 0, 0, tiled=True)
+
+        def split_pairs(value):
+            value = value.reshape(value.shape[0], heads_here, 2, P_SIZE)
+            return jnp.swapaxes(value, 1, 2).reshape(value.shape[0], 2, local)
+
+        up_part = lax.dynamic_slice_in_dim(adapt_in_up, row * rank_part, rank_part, 0)
+        w_block = jnp.concatenate([split_pairs(proj_inner), split_pairs(up_part)], axis=0)
+        w_all = lax.all_gather(w_block.reshape(part + rank_part, 2 * local), ("col", "row"))
+        w_all = w_all.reshape(col_count, row_count, part + rank_part, 2, local)
+        w_all = to_groups(w_all, heads_here).reshape(GROUPS, row_count, part + rank_part, 2 * WIDTH)
+        up_all = w_all[:, :, part:, :].reshape(GROUPS, rank_total, 2 * WIDTH)
+        up_all = lax.dynamic_slice_in_dim(up_all, adapter * RANK, RANK, 1)
+
+        down_part = lax.dynamic_slice_in_dim(adapt_out_down, row * rank_part, rank_part, 0)
+        p_block = jnp.concatenate([proj_out, down_part.T], axis=1)
+        p_all = lax.all_gather(p_block, ("col", "row")).reshape(col_count, row_count, local, part + rank_part)
+        if heads_here != QUAD:
+            p_all = jnp.moveaxis(p_all, 1, 0).reshape(row_count, GROUPS, WIDTH, part + rank_part)
+            p_all = jnp.moveaxis(p_all, 0, 1)
+        down_all = jnp.swapaxes(p_all[..., part:], 1, 2).reshape(GROUPS, WIDTH, rank_total)
+        down_all = jnp.swapaxes(lax.dynamic_slice_in_dim(down_all, adapter * RANK, RANK, 2), 1, 2)
+
+        w_state = lax.all_gather(shared, "row")
+        gain_all = lax.all_gather(norm_gain, "row").reshape(row_count, 1, part)
+
+        scalars = jnp.concatenate([step_bias, decay_log, skip_gain])
+        vectors = jnp.concatenate(
+            [conv_inner, conv_inner_bias[None], gate_gain[None], pad_lanes(scalars, local)[None]], axis=0
+        )
+        vectors = lax.all_gather(vectors, "col")
+        scalars = vectors[:, 6, : 3 * heads_here].reshape(col_count, 3, heads_here)
+        scalars = jnp.swapaxes(scalars, 0, 1).reshape(3, HEADS)
+        head_rows = jnp.pad(scalars[:2], ((0, 6), (0, LANES - HEADS)))
+        skip_wide = jnp.repeat(scalars[2], P_SIZE).reshape(GROUPS, 1, WIDTH)
+        vectors = jnp.concatenate(
+            [to_groups(vectors[:, :6], heads_here), skip_wide, jnp.zeros_like(skip_wide)], axis=1
+        )
+    up_all = jnp.pad(up_all, ((0, 0), (IN_LANE, LANES - IN_LANE - RANK), (0, 0)))
+    down_all = jnp.pad(down_all, ((0, 0), (OUT_LANE, LANES - OUT_LANE - RANK), (0, 0)))
     state_taps = jnp.concatenate([conv_state, conv_state_bias[None], jnp.zeros((3, 256), F32)], axis=0)
 
     token_f32 = ((chunk, LANES), F32)
@@ -796,22 +1115,22 @@
     ) = grouped_call(
         front_kernel,
         (x_rows, gain_all, w_state, state_taps, head_rows, w_all, up_all, vectors),
-        "aaaaaccc",
+        "aaaaawcc",
         [
             ((total_rows, D), BF16), ((chunk, 256), F32), token_f32, token_f32, token_f32,
             ((GROUPS, QUAD, chunk), F32), token_low, token_low, turned, ((total_rows, LANES), BF16),
             inner_low, inner_low, states, ((STATES, DI), BF16), ((8, DI), F32),
         ],
         "aaaaaaaaaalllll",
-        [((total_rows, 512), F32), turned, ((total_rows, WIDTH), F32)],
+        [((total_rows, 384), F32), turned, ((total_rows, WIDTH), F32)],
         flops=int(45e9),
     )
     decay = dec[0:1]
     entry = carry_in(fin, decay, row_count, col_count, seq_cols, True)
     out_rows, o, ent, aux, side_grad, out_up_grad = grouped_call(
         scan_kernel,
-        (x_rows, g_rows, out_up_all, p_all, down_all, vectors, gate, u, eloc, entry, step, cum, cum_t, bs, cs),
-        "aaacccllllaacaa",
+        (x_rows, g_rows, w_state, p_all, down_all, vectors, gate, u, eloc, entry, step, cum, cum_t, bs, cs),
+        "aaapccllllaacaa",
         [
             ((row_count, chunk, part), BF16), inner_low, ((blocks, STATES, DI), BF16), token_f32, token_low,
             ((RANK, D), F32),
@@ -824,7 +1143,7 @@
     dgate, dy, gloc, gfin, out_down_grad = grouped_call(
         gate_kernel,
         (g_rows, p_all, side_grad, down_all, vectors, gate, o, aux, cum, cs_t),
-        "acaccllaaa",
+        "apaccllaaa",
         [inner_low, inner_low, states, ((STATES, DI), BF16), ((GROUPS, RANK, WIDTH), F32)],
         "llllc",
         [((blocks, RANK, BLOCK), BF16)],
@@ -838,7 +1157,7 @@
             u, o, dy, dgate, ent, gloc, exit_grad, step, cum, cum_t, raw, scpre, bs, cs,
             out_down_grad, out_up_grad,
         ),
-        "aaaaccacaalllllllaacaaaaca",
+        "aaaawcacaalllllllaacaaaaca",
         [
             ((row_count, total_rows, part), BF16), ((row_count, GROUPS, RANK // row_count, 3 * WIDTH), F32),
             ((row_count, 2 * RANK, part), F32),

time: 434 us -> 418 us (0.963)
  Pallas kernels: 236 us -> 321 us
  blocking collectives: 72.9 us -> 0 us
  between operations: 15.2 us -> 4.17 us
  waiting for transfers between devices: 49.4 us -> 43.7 us
    pallas_call x0 -> x1, Pallas kernels: none -> 84.8 us  [start_exchange(): pl.pallas_call(start_kernel, in_specs=[anywhere] + [vmem] * (5 + len(vect...]
    all_gather x3 -> x0, blocking collectives: 72.9 us -> none  [the longest x1 35.7 us: per_device(): lax.all_gather(jnp.concatenate([proj_state, in_down, out_up], axis=1), 'r...]
    all_gather x2 -> x0, waiting for transfers between devices: 23.9 us -> none  [the longest x1 21.4 us: per_device(): lax.all_gather(p_block, ('col', 'row'))]
    ppermute x4, waiting for transfers between devices: 17 us -> 34.3 us  [carry_in(): other = lax.ppermute(total, 'row', pairs).astype(F32)]
    all_to_all x1 -> x0, starting transfers between devices: 4.59 us -> none  [per_device(): x_rows = lax.all_to_all(windows, 'row', 0, 0, tiled=True)]
  transfers between devices with their start and end apart: 12 -> 9, of which waited for: 6 -> 5; matrix products, arithmetic and copies ran while one was open for 9% -> 6% of each run, Pallas kernels for 38% -> 29%
where the time goes in v3:
time: 418 us; the launch traced here: 416 us
  Pallas kernels  321 us (77%)
  waiting for transfers between devices  43.7 us (10%)
  local copies, waits for them, and re-layouts  23.2 us (6%)
  other arithmetic  16.6 us (4%)
  starting transfers between devices  8.07 us (2%)
    pallas_call x4, Pallas kernels, grouped_call(): pl.pallas_call(kernel, grid=(GROUPS,), in_specs=[KINDS[kind](value.shape)...  194 us
    pallas_call x1, Pallas kernels, start_exchange(): pl.pallas_call(start_kernel, in_specs=[anywhere] + [vmem] * (5 + len(vect...  84.8 us
    pallas_call x1, Pallas kernels, finish_exchange(): pl.pallas_call(tail_kernel, in_specs=[anywhere, vmem, vmem], out_specs=[a...  41.9 us
    ppermute x4, waiting for transfers between devices, carry_in(): other = lax.ppermute(total, 'row', pairs).astype(F32)  34.3 us
    ppermute x3, waiting for transfers between devices, rows_to_parts(): piece = lax.ppermute(lax.dynamic_index_in_dim(value, peer), 'row', pairs)  8.58 us
  transfers between devices with their start and end apart: 9, of which 5 were waited for; matrix products, arithmetic and copies ran while one was open for 6% of the time, Pallas kernels for 29%

profile of v3, /device:TPU:0, one launch (start us, length us, event | category | flops | bytes accessed | tf_op | source)
XLA Modules:
  0.0 416.4 jit_solution(17797703761402494612)
XLA Ops:
  0.6 1.2 dynamic_slice.29
  5.1 1.7 copy.51
  6.8 1.6 copy.52
  8.4 1.1 copy.40
  9.6 1.0 constant_dynamic-slice_fusion.3
  10.6 0.8 fusion.8.shared_ref
  11.4 84.8 %shard_map.226 = (bf16[4,1040,256]{2,1,0:T(8,128)(2,1)}, bf16[8,4,432,512]{3,2,1,0:T(8,128)(2,1)}, bf16[4,256,384]{2,1,0:T(8,128)(2,1)}, f32[4,1,256]{2,1,0:T(1,...) custom-call(bf16[4096,256]{1,0:T(8,128)(2,1)} %x_ref.1, bf16[256,512]{1,0:T(8,128)(2,1)} %bitcast.66, ...), custom_call_target="tpu_custom_call" | custom-call | tf_op jit(solution)/shard_map/pallas_call | solution.py:832
  96.2 0.9 dynamic-slice_bitcast_fusion
  97.1 1.1 pad.20.up_ref
  98.2 0.7 maximum_maximum_fusion.sp_ref
  98.9 44.7 %shard_map.227 = (bf16[1040,1024]{1,0:T(8,128)(2,1)}, f32[1024,256]{1,0:T(8,128)}, f32[1024,128]{1,0:T(8,128)}, f32[1024,128]{1,0:T(8,128)}, f32[1024,128]{1,0:T...) custom-call(bf16[4,1040,256]{2,1,0:T(8,128)(2,1)} %get-tuple-element, ...), custom_call_target="tpu_custom_call" | custom-call | flops 44999999488 | bytes 40000000 | tf_op jit(solution)/shard_map/pallas_call | solution.py:917
  143.6 0.6 collective-permute-start
  144.2 3.6 all-to-all-start
  147.8 0.8 slice.87
  148.7 0.5 collective-permute-start.1
  149.2 0.8 collective-permute-done.1
  150.0 1.1 fusion.1
  151.0 2.0 collective-permute-start.2
  153.1 0.8 dynamic-slice_bitcast_fusion.1
  153.9 0.8 pad.19.down_ref
  154.8 30.1 %collective-permute-done.2 = bf16[128,2048]{1,0:T(8,128)(2,1)S(1)} collective-permute-done((bf16[128,2048]{1,0:T(8,128)(2,1)}, bf16[128,2048]{1,0:T(8,128)(2,1)S(1)}, u32[]{:S(2)}, u32[]{:S(2)}) %collective-permute-start.2) | collective-permute-done | bytes 524320 | tf_op jit(solution)/shard_map/ppermute | solution.py:974
  184.9 1.2 add_select_fusion.1.ein_ref
  186.1 1.3 copy-done
  187.4 46.7 %shard_map.228 = (bf16[4,1024,256]{2,1,0:T(8,128)(2,1)}, bf16[1024,2048]{1,0:T(8,128)(2,1)}, bf16[4,128,2048]{2,1,0:T(8,128)(2,1)}, f32[1024,128]{1,0:T(8,128)},...) custom-call(bf16[4,1040,256]{2,1,0:T(8,128)(2,1)} %get-tuple-element.80.x_ref, bf16[4,1024,256]{2,1,0:T(8,128)(2,1)} %copy-done, ...), custom_call_target="tpu_custom_call" | custom-call | flops 44999999488 | bytes 40000000 | tf_op jit(solution)/shard_map/pallas_call | solution.py:917
  234.1 24.9 %shard_map.229 = (bf16[1024,2048]{1,0:T(8,128)(2,1)}, bf16[1024,2048]{1,0:T(8,128)(2,1)}, f32[4,128,2048]{2,1,0:T(8,128)}, bf16[128,2048]{1,0:T(8,128)(2,1)}, f32[8,16,256]{2,1,0:T(8,128)}) custom-call(bf16[4,1024,256]{2,1,0:T(8,128)(2,1)} %copy-done, bf16[8,4,432,512]{3,2,1,0:T(8,128)(2,1)} %get-tuple-element.82.w_ref, ...), custom_call_target="tpu_custom_call" | custom-call | flops 24999999488 | bytes 40000000 | tf_op jit(solution)/shard_map/pallas_call | solution.py:917
  259.2 0.8 constant_dynamic-slice_fusion.2
  260.0 0.5 collective-permute-start.3
  260.5 0.8 collective-permute-done.6
  261.3 1.3 fusion.3
  262.9 8.6 %collective-permute-done.3 = bf16[1,1024,256]{2,1,0:T(8,128)(2,1)} collective-permute-done((bf16[1,1024,256]{2,1,0:T(8,128)(2,1)}, bf16[1,1024,256]{2,1,0:T(8,128)(2,1)}, u32[]{:S(2)}, u32[]{:S(2)}) %collective-permute-start.3) | collective-permute-done | bytes 524320 | tf_op jit(solution)/shard_map/ppermute | solution.py:1003
  271.5 2.2 constant_dynamic-slice_fusion
  273.7 0.5 collective-permute-start.4
  274.2 3.4 collective-permute-done.7
  277.6 2.2 add_select_fusion.gin_ref
  279.8 77.5 %shard_map.230 = (bf16[4,1040,256]{2,1,0:T(8,128)(2,1)}, f32[4,8,4,768]{3,2,1,0:T(4,128)}, f32[4,32,256]{2,1,0:T(8,128)}) custom-call(bf16[4,1040,256]{2,1,0:T(8,128)(2,1)} %get-tuple-element.80.x_ref, f32[4,1,256]{2,1,0:T(1,128)} %get-tuple-element.84.gain_ref, bf16[1040,1024]{1,0:T(8,128)(2,1)} %get-tuple-element.97.normed_ref, ...), custom_call_target="tpu_custom_call" | custom-call | flops 74999996416 | bytes 40000000 | tf_op jit(solution)/shard_map/pallas_call | solution.py:917
  357.3 41.9 %shard_map.231 = (bf16[4,1040,256]{2,1,0:T(8,128)(2,1)}, f32[4,8,4,768]{3,2,1,0:T(4,128)}, f32[8,32,256]{2,1,0:T(8,128)}) custom-call(bf16[4,1040,256]{2,1,0:T(8,128)(2,1)} %get-tuple-element.112.corr_ref, f32[4,8,4,768]{3,2,1,0:T(4,128)} %get-tuple-element.113.wide_ref, f32[4,32,256]{2,1,0:T(8,128)} %get-tuple-element.114.thin_ref), custom_call_target="tpu_custom_call" | custom-call | tf_op jit(solution)/shard_map/pallas_call | solution.py:862
  399.2 1.7 slice.88
  401.0 4.1 convert_add_fusion
  405.9 0.7 slice.107
  406.7 0.8 copy.46
  407.6 0.8 slice_convert_fusion
  408.3 1.3 fusion.14
  409.6 1.1 constant_dynamic-update-slice_fusion.1
  410.7 0.6 dynamic-slice_bitcast_fusion.2
  411.4 1.3 fusion.12
  412.7 1.3 fusion.10
  414.0 1.1 constant_dynamic-update-slice_fusion
  415.1 1.3 copy-done.2
  (35 shorter events, 1.4 us)
Async XLA Ops:
  5.1 93.1 %copy-start.6 = (f32[4,256]{1,0:T(4,128)S(1)}, f32[4,256]{1,0:T(4,128)}, u32[]{:S(2)}) copy-start(f32[4,256]{1,0:T(4,128)} %param.31) | copy-start | bytes 12292
  5.1 93.1 %copy-start.7 = (f32[256]{0:T(256)S(1)}, f32[256]{0:T(256)}, u32[]{:S(2)}) copy-start(f32[256]{0:T(256)} %param.32) | copy-start | bytes 3076
  143.6 6.4 %copy-start.3 = (bf16[128,2048]{1,0:T(8,128)(2,1)S(1)}, bf16[128,2048]{1,0:T(8,128)(2,1)}, u32[]{:S(2)}) copy-start(bf16[128,2048]{1,0:T(8,128)(2,1)} %get-tuple-element.89) | copy-start | bytes 1572868
  143.6 6.4 %collective-permute-start = (bf16[128,2048]{1,0:T(8,128)(2,1)}, bf16[128,2048]{1,0:T(8,128)(2,1)S(1)}, u32[]{:S(2)}, u32[]{:S(2)}) collective-permute-start(bf16[128,2048]{1,0:T(8,128)(2,1)} %get-tuple-element.89), channel_id=1, source_target_pairs={{0,8},{8,0},{16,24},{24,16},{1,9},{9,1},{17,25},{25,17},{2,10},{10... | collective-permute-start | bytes 1572872 | tf_op jit(solution)/shard_map/ppermute | solution.py:974
  144.2 41.8 %all-to-all-start = ((bf16[4,1024,256]{2,1,0:T(8,128)(2,1)}), bf16[4,1024,256]{2,1,0:T(8,128)(2,1)S(1)}, u32[]{:S(2)}, u32[]{:S(2)}) async-start(bf16[4,1024,256]{2,1,0:T(8,128)(2,1)} %bitcast.7), calls=%async_computation | async-start | bytes 4194304 | tf_op jit(solution)/shard_map/all_to_all | solution.py:1055
  148.7 1.3 collective-permute-start.1
  151.0 33.8 %collective-permute-start.2 = (bf16[128,2048]{1,0:T(8,128)(2,1)}, bf16[128,2048]{1,0:T(8,128)(2,1)S(1)}, u32[]{:S(2)}, u32[]{:S(2)}) collective-permute-start(bf16[128,2048]{1,0:T(8,128)(2,1)} %fusion.1), channel_id=1, source_target_pairs={{0,16},{8,24},{16,0},{24,8},{1,17},{9,25},{17,1},{25,9},{2,18},{10... | collective-permute-start | bytes 1572872 | tf_op jit(solution)/shard_map/ppermute | solution.py:974
  186.1 1.3 copy-start
  234.1 25.1 %copy-start.1 = (bf16[4,1024,256]{2,1,0:T(8,128)(2,1)S(1)}, bf16[4,1024,256]{2,1,0:T(8,128)(2,1)}, u32[]{:S(2)}) copy-start(bf16[4,1024,256]{2,1,0:T(8,128)(2,1)} %get-tuple-element.96) | copy-start | bytes 6291460
  234.1 28.7 %copy-start.8 = (s32[8]{0:T(128)S(1)}, s32[8]{0:T(128)}, u32[]{:S(2)}) copy-start(s32[8]{0:T(128)} %param.42) | copy-start | bytes 100
  259.1 2.2 collective-permute-start.6
  260.0 11.5 %collective-permute-start.3 = (bf16[1,1024,256]{2,1,0:T(8,128)(2,1)}, bf16[1,1024,256]{2,1,0:T(8,128)(2,1)}, u32[]{:S(2)}, u32[]{:S(2)}) collective-permute-start(bf16[1,1024,256]{2,1,0:T(8,128)(2,1)} %constant_dynamic-slice_fusion.2), channel_id=1, source_target_pairs={{0,8},{8,16},{16,24},{24,0},{1,9},{9,17},{17,25},{25,1},{2,10},{10... | collective-permute-start | bytes 1572872 | tf_op jit(solution)/shard_map/ppermute | solution.py:1003
  262.6 15.0 %collective-permute-start.7 = (bf16[128,2048]{1,0:T(8,128)(2,1)S(1)}, bf16[128,2048]{1,0:T(8,128)(2,1)}, u32[]{:S(2)}, u32[]{:S(2)}) collective-permute-start(bf16[128,2048]{1,0:T(8,128)(2,1)S(1)} %fusion.3), channel_id=1, source_target_pairs={{0,16},{8,24},{16,0},{24,8},{1,17},{9,25},{17,1},{25,9},{2,18},{10... | collective-permute-start | bytes 1572872 | tf_op jit(solution)/shard_map/ppermute | solution.py:974
  273.7 136.0 %collective-permute-start.4 = (bf16[1,1024,256]{2,1,0:T(8,128)(2,1)}, bf16[1,1024,256]{2,1,0:T(8,128)(2,1)}, u32[]{:S(2)}, u32[]{:S(2)}) collective-permute-start(bf16[1,1024,256]{2,1,0:T(8,128)(2,1)} %get-tuple-element.137), channel_id=1, source_target_pairs={{0,16},{8,24},{16,0},{24,8},{1,17},{9,25},{17,1},{25,9},{2,18},{10... | collective-permute-start | bytes 1572872 | tf_op jit(solution)/shard_map/ppermute | solution.py:1003
  274.2 139.8 %collective-permute-start.5 = (bf16[1,1024,256]{2,1,0:T(8,128)(2,1)}, bf16[1,1024,256]{2,1,0:T(8,128)(2,1)}, u32[]{:S(2)}, u32[]{:S(2)}) collective-permute-start(bf16[1,1024,256]{2,1,0:T(8,128)(2,1)} %get-tuple-element.136), channel_id=1, source_target_pairs={{0,24},{8,0},{16,8},{24,16},{1,25},{9,1},{17,9},{25,17},{2,26},{10... | collective-permute-start | bytes 1572872 | tf_op jit(solution)/shard_map/ppermute | solution.py:1003
  401.0 4.2 copy-start.4
  401.0 4.6 %copy-start.5 = (f32[8,32,256]{2,1,0:T(8,128)S(1)}, f32[8,32,256]{2,1,0:T(8,128)}, u32[]{:S(2)}) copy-start(f32[8,32,256]{2,1,0:T(8,128)} %get-tuple-element.116) | copy-start | bytes 786436
  415.1 1.3 copy-start.2

commit v4 on v3

--- a/solution.py
+++ b/solution.py
@@ -21,6 +21,7 @@
 HALO = 16
 IN_LANE = 32
 OUT_LANE = 48
+CAP = 80.0
 QUAD = 4
 WIDTH = QUAD * P_SIZE
 GROUPS = HEADS // QUAD
@@ -81,11 +82,11 @@
     return jnp.where((lane >= first) & (lane < first + RANK), values, 0.0)
 
 
-def out_block(w_ref, row, part):
+def out_block(w_ref, group, row, part):
     if w_ref.shape[2] == WIDTH:
-        return w_ref[0, row, :, :part]
+        return w_ref[group, row, :, :part]
     rows = WIDTH // 2
-    return jnp.concatenate([w_ref[0, row, :rows, :part], w_ref[0, row, :rows, part:]], axis=0)
+    return jnp.concatenate([w_ref[group, row, :rows, :part], w_ref[group, row, :rows, part:]], axis=0)
 
 
 def head_only(values, head):
@@ -109,16 +110,32 @@
 
 
 def at_block(k):
+    if isinstance(k, int):
+        return pl.ds(k * BLOCK, BLOCK)
     return pl.ds(pl.multiple_of(k * BLOCK, BLOCK), BLOCK)
 
 
 def at_rows(k):
+    if isinstance(k, int):
+        return pl.ds(HALO + k * BLOCK, BLOCK)
     return pl.ds(pl.multiple_of(HALO + k * BLOCK, HALO), BLOCK)
 
 
+def with_halo(k):
+    if k == 0:
+        return pl.ds(0, HALO + BLOCK)
+    return pl.ds(HALO + k * BLOCK, BLOCK)
+
+
+def padded_rows(value, first):
+    before = jnp.zeros((first, value.shape[1]), value.dtype)
+    after = jnp.zeros((LANES - first - value.shape[0], value.shape[1]), value.dtype)
+    return jnp.concatenate([before, value, after], axis=0)
+
+
 def front_kernel(
-    x_ref, gain_ref, wst_ref, sp_ref, hp_ref, w_ref, up_ref, vp_ref,
-    normed_ref, scpre_ref, raw_ref, step_ref, cum_ref, cum_t_ref, bs_ref, cs_ref, cs_t_ref, adv_ref,
+    place_ref, x_ref, gain_ref, wst_ref, sp_ref, hp_ref, w_ref, up_ref, vp_ref,
+    normed_ref, scpre_ref, ratio_ref, sig_ref, cum_ref, lead_ref, turned_ref, bs_ref, cs_ref, cs_t_ref, adv_ref,
     gate_ref, u_ref, eloc_ref, fin_ref, dec_ref,
     st_scr, bs_t_scr, val_scr,
 ):
@@ -169,51 +186,60 @@
             )
             step = jnp.maximum(raw, 0.0) + tail
             cum = split_left(lower, step * rate)
-            raw_ref[at_block(k), :] = raw
-            step_ref[at_block(k), :] = step
+            sig = sigmoid(raw)
+            ratio_ref[at_block(k), :] = jnp.where(raw < -20.0, 1.0, sig / jnp.maximum(step, 1e-30))
+            sig_ref[at_block(k), :] = sig
+            lead = jnp.log(jnp.maximum(step, 1e-37)) * LOG2E - cum
             cum_ref[at_block(k), :] = cum
+            lead_ref[at_block(k), :] = lead
             flipped = cum.T
+            flipped_lead = lead.T
             for g in range(GROUPS):
-                cum_t_ref[g, :, at_block(k)] = flipped[g * QUAD : (g + 1) * QUAD]
+                turned_ref[g, :QUAD, at_block(k)] = flipped[g * QUAD : (g + 1) * QUAD]
+                turned_ref[g, QUAD:, at_block(k)] = flipped_lead[g * QUAD : (g + 1) * QUAD]
+
+    up_rows = padded_rows(up_ref[0, 0], IN_LANE)
 
     def inner(rows):
-        total = mm(adv_ref[rows, :], up_ref[0])
+        total = mm(adv_ref[rows, :], up_rows)
         for r in range(row_count):
             total = total + mm(normed_ref[rows, r * part : (r + 1) * part], w_ref[0, r, :part, :])
         return total
 
-    val_scr[0:HALO, :] = inner(pl.ds(0, HALO))[:, WIDTH:]
     taps = vp_ref[0]
 
     def one_block(k, carry):
         state, decay = carry
-        product = inner(at_rows(k))
-        gate_ref[at_block(k), :] = product[:, :WIDTH].astype(BF16)
-        val_scr[at_rows(k), :] = product[:, WIDTH:]
-        window = val_scr[pl.ds(pl.multiple_of(8 + k * BLOCK, 8), BLOCK + 8), :]
+        product = inner(with_halo(k))
+        skip = HALO if k == 0 else 0
+        gate_ref[at_block(k), :] = product[skip:, :WIDTH].astype(BF16)
+        val_scr[with_halo(k), :] = product[:, WIDTH:]
+        window = val_scr[pl.ds(8 + k * BLOCK, BLOCK + 8), :]
         pre = delays(window, taps[0:4], taps[4:5])
         u_ref[at_block(k), :] = pre.astype(BF16)
         xs = (pre * sigmoid(pre)).astype(BF16).astype(F32)
         cum = cum_ref[at_block(k), :]
         last = cum[BLOCK - 1 : BLOCK]
-        weight = to_front(step_ref[at_block(k), :] * jnp.exp2(last - cum), group)
+        weight = to_front(jnp.exp2(last + lead_ref[at_block(k), :]), group)
         weighted = (xs * widen(weight)).astype(BF16)
-        eloc_ref[k] = state
+        eloc_ref[k] = state.astype(BF16)
         last8 = to_front(jnp.broadcast_to(last, (8, LANES)), group)
         fall = widen(jnp.exp2(last8))[0:1]
         return fall * state + mm(bs_t_scr[k], weighted), decay * fall
 
-    start = (jnp.zeros((STATES, WIDTH), F32), jnp.ones((1, WIDTH), F32))
-    state, decay = lax.fori_loop(0, blocks, one_block, start)
+    carry = (jnp.zeros((STATES, WIDTH), F32), jnp.ones((1, WIDTH), F32))
+    for k in range(blocks):
+        carry = one_block(k, carry)
+    state, decay = carry
     fin_ref[...] = state.astype(BF16)
     dec_ref[...] = jnp.broadcast_to(decay, (8, WIDTH))
 
 
 def scan_kernel(
-    x_ref, g_ref, wst_ref, w_ref, down_ref, vp_ref, gate_ref, u_ref, eloc_ref, ein_ref,
-    step_ref, cum_ref, cum_t_ref, bs_ref, cs_ref,
+    place_ref, x_ref, g_ref, wst_ref, w_ref, down_ref, vp_ref, gate_ref, u_ref, eloc_ref, ein_ref,
+    cum_ref, turned_ref, bs_ref, cs_ref,
     out_ref, o_ref, ent_ref, aux_ref, sg_ref, gup_ref,
-    score_scr, acc_scr, side_scr, square_scr,
+    score_scr, gained_scr, side_scr, square_scr,
 ):
     group = pl.program_id(0)
     row_count, _, part = x_ref.shape
@@ -221,7 +247,6 @@
 
     @pl.when(group == 0)
     def _():
-        acc_scr[...] = jnp.zeros_like(acc_scr)
         side_scr[...] = jnp.zeros_like(side_scr)
         square_scr[...] = jnp.zeros_like(square_scr)
         keep = iota((BLOCK, BLOCK), 0) >= iota((BLOCK, BLOCK), 1)
@@ -232,22 +257,23 @@
             score_scr[k] = jnp.where(keep, score, 0.0)
 
     taps = vp_ref[0]
+
+    down_rows = padded_rows(down_ref[0, 0], OUT_LANE)
 
     def one_block(k, before):
         rows = at_block(k)
         pre = u_ref[rows, :].astype(F32)
         conv = pre * sigmoid(pre)
         cum = to_front(cum_ref[rows, :], group)
-        step = to_front(step_ref[rows, :], group)
-        scaled = (conv.astype(BF16).astype(F32) * widen(step)).astype(BF16)
+        xs = conv.astype(BF16)
         score = score_scr[k]
-        entering = (eloc_ref[k] + before * ein_ref[...]).astype(BF16)
+        entering = (eloc_ref[k].astype(F32) + before * ein_ref[...]).astype(BF16)
         ent_ref[k] = entering
         total = widen(jnp.exp2(cum)) * mm(cs_ref[rows, :], entering)
         for h in range(QUAD):
-            spread = cum[:, h : h + 1] - cum_t_ref[0, h : h + 1, rows]
-            weights = (score * jnp.exp2(jnp.minimum(spread, 0.0))).astype(BF16)
-            total = total + mm(weights, head_only(scaled, h))
+            spread = cum[:, h : h + 1] + turned_ref[0, QUAD + h : QUAD + h + 1, rows]
+            weights = (score * jnp.exp2(jnp.minimum(spread, CAP))).astype(BF16)
+            total = total + mm(weights, head_only(xs, h))
         output = total + taps[6:7] * conv
         o_ref[rows, :] = output.astype(BF16)
         gate = gate_ref[rows, :].astype(F32)
@@ -255,13 +281,13 @@
         square = gated * gated
         square_scr[rows, :] += square[:, :LANES] + square[:, LANES:]
         gained = (gated * taps[5:6]).astype(BF16)
-        for r in range(row_count):
-            cols = slice(r * part, (r + 1) * part)
-            acc_scr[rows, cols] += mm(gained, out_block(w_ref, r, part))
-        side_scr[rows, :] += mm_nt(gained, down_ref[0])
+        gained_scr[group, rows, :] = gained
+        side_scr[rows, :] += mm_nt(gained, down_rows)
         return before * widen(jnp.exp2(cum[BLOCK - 8 :]))[7:8]
 
-    lax.fori_loop(0, blocks, one_block, jnp.ones((1, WIDTH), F32))
+    before = jnp.ones((1, WIDTH), F32)
+    for k in range(blocks):
+        before = one_block(k, before)
 
     @pl.when(group == pl.num_programs(0) - 1)
     def _():
@@ -282,7 +308,9 @@
             product = jnp.sum(side_grad.astype(F32) * side_raw, axis=1, keepdims=True)
             for r in range(row_count):
                 cols = slice(r * part, (r + 1) * part)
-                raw = acc_scr[rows, cols]
+                raw = mm(gained_scr[0, rows, :], out_block(w_ref, 0, r, part))
+                for c in range(1, GROUPS):
+                    raw = raw + mm(gained_scr[c, rows, :], out_block(w_ref, c, r, part))
                 cot = g_ref[r, rows, :]
                 product = product + jnp.sum(raw * cot.astype(F32), axis=1, keepdims=True)
                 total = x_ref[r, at_rows(k), :].astype(F32) + raw * rms + mm_nt(side, wst_ref[r, :, 256:384])
@@ -295,7 +323,7 @@
 
 
 def gate_kernel(
-    g_ref, w_ref, sg_ref, down_ref, vp_ref, gate_ref, o_ref, aux_ref, cum_ref, cs_t_ref,
+    place_ref, g_ref, w_ref, sg_ref, down_ref, vp_ref, gate_ref, o_ref, aux_ref, cum_ref, cs_t_ref,
     dgate_ref, dy_ref, gloc_ref, gfin_ref, gdown_ref,
     sg_t_scr,
 ):
@@ -312,12 +340,14 @@
     taps = vp_ref[0]
     gdown_ref[0] = jnp.zeros((RANK, WIDTH), F32)
 
+    down_rows = padded_rows(down_ref[0, 0], OUT_LANE)
+
     def one_block(i, state):
         k = blocks - 1 - i
         rows = at_block(k)
-        dmix = mm(sg_ref[rows, :], down_ref[0])
+        dmix = mm(sg_ref[rows, :], down_rows)
         for r in range(row_count):
-            dmix = dmix + mm_nt(g_ref[r, rows, :], out_block(w_ref, r, part))
+            dmix = dmix + mm_nt(g_ref[r, rows, :], out_block(w_ref, 0, r, part))
         gate = gate_ref[rows, :].astype(F32)
         output = o_ref[rows, :].astype(F32)
         sig = sigmoid(gate)
@@ -335,17 +365,19 @@
         dy_ref[rows, :] = dy.astype(BF16)
         cum = to_front(cum_ref[rows, :], group)
         factor = widen(jnp.exp2(cum))
-        gloc_ref[k] = state
+        gloc_ref[k] = state.astype(BF16)
         return factor[BLOCK - 1 : BLOCK] * state + mm(cs_t_ref[k], (factor * dy).astype(BF16))
 
-    state = lax.fori_loop(0, blocks, one_block, jnp.zeros((STATES, WIDTH), F32))
+    state = jnp.zeros((STATES, WIDTH), F32)
+    for i in range(blocks):
+        state = one_block(i, state)
     gfin_ref[...] = state.astype(BF16)
 
 
 def back_kernel(
-    x_ref, gain_ref, normed_ref, wst_ref, w_ref, up_ref, adv_ref, vp_ref, sp_ref, hp_ref,
+    place_ref, x_ref, gain_ref, normed_ref, wst_ref, w_ref, up_ref, adv_ref, vp_ref, sp_ref, hp_ref,
     u_ref, o_ref, dy_ref, dgate_ref, ent_ref, gloc_ref, gin_ref,
-    step_ref, cum_ref, cum_t_ref, raw_ref, scpre_ref, bs_ref, cs_ref, out_down_ref, out_up_ref,
+    cum_ref, lead_ref, turned_ref, ratio_ref, sig_ref, scpre_ref, bs_ref, cs_ref, out_down_ref, out_up_ref,
     corr_ref, wide_ref, thin_ref,
     score_scr, dscore_scr, db_scr, dc_scr, dcum_scr, dstep_scr, dlast_scr, du_scr, ig_scr, ng_scr, adg_scr, adv_t_scr, up_scr, in_scr,
 ):
@@ -376,68 +408,66 @@
         pre = u_ref[rows, :].astype(F32)
         sig = sigmoid(pre)
         conv = pre * sig
-        xs = conv.astype(BF16).astype(F32)
+        xs_low = conv.astype(BF16)
+        xs = xs_low.astype(F32)
         cum = to_front(cum_ref[rows, :], group)
-        step_w = widen(to_front(step_ref[rows, :], group))
-        scaled_low = (xs * step_w).astype(BF16)
-        scaled = scaled_low.astype(F32)
+        lead = to_front(lead_ref[rows, :], group)
         dy_low = dy_ref[rows, :]
         dy = dy_low.astype(F32)
         b_rows = bs_ref[rows, :]
         c_rows = cs_ref[rows, :]
         score = jnp.where(keep, score_scr[k], 0.0)
         dscore = dscore_scr[k]
-        ending = gloc_ref[k] + after * gin_ref[...]
+        ending = gloc_ref[k].astype(F32) + after * gin_ref[...]
         ending_low = ending.astype(BF16)
         last = cum[BLOCK - 1 : BLOCK]
-        to_end = widen(jnp.exp2(last - cum))
-        dscaled_state = to_end * mm(b_rows, ending_low)
-        dscaled = dscaled_state
+        to_end = widen(jnp.exp2(last + lead))
+        dxs_state = to_end * mm(b_rows, ending_low)
+        dxs = dxs_state
         for h in range(QUAD):
-            spread = cum_t_ref[0, h : h + 1, rows] - cum[:, h : h + 1]
-            damp = jnp.exp2(jnp.minimum(spread, 0.0))
+            spread = turned_ref[0, h : h + 1, rows] + lead[:, h : h + 1]
+            damp = jnp.exp2(jnp.minimum(spread, CAP))
             weights = (score * damp).astype(BF16)
             dy_head = head_only(dy_low, h)
-            dscaled = dscaled + mm(weights, dy_head)
-            dscore = dscore + mm_nt(scaled_low, dy_head) * damp
+            dxs = dxs + mm(weights, dy_head)
+            dscore = dscore + mm_nt(xs_low, dy_head) * damp
         dscore_scr[k] = dscore
         from_start = widen(jnp.exp2(cum))
         fall = from_start[BLOCK - 1 : BLOCK]
         entering_low = ent_ref[k]
         entering = entering_low.astype(F32)
         dc_scr[rows, :] += mm_nt((from_start * dy).astype(BF16), entering_low)
-        db_scr[rows, :] += mm_nt((to_end * scaled).astype(BF16), ending_low)
+        db_scr[rows, :] += mm_nt((to_end * xs).astype(BF16), ending_low)
         scan_out = o_ref[rows, :].astype(F32) - taps[6:7] * conv
-        dcum_scr[rows, :] += split_right(dy * scan_out - scaled * dscaled, pick)
-        dstep_scr[rows, :] += split_right(xs * dscaled, pick)
-        ends = jnp.sum(scaled * dscaled_state, axis=0, keepdims=True)
+        inward = mm((xs * dxs).astype(BF16), pick)
+        dcum_scr[rows, :] += mm((dy * scan_out).astype(BF16), pick) - inward
+        dstep_scr[rows, :] += inward
+        ends = jnp.sum(xs * dxs_state, axis=0, keepdims=True)
         ends = ends + fall * jnp.sum(entering * ending, axis=0, keepdims=True)
         dlast_scr[k] += split_right(jnp.broadcast_to(ends, (8, WIDTH)), pick)
-        dconv = taps[6:7] * dy + step_w * dscaled
+        dconv = taps[6:7] * dy + dxs
         du_scr[at_rows(k), :] = dconv * (sig + conv * (1.0 - sig))
         return after * fall
 
-    lax.fori_loop(0, blocks, one_block, jnp.ones((1, WIDTH), F32))
-
-    def spread_back(rows, window, count):
-        dval = advances(window, taps[0:4], count)
-        ig_scr[rows, WIDTH:] = dval.astype(BF16)
+    after = jnp.ones((1, WIDTH), F32)
+    for i in range(blocks):
+        after = one_block(i, after)
+    up_rows = padded_rows(up_ref[0, 0], IN_LANE)
+
+    ig_scr[0:HALO, :WIDTH] = jnp.zeros((HALO, WIDTH), BF16)
+    for k in range(blocks):
+        rows = with_halo(k)
+        extra = HALO if k == 0 else 0
+        ig_scr[at_rows(k), :WIDTH] = dgate_ref[at_block(k), :]
+        window = du_scr[pl.ds(HALO + k * BLOCK - extra, BLOCK + extra + 8), :]
+        ig_scr[rows, WIDTH:] = advances(window, taps[0:4], BLOCK + extra).astype(BF16)
         grad = ig_scr[rows, :]
-        adg_scr[rows, :] += mm_nt(grad, up_ref[0])
+        adg_scr[rows, :] += mm_nt(grad, up_rows)
         for r in range(row_count):
             ng_scr[rows, r * part : (r + 1) * part] += mm_nt(grad, w_ref[0, r, :part, :])
-        return grad
-
-    ig_scr[0:HALO, :WIDTH] = jnp.zeros((HALO, WIDTH), BF16)
-    first = spread_back(pl.ds(0, HALO), du_scr[0 : HALO + 8, :], HALO)
-    up_scr[...] = mm_tn(adv_ref[0:HALO, :], first)[IN_LANE : IN_LANE + RANK]
-
-    @pl.loop(0, blocks)
-    def _(k):
-        ig_scr[at_rows(k), :WIDTH] = dgate_ref[at_block(k), :]
-        window = du_scr[pl.ds(pl.multiple_of(HALO + k * BLOCK, 8), BLOCK + 8), :]
-        grad = spread_back(at_rows(k), window, BLOCK)
-        up_scr[...] += mm(adv_t_scr[k], grad)
+        if k == 0:
+            up_scr[...] = mm_tn(adv_ref[0:HALO, :], grad[:HALO])[IN_LANE : IN_LANE + RANK]
+        up_scr[...] += mm(adv_t_scr[k], grad[extra:])
 
     share = RANK // row_count
     for r in range(row_count):
@@ -461,13 +491,13 @@
             du_scr[at_rows(k), :] = jnp.concatenate([db, dc], axis=1) * slope
             is_last = iota((BLOCK, LANES), 0) == BLOCK - 1
             dcum = dcum_scr[rows, :] + jnp.where(is_last, dlast_scr[k, 0:1, :], 0.0)
-            dstep = dstep_scr[rows, :] + split_left(upper, dcum) * rate
-            dstep_scr[rows, :] = dstep * sigmoid(raw_ref[rows, :])
+            slower = split_left(upper, dcum) * (rate * sig_ref[rows, :])
+            dstep_scr[rows, :] = dstep_scr[rows, :] * ratio_ref[rows, :] + slower
 
         def finish(rows, window, count, draw):
             dstate = advances(window, sp_ref[0:4], count).astype(BF16)
             adapt = adg_scr[rows, :].astype(BF16)
-            mixed = adapt if draw is None else adapt + draw
+            mixed = adapt + draw
             total = jnp.zeros((count, 1), F32)
             square = jnp.zeros((count, 1), F32)
             grads = []
@@ -488,12 +518,13 @@
                 corr_ref[r, rows, :] = (inv * grads[r] - factor * piece).astype(BF16)
 
         in_scr[...] = jnp.zeros_like(in_scr)
-        finish(pl.ds(0, HALO), du_scr[0 : HALO + 8, :], HALO, None)
-
-        @pl.loop(0, blocks)
-        def _(k):
-            window = du_scr[pl.ds(pl.multiple_of(HALO + k * BLOCK, 8), BLOCK + 8), :]
-            finish(at_rows(k), window, BLOCK, dstep_scr[at_block(k), :].astype(BF16))
+        for k in range(blocks):
+            extra = HALO if k == 0 else 0
+            window = du_scr[pl.ds(HALO + k * BLOCK - extra, BLOCK + extra + 8), :]
+            draw = dstep_scr[at_block(k), :].astype(BF16)
+            if k == 0:
+                draw = jnp.concatenate([jnp.zeros((HALO, LANES), BF16), draw], axis=0)
+            finish(with_halo(k), window, BLOCK + extra, draw)
 
         for r in range(row_count):
             thin_ref[r, 0:RANK, :] = in_scr[:, r * part : (r + 1) * part]
@@ -576,10 +607,10 @@
 
 
 def start_kernel(
-    x_ref, w_ref, up_ref, p_ref, down_ref, shared_ref, gain_ref, conv_ref, bias_ref, gate_ref, step_ref, rate_ref,
-    skip_ref,
+    x_ref, w_ref, up_ref, p_ref, down_ref, state_ref, in_ref, out_ref, gain_ref, conv_ref, bias_ref, gate_ref, step_ref, rate_ref,
+    skip_ref, adapter_ref,
     x_out, w_out, shared_out, gain_out, vec_out, head_out,
-    block_scr, zero_scr,
+    block_scr, zero_scr, shared_ref,
     own_sem, send_sem, recv_sem, row_send, row_recv, col_send, col_recv,
 ):
     col_count, row_count = w_out.shape[:2]
@@ -620,6 +651,18 @@
     block_scr[first : first + rank_part // 2, :WIDTH] = downs[: rank_part // 2]
     block_scr[first : first + rank_part // 2, WIDTH:] = downs[rank_part // 2 :]
     zero_scr[...] = jnp.zeros_like(zero_scr)
+    shift = adapter_ref[col] * RANK
+    source = iota((LANES, LANES), 0) - shift
+    target = iota((LANES, LANES), 1)
+    chosen = (source >= 0) & (source < RANK)
+    ins = (chosen & (source == target - IN_LANE)).astype(F32).astype(BF16)
+    outs = (chosen & (source == target - OUT_LANE)).astype(F32).astype(BF16)
+    states = 2 * STATES
+    shared_ref[:, :states] = state_ref[:states, :].astype(F32).T.astype(BF16)
+    steps = jnp.concatenate(
+        [state_ref[states:, :].astype(F32), jnp.zeros((LANES - HEADS, part), F32)], axis=0
+    ).T
+    shared_ref[:, states:] = (steps + mm(in_ref[...], ins) + mm(out_ref[...], outs)).astype(BF16)
     vec_out[col, 0:4, :] = conv_ref[...]
     vec_out[col, 4:5, :] = bias_ref[...]
     vec_out[col, 5:6, :] = gate_ref[...]
@@ -690,7 +733,7 @@
     for copy in small:
         copy.start()
 
-    cut = (w_out.shape[2] * 60 // 100 + 8) // 16 * 16
+    cut = (w_out.shape[2] * 65 // 100 + 8) // 16 * 16
     spans = (pl.ds(0, cut), pl.ds(cut, w_out.shape[2] - cut))
     has_up = high < high_count - 1
     has_down = high > 0
@@ -758,31 +801,37 @@
             event(starting, 0, far(side, step, distance), across, ("core",), valid=within(step, distance))
 
     def relay(starting):
+        def windows():
+            if starting:
+                each_window(True, lambda copy: copy.start())
+
+        event(starting, 0, col, row, ("up", "down"), arrives=False)
         event(starting, 1, col, row, ("x", "y"), arrives=False)
-        event(starting, 0, col, row, ("up", "down", "y", "x"), arrives=False)
-        event(starting, 1, col, row, ("up", "down", "core"), arrives=False)
-        event(starting, 0, col, row, ("core",), arrives=False)
-        event(starting, 1, side, row, ("y", "up", "down", "core"))
+        event(starting, 0, col, row, ("y", "x", "core"), arrives=False)
+        event(starting, 1, col, row, ("core",), arrives=False)
+        event(starting, 1, side, row, ("y", "core"))
+        along(starting, 0, 1)
+        event(starting, 1, col, row, ("up", "down"), arrives=False)
+        event(starting, 0, col, across, ("x", "core"))
+        event(starting, 1, side, row, ("up", "down"), arrives=False)
         event(starting, 1, col, across, ("up", "down", "core"))
-        along(starting, 0, 1)
+        for d in range(2, high_count - 1):
+            along(starting, 0, d)
         event(starting, 1, side, across, ("up", "down", "core"))
-        if starting:
-            each_window(True, lambda copy: copy.start())
-        event(starting, 0, col, across, ("x", "core"))
+        over(starting, 1)
+        along(starting, 0, high_count - 1)
+        windows()
+        along(starting, 1, 1)
+        over(starting, 2)
+        event(starting, 0, side, row, ("core",))
+        event(starting, 0, side, across, ("core",))
+        last(starting, 1)
         for d in range(2, high_count):
-            along(starting, 0, d)
-            along(starting, 1, d - 1)
-            if d == 2:
-                event(starting, 0, side, row, ("core",))
-                over(starting, 1)
-                event(starting, 0, side, across, ("core",))
-            else:
-                over(starting, d - 1)
-                last(starting, d - 2)
-        along(starting, 1, high_count - 1)
-        over(starting, high_count - 1)
-        if high_count > 2:
-            last(starting, high_count - 2)
+            if d > 2:
+                over(starting, d)
+            along(starting, 1, d)
+            if d > 2:
+                last(starting, d - 1)
         last(starting, high_count - 1)
 
     own_block.wait()
@@ -821,7 +870,7 @@
     relay(False)
 
 
-def start_exchange(x, w, up, p, down, shared, vectors, row_count, col_count):
+def start_exchange(x, w, up, p, down, shared, vectors, adapter_id, row_count, col_count):
     part = x.shape[1]
     rank_part = up.shape[0] // row_count
     block_rows = part + rank_part + WIDTH // 2 + rank_part // 2
@@ -831,25 +880,25 @@
     dma = pltpu.SemaphoreType.DMA
     return pl.pallas_call(
         start_kernel,
-        in_specs=[anywhere] + [vmem] * (5 + len(vectors)),
+        in_specs=[anywhere] + [vmem] * (7 + len(vectors)) + [pl.BlockSpec(memory_space=pltpu.SMEM)],
         out_specs=[anywhere] * 3 + [vmem] * 3,
         out_shape=[
             jax.ShapeDtypeStruct((row_count, chunk + HALO, part), BF16),
             jax.ShapeDtypeStruct((col_count, row_count, block_rows, 2 * WIDTH), BF16),
-            jax.ShapeDtypeStruct((row_count,) + shared.shape, BF16),
+            jax.ShapeDtypeStruct((row_count, part, 384), BF16),
             jax.ShapeDtypeStruct((row_count, 1, part), F32),
             jax.ShapeDtypeStruct((col_count, 8, WIDTH), F32),
             jax.ShapeDtypeStruct((8, LANES), F32),
         ],
         scratch_shapes=[
             pltpu.VMEM((block_rows, 2 * WIDTH), BF16), pltpu.VMEM((HALO, part), BF16),
-            dma((3 + row_count,)), dma((2, col_count, row_count, 5)), dma((2, col_count, row_count)),
+            pltpu.VMEM((part, 384), BF16), dma((3 + row_count,)), dma((2, col_count, row_count, 5)), dma((2, col_count, row_count)),
             dma((3 * row_count,)), dma((3 * row_count,)), dma((col_count,)), dma((col_count,)),
         ],
         compiler_params=pltpu.CompilerParams(
             collective_id=1, has_side_effects=True, vmem_limit_bytes=VMEM_BYTES
         ),
-    )(x, w, up, p, down, shared, *vectors)
+    )(x, w, up, p, down, *shared, *vectors, adapter_id)
 
 
 def finish_exchange(corr, wide, thin):
@@ -881,49 +930,71 @@
 
 
 def whole_spec(shape):
-    return pl.BlockSpec(shape, lambda c: (0,) * len(shape))
+    return pl.BlockSpec(shape, lambda c, s: (0,) * len(shape))
 
 
 def lead_spec(shape):
-    return pl.BlockSpec((1,) + tuple(shape[1:]), lambda c: (c,) + (0,) * (len(shape) - 1))
+    return pl.BlockSpec((1,) + tuple(shape[1:]), lambda c, s: (c,) + (0,) * (len(shape) - 1))
 
 
 def lane_spec(shape):
     block = tuple(shape[:-1]) + (WIDTH,)
-    return pl.BlockSpec(block, lambda c: (0,) * (len(shape) - 1) + (c,))
+    return pl.BlockSpec(block, lambda c, s: (0,) * (len(shape) - 1) + (c,))
 
 
 def second_spec(shape):
     block = (shape[0], 1) + tuple(shape[2:])
-    return pl.BlockSpec(block, lambda c: (0, c) + (0,) * (len(shape) - 2))
+    return pl.BlockSpec(block, lambda c, s: (0, c) + (0,) * (len(shape) - 2))
 
 
 def front_spec(shape):
     if shape[2] % 3 == 0 and shape[2] // 3 * 2 >= WIDTH and shape[3] == 2 * WIDTH and shape[1] == 4:
-        return pl.BlockSpec((1, shape[1], shape[2] // 3 * 2, shape[3]), lambda c: (c, 0, 0, 0))
+        return pl.BlockSpec((1, shape[1], shape[2] // 3 * 2, shape[3]), lambda c, s: (c, 0, 0, 0))
     return lead_spec(shape)
+
+
+def full_back_spec(shape):
+    if shape[2] > WIDTH:
+        return pl.BlockSpec((shape[0], shape[1], shape[2] // 3, shape[3]), lambda c, s: (0, 0, 2, 0))
+    return whole_spec(shape)
 
 
 def back_spec(shape):
     if shape[2] > WIDTH:
-        return pl.BlockSpec((1, shape[1], shape[2] // 3, shape[3]), lambda c: (c, 0, 2, 0))
+        return pl.BlockSpec((1, shape[1], shape[2] // 3, shape[3]), lambda c, s: (c, 0, 2, 0))
     return lead_spec(shape)
 
 
-KINDS = {"w": front_spec, "p": back_spec, "s": second_spec, "a": whole_spec, "c": lead_spec, "l": lane_spec}
-
-
-def grouped_call(kernel, inputs, kinds, outputs, out_kinds, scratch, flops=0):
+def up_spec(shape):
+    first = WIDTH // RANK if shape[2] > RANK else 0
+    return pl.BlockSpec((1, 1, RANK, 2 * WIDTH), lambda c, s: (c, s[0], first + s[1], 0))
+
+
+def down_spec(shape):
+    first = shape[2] // RANK - 1
+    return pl.BlockSpec((1, 1, RANK, WIDTH), lambda c, s: (c, s[0], first, s[1]))
+
+
+KINDS = {
+    "a": whole_spec, "c": lead_spec, "l": lane_spec, "s": second_spec, "w": front_spec, "f": full_back_spec,
+    "p": back_spec, "u": up_spec, "d": down_spec,
+}
+
+
+def grouped_call(kernel, place, inputs, kinds, outputs, out_kinds, scratch, flops=0):
     return pl.pallas_call(
         kernel,
-        grid=(GROUPS,),
-        in_specs=[KINDS[kind](value.shape) for kind, value in zip(kinds, inputs)],
-        out_specs=[KINDS[kind](shape) for kind, (shape, _) in zip(out_kinds, outputs)],
+        grid_spec=pltpu.PrefetchScalarGridSpec(
+            num_scalar_prefetch=1,
+            grid=(GROUPS,),
+            in_specs=[KINDS[kind](value.shape) for kind, value in zip(kinds, inputs)],
+            out_specs=[KINDS[kind](shape) for kind, (shape, _) in zip(out_kinds, outputs)],
+            scratch_shapes=[pltpu.VMEM(shape, dtype) for shape, dtype in scratch],
+        ),
         out_shape=[jax.ShapeDtypeStruct(shape, dtype) for shape, dtype in outputs],
-        scratch_shapes=[pltpu.VMEM(shape, dtype) for shape, dtype in scratch],
         compiler_params=pltpu.CompilerParams(vmem_limit_bytes=VMEM_BYTES),
         cost_estimate=pl.CostEstimate(flops=flops, bytes_accessed=40_000_000, transcendentals=0),
-    )(*inputs)
+    )(place, *inputs)
 
 
 def to_groups(value, heads_here):
@@ -993,19 +1064,6 @@
     return before
 
 
-def rows_to_parts(value):
-    row_count = value.shape[0]
-    row = lax.axis_index("row")
-    result = value
-    for d in range(1, row_count):
-        peer = lax.rem(row + d, row_count)
-        pairs = [(i, (i + d) % row_count) for i in range(row_count)]
-        piece = lax.ppermute(lax.dynamic_index_in_dim(value, peer), "row", pairs)
-        source = lax.rem(row + row_count - d, row_count)
-        result = lax.dynamic_update_slice_in_dim(result, piece, source, 0)
-    return result
-
-
 def per_device(
     block_in, norm_gain, proj_inner, proj_state, conv_inner, conv_inner_bias, conv_state, conv_state_bias,
     step_bias, decay_log, skip_gain, gate_gain, proj_out, adapt_in_down, adapt_in_up, adapt_out_down,
@@ -1027,32 +1085,23 @@
     rank_share = rank_total // col_count
     adapter = lax.dynamic_index_in_dim(adapter_id, col // seq_cols, keepdims=False)
 
-    in_down = lax.dynamic_slice_in_dim(adapt_in_down, adapter * RANK, RANK, 1)
-    out_up = lax.dynamic_slice_in_dim(adapt_out_up, adapter * RANK, RANK, 1)
-    shared = pad_lanes(jnp.concatenate([proj_state, in_down, out_up], axis=1), 384)
     relayed = row_count == 4 and heads_here == QUAD and seq_cols == 1 and part == WIDTH
+    place = jnp.zeros((2,), jnp.int32)
     if relayed:
         x_rows, w_all, w_state, gain_all, vectors, head_rows = start_exchange(
             block_in, proj_inner.reshape(part, 2 * local), adapt_in_up.reshape(rank_total, 2 * local), proj_out,
-            adapt_out_down, shared,
+            adapt_out_down, (proj_state.T, adapt_in_down, adapt_out_up),
             (
                 norm_gain[None], conv_inner, conv_inner_bias[None], gate_gain[None], step_bias[None],
                 decay_log[None], skip_gain[None],
             ),
-            row_count, col_count,
+            adapter_id, row_count, col_count,
         )
         per_part = rank_part // RANK
-        source = adapter // per_part
-        place = lax.rem(adapter, per_part)
-        zero = jnp.int32(0)
-        up_all = lax.dynamic_slice(
-            w_all, (zero, source, part + place * RANK, zero), (GROUPS, 1, RANK, 2 * WIDTH)
-        )[:, 0]
-        down_all = lax.dynamic_slice(
-            w_all, (zero, source, jnp.int32(part + rank_part + WIDTH // 2), place * WIDTH), (GROUPS, 1, RANK, WIDTH)
-        )[:, 0]
-        p_all = w_all
-        g_rows = lax.all_to_all(cotangent.reshape(row_count, chunk, part), "row", 0, 0, tiled=True)
+        place = jnp.stack([adapter // per_part, lax.rem(adapter, per_part)])
+        up_all = down_all = p_all = w_all
+        x_rows, cot = lax.optimization_barrier((x_rows, cotangent))
+        g_rows = lax.all_to_all(cot.reshape(row_count, chunk, part), "row", 0, 0, tiled=True)
     else:
         head = jnp.zeros((HALO, part), BF16)
         if seq_cols > 1:
@@ -1074,7 +1123,7 @@
         w_all = w_all.reshape(col_count, row_count, part + rank_part, 2, local)
         w_all = to_groups(w_all, heads_here).reshape(GROUPS, row_count, part + rank_part, 2 * WIDTH)
         up_all = w_all[:, :, part:, :].reshape(GROUPS, rank_total, 2 * WIDTH)
-        up_all = lax.dynamic_slice_in_dim(up_all, adapter * RANK, RANK, 1)
+        up_all = lax.dynamic_slice_in_dim(up_all, adapter * RANK, RANK, 1)[:, None]
 
         down_part = lax.dynamic_slice_in_dim(adapt_out_down, row * rank_part, rank_part, 0)
         p_block = jnp.concatenate([proj_out, down_part.T], axis=1)
@@ -1083,8 +1132,11 @@
             p_all = jnp.moveaxis(p_all, 1, 0).reshape(row_count, GROUPS, WIDTH, part + rank_part)
             p_all = jnp.moveaxis(p_all, 0, 1)
         down_all = jnp.swapaxes(p_all[..., part:], 1, 2).reshape(GROUPS, WIDTH, rank_total)
-        down_all = jnp.swapaxes(lax.dynamic_slice_in_dim(down_all, adapter * RANK, RANK, 2), 1, 2)
-
+        down_all = jnp.swapaxes(lax.dynamic_slice_in_dim(down_all, adapter * RANK, RANK, 2), 1, 2)[:, None]
+
+        in_down = lax.dynamic_slice_in_dim(adapt_in_down, adapter * RANK, RANK, 1)
+        out_up = lax.dynamic_slice_in_dim(adapt_out_up, adapter * RANK, RANK, 1)
+        shared = pad_lanes(jnp.concatenate([proj_state, in_down, out_up], axis=1), 384)
         w_state = lax.all_gather(shared, "row")
         gain_all = lax.all_gather(norm_gain, "row").reshape(row_count, 1, part)
 
@@ -1100,64 +1152,68 @@
         vectors = jnp.concatenate(
             [to_groups(vectors[:, :6], heads_here), skip_wide, jnp.zeros_like(skip_wide)], axis=1
         )
-    up_all = jnp.pad(up_all, ((0, 0), (IN_LANE, LANES - IN_LANE - RANK), (0, 0)))
-    down_all = jnp.pad(down_all, ((0, 0), (OUT_LANE, LANES - OUT_LANE - RANK), (0, 0)))
     state_taps = jnp.concatenate([conv_state, conv_state_bias[None], jnp.zeros((3, 256), F32)], axis=0)
 
     token_f32 = ((chunk, LANES), F32)
     token_low = ((chunk, LANES), BF16)
     inner_low = ((chunk, DI), BF16)
-    states = ((blocks, STATES, DI), F32)
+    states = ((blocks, STATES, DI), BF16)
     score_box = ((blocks, BLOCK, BLOCK), F32)
-    turned = ((blocks, STATES, BLOCK), BF16)
+    flipped = ((blocks, STATES, BLOCK), BF16)
     (
-        normed, scpre, raw, step, cum, cum_t, bs, cs, cs_t, adv, gate, u, eloc, fin, dec,
+        normed, scpre, ratio, sig, cum, lead, turned, bs, cs, cs_t, adv, gate, u, eloc, fin, dec,
     ) = grouped_call(
         front_kernel,
+        place,
         (x_rows, gain_all, w_state, state_taps, head_rows, w_all, up_all, vectors),
-        "aaaaawcc",
+        "aaaaawuc",
         [
-            ((total_rows, D), BF16), ((chunk, 256), F32), token_f32, token_f32, token_f32,
-            ((GROUPS, QUAD, chunk), F32), token_low, token_low, turned, ((total_rows, LANES), BF16),
+            ((total_rows, D), BF16), ((chunk, 256), F32), token_f32, token_f32, token_f32, token_f32,
+            ((GROUPS, 2 * QUAD, chunk), F32), token_low, token_low, flipped, ((total_rows, LANES), BF16),
             inner_low, inner_low, states, ((STATES, DI), BF16), ((8, DI), F32),
         ],
-        "aaaaaaaaaalllll",
-        [((total_rows, 384), F32), turned, ((total_rows, WIDTH), F32)],
+        "aaaaaaaaaaalllll",
+        [((total_rows, 384), F32), flipped, ((total_rows, WIDTH), F32)],
         flops=int(45e9),
     )
     decay = dec[0:1]
+    fin, g_rows = lax.optimization_barrier((fin, g_rows))
     entry = carry_in(fin, decay, row_count, col_count, seq_cols, True)
     out_rows, o, ent, aux, side_grad, out_up_grad = grouped_call(
         scan_kernel,
-        (x_rows, g_rows, w_state, p_all, down_all, vectors, gate, u, eloc, entry, step, cum, cum_t, bs, cs),
-        "aaapccllllaacaa",
+        place,
+        (x_rows, g_rows, w_state, p_all, down_all, vectors, gate, u, eloc, entry, cum, turned, bs, cs),
+        "aaafdcllllacaa",
         [
             ((row_count, chunk, part), BF16), inner_low, ((blocks, STATES, DI), BF16), token_f32, token_low,
             ((RANK, D), F32),
         ],
         "allaaa",
-        [score_box, ((chunk, D), F32), token_f32, token_f32],
+        [score_box, ((GROUPS, chunk, WIDTH), BF16), token_f32, token_f32],
         flops=int(45e9),
     )
-    block_out = rows_to_parts(out_rows).reshape(col_tokens, part)
+    block_out = lax.all_to_all(out_rows, "row", 0, 0, tiled=True).reshape(col_tokens, part)
     dgate, dy, gloc, gfin, out_down_grad = grouped_call(
         gate_kernel,
+        place,
         (g_rows, p_all, side_grad, down_all, vectors, gate, o, aux, cum, cs_t),
-        "apaccllaaa",
+        "apadcllaaa",
         [inner_low, inner_low, states, ((STATES, DI), BF16), ((GROUPS, RANK, WIDTH), F32)],
         "llllc",
         [((blocks, RANK, BLOCK), BF16)],
         flops=int(25e9),
     )
+    gfin, block_out = lax.optimization_barrier((gfin, block_out))
     exit_grad = carry_in(gfin, decay, row_count, col_count, seq_cols, False)
     corr, wide, thin = grouped_call(
         back_kernel,
+        place,
         (
             x_rows, gain_all, normed, w_state, w_all, up_all, adv, vectors, state_taps, head_rows,
-            u, o, dy, dgate, ent, gloc, exit_grad, step, cum, cum_t, raw, scpre, bs, cs,
+            u, o, dy, dgate, ent, gloc, exit_grad, cum, lead, turned, ratio, sig, scpre, bs, cs,
             out_down_grad, out_up_grad,
         ),
-        "aaaawcacaalllllllaacaaaaca",
+        "aaaawuacaalllllllaacaaaaaca",
         [
             ((row_count, total_rows, part), BF16), ((row_count, GROUPS, RANK // row_count, 3 * WIDTH), F32),
             ((row_count, 2 * RANK, part), F32),
@@ -1178,15 +1234,15 @@
         wide = to_cols(wide, heads_here, col_count)
         wide = jnp.swapaxes(wide, 0, 1).reshape(row_count, col_count, share, 3 * local)
     corr, wide, thin = finish_exchange(corr, wide, thin)
-    input_grad = cotangent.astype(F32) + corr[:, HALO:].reshape(col_tokens, part).astype(F32)
-    early = corr[:, :HALO].astype(F32)
-    for r in range(1, row_count):
-        input_grad = input_grad.at[r * chunk - HALO : r * chunk].add(early[r])
+    late = jnp.zeros((1, HALO, part), BF16)
     if seq_cols > 1:
         pairs = [(i, (i - 1) % col_count) for i in range(col_count)]
-        late = lax.ppermute(corr[0, :HALO], "col", pairs).astype(F32)
+        late = lax.ppermute(corr[0:1, :HALO], "col", pairs)
         late = jnp.where(lax.rem(col, seq_cols) < seq_cols - 1, late, jnp.zeros_like(late))
-        input_grad = input_grad.at[-HALO:].add(late)
+    early = jnp.concatenate([corr[1:, :HALO], late], axis=0)
+    early = jnp.pad(early, ((0, 0), (chunk - HALO, 0), (0, 0))).astype(F32)
+    input_grad = cotangent.reshape(row_count, chunk, part).astype(F32) + corr[:, HALO:].astype(F32) + early
+    input_grad = input_grad.reshape(col_tokens, part)
     wide = jnp.swapaxes(wide, 0, 1).reshape(col_count, RANK, 3 * local)
     owner = jnp.repeat(adapter_id, seq_cols)
     adapters = rank_total // RANK
@@ -1196,10 +1252,16 @@
     in_up = wide[:, : 2 * local].reshape(rank_total, 2, heads_here, P_SIZE)
     in_up = jnp.swapaxes(in_up, 1, 2).reshape(rank_total, heads_here, 2 * P_SIZE)
     out_down = wide[:, 2 * local :]
-    thin = jnp.sum(jnp.where(chosen[:, :, None, None], thin[:, None], 0.0), axis=0)
-    thin = thin.reshape(adapters, 2, RANK, part)
-    thin = jnp.transpose(thin, (1, 3, 0, 2)).reshape(2, part, rank_total)
-    thin = lax.dynamic_slice_in_dim(thin, col * rank_share, rank_share, 2)
+    if rank_share <= RANK:
+        mine = owner == (col * rank_share) // RANK
+        thin = jnp.sum(jnp.where(mine[:, None, None], thin, 0.0), axis=0).reshape(2, RANK, part)
+        thin = lax.dynamic_slice_in_dim(thin, lax.rem(col * rank_share, RANK), rank_share, 1)
+        thin = jnp.swapaxes(thin, 1, 2)
+    else:
+        thin = jnp.sum(jnp.where(chosen[:, :, None, None], thin[:, None], 0.0), axis=0)
+        thin = thin.reshape(adapters, 2, RANK, part)
+        thin = jnp.transpose(thin, (1, 3, 0, 2)).reshape(2, part, rank_total)
+        thin = lax.dynamic_slice_in_dim(thin, col * rank_share, rank_share, 2)
     return block_out, input_grad, thin[0], in_up, out_down, thin[1]
 
 

time: 418 us -> 330 us (0.79)
  Pallas kernels: 321 us -> 261 us
  waiting for transfers between devices: 43.7 us -> 30.1 us
  local copies, waits for them, and re-layouts: 23.2 us -> 10.4 us
    pallas_call x5, Pallas kernels: 279 us -> 223 us  [the longest x4 146 us: grouped_call(): pl.pallas_call(kernel, grid_spec=pltpu.PrefetchScalarGridSpec(num_scalar_...]
    ppermute x3 -> x0, waiting for transfers between devices: 8.58 us -> none  [rows_to_parts(): piece = lax.ppermute(lax.dynamic_index_in_dim(value, peer), 'row', pairs)]
    ppermute x4, waiting for transfers between devices: 34.3 us -> 28 us  [carry_in(): other = lax.ppermute(total, 'row', pairs).astype(F32)]
    pallas_call x1, Pallas kernels: 41.9 us -> 37.5 us  [finish_exchange(): pl.pallas_call(tail_kernel, in_specs=[anywhere, vmem, vmem], out_specs=[a...]
  transfers between devices with their start and end apart: 9 -> 7, of which waited for: 5 -> 5; matrix products, arithmetic and copies ran while one was open for 6% -> 1% of each run, Pallas kernels for 29% -> 17%
where the time goes in v4:
time: 330 us; the launch traced here: 329 us
  Pallas kernels  261 us (79%)
  waiting for transfers between devices  30.1 us (9%)
  other arithmetic  13.5 us (4%)
  starting transfers between devices  10.9 us (3%)
  local copies, waits for them, and re-layouts  10.4 us (3%)
  between operations  3.42 us (1%)
    pallas_call x4, Pallas kernels, grouped_call(): pl.pallas_call(kernel, grid_spec=pltpu.PrefetchScalarGridSpec(num_scalar_...  146 us
    pallas_call x1, Pallas kernels, start_exchange(): pl.pallas_call(start_kernel, in_specs=[anywhere] + [vmem] * (7 + len(vect...  77.5 us
    pallas_call x1, Pallas kernels, finish_exchange(): pl.pallas_call(tail_kernel, in_specs=[anywhere, vmem, vmem], out_specs=[a...  37.5 us
    ppermute x4, waiting for transfers between devices, carry_in(): other = lax.ppermute(total, 'row', pairs).astype(F32)  28 us
  transfers between devices with their start and end apart: 7, of which 5 were waited for; matrix products, arithmetic and copies ran while one was open for 1% of the time, Pallas kernels for 17%

profile of v4, /device:TPU:0, one launch (start us, length us, event | category | flops | bytes accessed | tf_op | source)
XLA Modules:
  0.0 329.2 jit_solution(18283179063240376825)
XLA Ops:
  0.6 1.7 copy.45
  2.3 1.6 copy.46
  3.9 77.5 %shard_map.226 = (bf16[4,1040,256]{2,1,0:T(8,128)(2,1)}, bf16[8,4,432,512]{3,2,1,0:T(8,128)(2,1)}, bf16[4,256,384]{2,1,0:T(8,128)(2,1)}, f32[4,1,256]{2,1,0:T(1,...) custom-call(bf16[4096,256]{1,0:T(8,128)(2,1)} %x_ref.1, bf16[256,512]{1,0:T(8,128)(2,1)} %bitcast.49, ...), custom_call_target="tpu_custom_call" | custom-call | tf_op jit(solution)/shard_map/pallas_call | solution.py:881
  81.4 0.0 copy-start.4
  81.4 0.0 copy-start.2
  81.4 0.0 copy-start.3
  81.4 3.9 %all-to-all-start = ((bf16[4,1024,256]{2,1,0:T(8,128)(2,1)}), bf16[4,1024,256]{2,1,0:T(8,128)(2,1)S(1)}, u32[]{:S(2)}, u32[]{:S(2)}) async-start(bf16[4,1024,256]{2,1,0:T(8,128)(2,1)} %bitcast.11), calls=%async_computation | async-start | bytes 4194304 | tf_op jit(solution)/shard_map/all_to_all | solution.py:1104
  85.4 0.6 dynamic_slice.5
  88.6 0.7 pad_add_fusion.place_ref
  89.2 0.1 pad.8.clone
  89.3 0.0 copy-done.3
  89.3 0.7 maximum_maximum_fusion.sp_ref
  90.0 33.0 %shard_map.227 = (bf16[1040,1024]{1,0:T(8,128)(2,1)}, f32[1024,256]{1,0:T(8,128)}, f32[1024,128]{1,0:T(8,128)}, f32[1024,128]{1,0:T(8,128)}, f32[1024,128]{1,0:T...) custom-call(s32[2]{0:T(128)} %pad_add_fusion.place_ref, ...), custom_call_target="tpu_custom_call" | custom-call | flops 44999999488 | bytes 40000000 | tf_op jit(solution)/shard_map/pallas_call | solution.py:985
  123.0 0.0 all-to-all-done.g_ref
  123.0 0.0 copy-start
  123.0 0.7 collective-permute-start
  123.7 0.9 slice.21
  124.6 0.1 collective-permute-start.1
  124.6 1.1 collective-permute-done.1
  125.7 0.0 collective-permute-done
  125.7 1.3 fusion.2
  127.0 1.5 collective-permute-start.2
  128.6 12.6 %collective-permute-done.2 = bf16[128,2048]{1,0:T(8,128)(2,1)} collective-permute-done((bf16[128,2048]{1,0:T(8,128)(2,1)S(1)}, bf16[128,2048]{1,0:T(8,128)(2,1)}, u32[]{:S(2)}, u32[]{:S(2)}) %collective-permute-start.2) | collective-permute-done | bytes 524320 | tf_op jit(solution)/shard_map/ppermute | solution.py:1045
  141.2 2.2 add_select_fusion.1.ein_ref
  143.4 34.9 %shard_map.228 = (bf16[4,1024,256]{2,1,0:T(8,128)(2,1)}, bf16[1024,2048]{1,0:T(8,128)(2,1)}, bf16[4,128,2048]{2,1,0:T(8,128)(2,1)}, f32[1024,128]{1,0:T(8,128)},...) custom-call(s32[2]{0:T(128)} %pad_add_fusion.place_ref, bf16[4,1040,256]{2,1,0:T(8,128)(2,1)} %get-tuple-element.52.x_ref, ...), custom_call_target="tpu_custom_call" | custom-call | flops 44999999488 | bytes 40000000 | tf_op jit(solution)/shard_map/pallas_call | solution.py:985
  178.4 3.8 %all-to-all-start.1 = ((bf16[4,1024,256]{2,1,0:T(8,128)(2,1)}), bf16[4,1024,256]{2,1,0:T(8,128)(2,1)S(1)}, u32[]{:S(2)}, u32[]{:S(2)}) async-start(bf16[4,1024,256]{2,1,0:T(8,128)(2,1)} %get-tuple-element.75), calls=%async_computation.1 | async-start | bytes 4194304 | tf_op jit(solution)/shard_map/all_to_all | solution.py:1195
  182.2 24.4 %shard_map.229 = (bf16[1024,2048]{1,0:T(8,128)(2,1)}, bf16[1024,2048]{1,0:T(8,128)(2,1)}, bf16[4,128,2048]{2,1,0:T(8,128)(2,1)}, bf16[128,2048]{1,0:T(8,128)(2,1)}, f32[8,16,256]{2,1,0:T(8,128)}) custom-call(s32[2]{0:T(128)} %pad_add_fusion.place_ref, bf16[4,1024,256]{2,1,0:T(8,128)(2,1)} %copy-done, ...), custom_call_target="tpu_custom_call" | custom-call | flops 24999999488 | bytes 40000000 | tf_op jit(solution)/shard_map/pallas_call | solution.py:985
  206.6 1.1 all-to-all-done.1
  207.7 0.0 collective-permute-start.3
  207.7 2.1 collective-permute-done.3
  209.8 1.3 fusion.4
  211.1 0.8 collective-permute-start.4
  211.9 0.1 iota_compare_fusion
  212.0 13.2 %collective-permute-done.4 = bf16[128,2048]{1,0:T(8,128)(2,1)} collective-permute-done((bf16[128,2048]{1,0:T(8,128)(2,1)S(1)}, bf16[128,2048]{1,0:T(8,128)(2,1)}, u32[]{:S(2)}, u32[]{:S(2)}) %collective-permute-start.4) | collective-permute-done | bytes 524320 | tf_op jit(solution)/shard_map/ppermute | solution.py:1045
  225.2 2.2 add_select_fusion.gin_ref
  227.4 53.6 %shard_map.230 = (bf16[4,1040,256]{2,1,0:T(8,128)(2,1)}, f32[4,8,4,768]{3,2,1,0:T(4,128)}, f32[4,32,256]{2,1,0:T(8,128)}) custom-call(s32[2]{0:T(128)} %pad_add_fusion.place_ref, bf16[4,1040,256]{2,1,0:T(8,128)(2,1)} %get-tuple-element.52.x_ref, f32[4,1,256]{2,1,0:T(1,128)} %get-tuple-element.53.gain_ref, bf16[1040,1024]{1,0:T(8,128)(2,1)} %get-tuple-element.77.normed_ref, ...), custom_call_target="tpu_custom_call" | custom-call | flops 74999996416 | bytes 40000000 | tf_op jit(solution)/shard_map/pallas_call | solution.py:985
  281.0 37.5 %shard_map.231 = (bf16[4,1040,256]{2,1,0:T(8,128)(2,1)}, f32[4,8,4,768]{3,2,1,0:T(4,128)}, f32[8,32,256]{2,1,0:T(8,128)}) custom-call(bf16[4,1040,256]{2,1,0:T(8,128)(2,1)} %get-tuple-element.90.corr_ref, f32[4,8,4,768]{3,2,1,0:T(4,128)} %get-tuple-element.91.wide_ref, f32[4,32,256]{2,1,0:T(8,128)} %get-tuple-element.92.thin_ref), custom_call_target="tpu_custom_call" | custom-call | tf_op jit(solution)/shard_map/pallas_call | solution.py:911
  318.5 1.1 copy.36
  319.6 0.1 copy.37
  319.7 0.3 select_reduce_fusion
  320.0 0.7 slice.30
  320.7 0.7 slice.23
  321.4 0.1 copy.38
  321.6 0.8 copy.40
  322.4 0.1 select_reduce_fusion.1
  322.5 0.6 slice_bitcast_fusion
  323.1 4.7 %fusion = f32[4,1024,256]{2,1,0:T(8,128)} fusion(bf16[4,1024,256]{2,1,0:T(8,128)(2,1)} %bitcast.30, bf16[3,16,256]{2,1,0:T(8,128)(2,1)S(1)} %slice.23, bf16[4,1040,256]{2,1,0:T(8,128)(2,1)} %get-tuple-element.93), kind=kLoop, calls=%fused_computation.1 | loop fusion | flops 5242880 | bytes 8413184 | tf_op jit(solution)/shard_map/add | solution.py:1244
  327.9 1.3 copy.48
  (10 shorter events, 0.1 us)
Async XLA Ops:
  81.4 4.0 %copy-start.4 = (s32[8]{0:T(128)S(1)}, s32[8]{0:T(128)}, u32[]{:S(2)}) copy-start(s32[8]{0:T(128)} %adapter_ref.1) | copy-start | bytes 100
  81.4 7.9 %copy-start.2 = (f32[4,256]{1,0:T(4,128)S(1)}, f32[4,256]{1,0:T(4,128)}, u32[]{:S(2)}) copy-start(f32[4,256]{1,0:T(4,128)} %param.25) | copy-start | bytes 12292
  81.4 7.9 %copy-start.3 = (f32[256]{0:T(256)S(1)}, f32[256]{0:T(256)}, u32[]{:S(2)}) copy-start(f32[256]{0:T(256)} %param.26) | copy-start | bytes 3076
  81.4 41.6 %all-to-all-start = ((bf16[4,1024,256]{2,1,0:T(8,128)(2,1)}), bf16[4,1024,256]{2,1,0:T(8,128)(2,1)S(1)}, u32[]{:S(2)}, u32[]{:S(2)}) async-start(bf16[4,1024,256]{2,1,0:T(8,128)(2,1)} %bitcast.11), calls=%async_computation | async-start | bytes 4194304 | tf_op jit(solution)/shard_map/all_to_all | solution.py:1104
  123.0 20.4 %copy-start = (bf16[4,1024,256]{2,1,0:T(8,128)(2,1)}, bf16[4,1024,256]{2,1,0:T(8,128)(2,1)S(1)}, u32[]{:S(2)}) copy-start(bf16[4,1024,256]{2,1,0:T(8,128)(2,1)S(1)} %all-to-all-done.g_ref) | copy-start | bytes 6291460
  123.0 2.7 collective-permute-start
  124.6 1.2 collective-permute-start.1
  127.0 14.2 %collective-permute-start.2 = (bf16[128,2048]{1,0:T(8,128)(2,1)S(1)}, bf16[128,2048]{1,0:T(8,128)(2,1)}, u32[]{:S(2)}, u32[]{:S(2)}) collective-permute-start(bf16[128,2048]{1,0:T(8,128)(2,1)S(1)} %fusion.2), channel_id=1, source_target_pairs={{0,16},{8,24},{16,0},{24,8},{1,17},{9,25},{17,1},{25,9},{2,18},{10... | collective-permute-start | bytes 1572872 | tf_op jit(solution)/shard_map/ppermute | solution.py:1045
  178.4 29.3 %all-to-all-start.1 = ((bf16[4,1024,256]{2,1,0:T(8,128)(2,1)}), bf16[4,1024,256]{2,1,0:T(8,128)(2,1)S(1)}, u32[]{:S(2)}, u32[]{:S(2)}) async-start(bf16[4,1024,256]{2,1,0:T(8,128)(2,1)} %get-tuple-element.75), calls=%async_computation.1 | async-start | bytes 4194304 | tf_op jit(solution)/shard_map/all_to_all | solution.py:1195
  207.7 2.1 collective-permute-start.3
  211.1 14.1 %collective-permute-start.4 = (bf16[128,2048]{1,0:T(8,128)(2,1)S(1)}, bf16[128,2048]{1,0:T(8,128)(2,1)}, u32[]{:S(2)}, u32[]{:S(2)}) collective-permute-start(bf16[128,2048]{1,0:T(8,128)(2,1)S(1)} %fusion.4), channel_id=1, source_target_pairs={{0,16},{8,24},{16,0},{24,8},{1,17},{9,25},{17,1},{25,9},{2,18},{10... | collective-permute-start | bytes 1572872 | tf_op jit(solution)/shard_map/ppermute | solution.py:1045
  319.6 2.9 copy-start.1

commit v5 on v4

--- a/solution.py
+++ b/solution.py
@@ -134,7 +134,7 @@
 
 
 def front_kernel(
-    place_ref, x_ref, gain_ref, wst_ref, sp_ref, hp_ref, w_ref, up_ref, vp_ref,
+    place_ref, x_ref, gain_ref, wst_ref, sp_ref, sb_ref, hp_ref, w_ref, up_ref, vp_ref,
     normed_ref, scpre_ref, ratio_ref, sig_ref, cum_ref, lead_ref, turned_ref, bs_ref, cs_ref, cs_t_ref, adv_ref,
     gate_ref, u_ref, eloc_ref, fin_ref, dec_ref,
     st_scr, bs_t_scr, val_scr,
@@ -170,7 +170,7 @@
         @pl.loop(0, blocks)
         def _(k):
             window = st_scr[pl.ds(pl.multiple_of(8 + k * BLOCK, 8), BLOCK + 8), :256]
-            pre = delays(window, sp_ref[0:4], sp_ref[4:5])
+            pre = delays(window, sp_ref[...], sb_ref[...])
             conv = pre * sigmoid(pre)
             b_rows = conv[:, :STATES].astype(BF16)
             c_rows = conv[:, STATES:].astype(BF16)
@@ -495,7 +495,7 @@
             dstep_scr[rows, :] = dstep_scr[rows, :] * ratio_ref[rows, :] + slower
 
         def finish(rows, window, count, draw):
-            dstate = advances(window, sp_ref[0:4], count).astype(BF16)
+            dstate = advances(window, sp_ref[...], count).astype(BF16)
             adapt = adg_scr[rows, :].astype(BF16)
             mixed = adapt + draw
             total = jnp.zeros((count, 1), F32)
@@ -542,8 +542,9 @@
 def tail_kernel(
     corr_ref, wide_ref, thin_ref,
     corr_out, wide_out, thin_out,
-    wide_scr, thin_scr, wide_sum, thin_sum, wide_col,
-    own_sem, corr_send, corr_recv, row_send, row_recv, col_send, col_recv, last_send, last_recv,
+    wide_pair, thin_pair, wide_both, thin_both, wide_scr, thin_scr, wide_sum, thin_sum, wide_col,
+    own_sem, corr_send, corr_recv, pair_send, pair_recv, row_send, row_recv, col_send, col_recv, last_send, last_recv,
+    core_send, core_recv,
 ):
     row_count = corr_ref.shape[0]
     col_count = thin_out.shape[0]
@@ -564,11 +565,15 @@
         copy.start()
         return copy
 
+    chips = row_count // 2
+    parity = lax.rem(row, 2)
+    chip = row // 2
+    core = row + 1 - 2 * parity
     first = []
-    for d in range(1, row_count):
-        peer = lax.rem(row + d, row_count)
-        first.append(send(wide_ref.at[peer], wide_scr.at[row], row_send, row_recv, d, on_row(peer)))
-        first.append(send(thin_ref.at[peer], thin_scr.at[row], row_send, row_recv, row_count + d, on_row(peer)))
+    for j in range(chips):
+        theirs = 2 * j + 1 - parity
+        first.append(send(wide_ref.at[theirs], wide_pair.at[j], pair_send, pair_recv, j, on_row(core)))
+        first.append(send(thin_ref.at[theirs], thin_pair.at[j], pair_send, pair_recv, chips + j, on_row(core)))
     moved = []
     for d in range(1, row_count):
         peer = lax.rem(row + d, row_count)
@@ -577,12 +582,23 @@
     own.start()
     for copy in first:
         copy.wait()
-    wide = wide_ref[row]
-    thin = thin_ref[row]
-    for d in range(1, row_count):
-        peer = lax.rem(row + d, row_count)
-        wide = wide + wide_scr[peer]
-        thin = thin + thin_scr[peer]
+    for j in range(chips):
+        wide_both[j] = wide_ref[2 * j + parity] + wide_pair[j]
+        thin_both[j] = thin_ref[2 * j + parity] + thin_pair[j]
+    across = []
+    for d in range(1, chips):
+        there = lax.rem(chip + d, chips)
+        peer = on_row(2 * there + parity)
+        across.append(send(wide_both.at[there], wide_scr.at[chip], row_send, row_recv, d, peer))
+        across.append(send(thin_both.at[there], thin_scr.at[chip], row_send, row_recv, chips + d, peer))
+    for copy in across:
+        copy.wait()
+    wide = wide_both[chip]
+    thin = thin_both[chip]
+    for d in range(1, chips):
+        there = lax.rem(chip + d, chips)
+        wide = wide + wide_scr[there]
+        thin = thin + thin_scr[there]
     wide_sum[...] = wide
     thin_sum[...] = thin
     second = []
@@ -595,11 +611,18 @@
     for copy in second:
         copy.wait()
     third = []
-    for d in range(1, row_count):
-        peer = lax.rem(row + d, row_count)
-        third.append(send(wide_col, wide_out.at[row], last_send, last_recv, d, on_row(peer)))
+    for d in range(1, chips):
+        there = lax.rem(chip + d, chips)
+        third.append(send(wide_col, wide_out.at[row], last_send, last_recv, d, on_row(2 * there + parity)))
+    fourth = [send(wide_col, wide_out.at[row], core_send, core_recv, 0, on_row(core))]
     wide_out[row] = wide_col[...]
+    for d in range(1, chips):
+        third[d - 1].wait_recv()
+        source = 2 * lax.rem(chip + chips - d, chips) + parity
+        fourth.append(send(wide_out.at[source], wide_out.at[source], core_send, core_recv, d, on_row(core)))
     for copy in third:
+        copy.wait_send()
+    for copy in fourth:
         copy.wait()
     for copy in moved:
         copy.wait()
@@ -609,7 +632,7 @@
 def start_kernel(
     x_ref, w_ref, up_ref, p_ref, down_ref, state_ref, in_ref, out_ref, gain_ref, conv_ref, bias_ref, gate_ref, step_ref, rate_ref,
     skip_ref, adapter_ref,
-    x_out, w_out, shared_out, gain_out, vec_out, head_out,
+    x_out, w_out, shared_out, gain_out, vec_out, head_out, place_out,
     block_scr, zero_scr, shared_ref,
     own_sem, send_sem, recv_sem, row_send, row_recv, col_send, col_recv,
 ):
@@ -651,7 +674,11 @@
     block_scr[first : first + rank_part // 2, :WIDTH] = downs[: rank_part // 2]
     block_scr[first : first + rank_part // 2, WIDTH:] = downs[rank_part // 2 :]
     zero_scr[...] = jnp.zeros_like(zero_scr)
-    shift = adapter_ref[col] * RANK
+    adapter = adapter_ref[col]
+    shift = adapter * RANK
+    per_part = rank_part // RANK
+    place_out[0] = adapter // per_part
+    place_out[1] = adapter - adapter // per_part * per_part
     source = iota((LANES, LANES), 0) - shift
     target = iota((LANES, LANES), 1)
     chosen = (source >= 0) & (source < RANK)
@@ -881,7 +908,7 @@
     return pl.pallas_call(
         start_kernel,
         in_specs=[anywhere] + [vmem] * (7 + len(vectors)) + [pl.BlockSpec(memory_space=pltpu.SMEM)],
-        out_specs=[anywhere] * 3 + [vmem] * 3,
+        out_specs=[anywhere] * 3 + [vmem] * 3 + [pl.BlockSpec(memory_space=pltpu.SMEM)],
         out_shape=[
             jax.ShapeDtypeStruct((row_count, chunk + HALO, part), BF16),
             jax.ShapeDtypeStruct((col_count, row_count, block_rows, 2 * WIDTH), BF16),
@@ -889,6 +916,7 @@
             jax.ShapeDtypeStruct((row_count, 1, part), F32),
             jax.ShapeDtypeStruct((col_count, 8, WIDTH), F32),
             jax.ShapeDtypeStruct((8, LANES), F32),
+            jax.ShapeDtypeStruct((2,), jnp.int32),
         ],
         scratch_shapes=[
             pltpu.VMEM((block_rows, 2 * WIDTH), BF16), pltpu.VMEM((HALO, part), BF16),
@@ -899,6 +927,100 @@
             collective_id=1, has_side_effects=True, vmem_limit_bytes=VMEM_BYTES
         ),
     )(x, w, up, p, down, *shared, *vectors, adapter_id)
+
+
+def carry_kernel(
+    forward, state_ref, decay_ref,
+    out_ref,
+    other_scr, other_decay, total_scr, total_in,
+    core_send, core_recv, across_send, across_recv, share_send, share_recv,
+):
+    row = lax.axis_index("row")
+    parity = lax.rem(row, 2)
+    chip = row // 2
+    core = row + 1 - 2 * parity
+    across = lax.rem(row + 2, 4)
+    barrier = pltpu.get_barrier_semaphore()
+    for peer in (core, across):
+        pl.semaphore_signal(barrier, inc=1, device_id=on_row(peer), device_id_type=MESH)
+    pl.semaphore_wait(barrier, 2)
+
+    def remote(source, target, sends, recvs, index, peer):
+        return pltpu.make_async_remote_copy(
+            src_ref=source, dst_ref=target, send_sem=sends.at[index], recv_sem=recvs.at[index],
+            device_id=on_row(peer), device_id_type=MESH,
+        )
+
+    swaps = [
+        remote(state_ref, other_scr, core_send, core_recv, 0, core),
+        remote(decay_ref, other_decay, core_send, core_recv, 1, core),
+    ]
+    for copy in swaps:
+        copy.start()
+    for copy in swaps:
+        copy.wait()
+    half = state_ref.shape[1] // 2
+    rows = state_ref.shape[0] // 2
+    second = parity == (1 if forward else 0)
+    sends = chip == (0 if forward else 1)
+
+    @pl.when(sends)
+    def _():
+        for p in range(2):
+
+            @pl.when(parity == p)
+            def _():
+                cols = slice(p * half, (p + 1) * half)
+                for q in range(2):
+                    part = slice(q * rows, (q + 1) * rows)
+                    mine = state_ref[part, cols].astype(F32)
+                    other = other_scr[part, cols].astype(F32)
+                    late = mine + other * decay_ref[0:1, cols]
+                    early = other + mine * other_decay[0:1, cols]
+                    total_scr[q] = jnp.where(second, late, early).astype(BF16)
+                    remote(total_scr.at[q], total_in.at[p, q], across_send, across_recv, q, across).start()
+        out_ref[...] = jnp.where(second, other_scr[...].astype(F32), 0.0)
+        for q in range(2):
+            remote(total_scr.at[q], total_in.at[parity, q], across_send, across_recv, q, across).wait_send()
+
+    @pl.when(jnp.logical_not(sends))
+    def _():
+        for q in range(2):
+            remote(total_scr.at[q], total_in.at[parity, q], across_send, across_recv, q, across).wait_recv()
+            remote(
+                total_in.at[parity, q], total_in.at[parity, q], share_send, share_recv, q, core
+            ).start()
+        for q in range(2):
+            remote(
+                total_in.at[parity, q], total_in.at[1 - parity, q], share_send, share_recv, q, core
+            ).wait()
+        for p in range(2):
+            for q in range(2):
+                cols = slice(p * half, (p + 1) * half)
+                part = slice(q * rows, (q + 1) * rows)
+                total = total_in[p, q].astype(F32)
+                later = other_scr[part, cols].astype(F32) + total * other_decay[0:1, cols]
+                out_ref[part, cols] = jnp.where(second, later, total)
+
+
+def carry_over(state, decay, forward):
+    vmem = pl.BlockSpec(memory_space=pltpu.VMEM)
+    dma = pltpu.SemaphoreType.DMA
+    rows, cols = state.shape
+    return pl.pallas_call(
+        functools.partial(carry_kernel, forward),
+        in_specs=[vmem, vmem],
+        out_specs=vmem,
+        out_shape=jax.ShapeDtypeStruct(state.shape, F32),
+        scratch_shapes=[
+            pltpu.VMEM(state.shape, BF16), pltpu.VMEM(decay.shape, F32),
+            pltpu.VMEM((2, rows // 2, cols // 2), BF16), pltpu.VMEM((2, 2, rows // 2, cols // 2), BF16),
+            dma((2,)), dma((2,)), dma((2,)), dma((2,)), dma((2,)), dma((2,)),
+        ],
+        compiler_params=pltpu.CompilerParams(
+            collective_id=2 if forward else 3, has_side_effects=True, vmem_limit_bytes=VMEM_BYTES
+        ),
+    )(state, decay)
 
 
 def finish_exchange(corr, wide, thin):
@@ -918,10 +1040,11 @@
             jax.ShapeDtypeStruct((col_count,) + thin.shape[1:], F32),
         ],
         scratch_shapes=[
-            pltpu.VMEM(wide.shape, F32), pltpu.VMEM(thin.shape, F32), pltpu.VMEM(wide.shape[1:], F32),
-            pltpu.VMEM(thin.shape[1:], F32), pltpu.VMEM(wide.shape[1:], F32),
-            dma((1,)), dma((row_count,)), dma((row_count,)), dma((2 * row_count,)), dma((2 * row_count,)),
-            dma((2 * col_count,)), dma((2 * col_count,)), dma((row_count,)), dma((row_count,)),
+            *[pltpu.VMEM((row_count // 2,) + value.shape[1:], F32) for value in (wide, thin) * 3],
+            pltpu.VMEM(wide.shape[1:], F32), pltpu.VMEM(thin.shape[1:], F32), pltpu.VMEM(wide.shape[1:], F32),
+            dma((1,)), dma((row_count,)), dma((row_count,)), dma((row_count,)), dma((row_count,)),
+            dma((row_count,)), dma((row_count,)), dma((2 * col_count,)), dma((2 * col_count,)),
+            dma((row_count // 2,)), dma((row_count // 2,)), dma((row_count // 2,)), dma((row_count // 2,)),
         ],
         compiler_params=pltpu.CompilerParams(
             collective_id=0, has_side_effects=True, vmem_limit_bytes=VMEM_BYTES
@@ -1088,7 +1211,7 @@
     relayed = row_count == 4 and heads_here == QUAD and seq_cols == 1 and part == WIDTH
     place = jnp.zeros((2,), jnp.int32)
     if relayed:
-        x_rows, w_all, w_state, gain_all, vectors, head_rows = start_exchange(
+        x_rows, w_all, w_state, gain_all, vectors, head_rows, place = start_exchange(
             block_in, proj_inner.reshape(part, 2 * local), adapt_in_up.reshape(rank_total, 2 * local), proj_out,
             adapt_out_down, (proj_state.T, adapt_in_down, adapt_out_up),
             (
@@ -1097,8 +1220,6 @@
             ),
             adapter_id, row_count, col_count,
         )
-        per_part = rank_part // RANK
-        place = jnp.stack([adapter // per_part, lax.rem(adapter, per_part)])
         up_all = down_all = p_all = w_all
         x_rows, cot = lax.optimization_barrier((x_rows, cotangent))
         g_rows = lax.all_to_all(cot.reshape(row_count, chunk, part), "row", 0, 0, tiled=True)
@@ -1152,7 +1273,7 @@
         vectors = jnp.concatenate(
             [to_groups(vectors[:, :6], heads_here), skip_wide, jnp.zeros_like(skip_wide)], axis=1
         )
-    state_taps = jnp.concatenate([conv_state, conv_state_bias[None], jnp.zeros((3, 256), F32)], axis=0)
+    state_taps = conv_state
 
     token_f32 = ((chunk, LANES), F32)
     token_low = ((chunk, LANES), BF16)
@@ -1165,8 +1286,8 @@
     ) = grouped_call(
         front_kernel,
         place,
-        (x_rows, gain_all, w_state, state_taps, head_rows, w_all, up_all, vectors),
-        "aaaaawuc",
+        (x_rows, gain_all, w_state, state_taps, conv_state_bias[None], head_rows, w_all, up_all, vectors),
+        "aaaaaawuc",
         [
             ((total_rows, D), BF16), ((chunk, 256), F32), token_f32, token_f32, token_f32, token_f32,
             ((GROUPS, 2 * QUAD, chunk), F32), token_low, token_low, flipped, ((total_rows, LANES), BF16),
@@ -1178,7 +1299,10 @@
     )
     decay = dec[0:1]
     fin, g_rows = lax.optimization_barrier((fin, g_rows))
-    entry = carry_in(fin, decay, row_count, col_count, seq_cols, True)
+    if relayed:
+        entry = carry_over(fin, dec, True)
+    else:
+        entry = carry_in(fin, decay, row_count, col_count, seq_cols, True)
     out_rows, o, ent, aux, side_grad, out_up_grad = grouped_call(
         scan_kernel,
         place,
@@ -1204,7 +1328,10 @@
         flops=int(25e9),
     )
     gfin, block_out = lax.optimization_barrier((gfin, block_out))
-    exit_grad = carry_in(gfin, decay, row_count, col_count, seq_cols, False)
+    if relayed:
+        exit_grad = carry_over(gfin, dec, False)
+    else:
+        exit_grad = carry_in(gfin, decay, row_count, col_count, seq_cols, False)
     corr, wide, thin = grouped_call(
         back_kernel,
         place,

time: 330 us -> 322 us (0.976)
  Pallas kernels: 261 us -> 295 us
  waiting for transfers between devices: 30.1 us -> 2 us
  other arithmetic: 13.5 us -> 6.22 us
    ppermute x5 -> x0, waiting for transfers between devices: 29.1 us -> none  [the longest x4 28 us: carry_in(): other = lax.ppermute(total, 'row', pairs).astype(F32)]
    pallas_call x0 -> x2, Pallas kernels: none -> 26.5 us  [carry_over(): pl.pallas_call(functools.partial(carry_kernel, forward), in_specs=[vmem,...]
    pallas_call x1, Pallas kernels: 37.5 us -> 44.9 us  [finish_exchange(): pl.pallas_call(tail_kernel, in_specs=[anywhere, vmem, vmem], out_specs=[a...]
    select_n x3 -> x0, other arithmetic: 4.45 us -> none  [the longest x2 4.44 us: carry_in(): before = jnp.where(behind, before + reach * other, before)]
  transfers between devices with their start and end apart: 7 -> 2, of which waited for: 5 -> 1; matrix products, arithmetic and copies ran while one was open for 1% -> 0% of each run, Pallas kernels for 17% -> 18%
where the time goes in v5:
time: 322 us; the launch traced here: 321 us
  Pallas kernels  295 us (92%)
  local copies, waits for them, and re-layouts  8.83 us (3%)
  starting transfers between devices  8.56 us (3%)
  other arithmetic  6.22 us (2%)
    pallas_call x4, Pallas kernels, grouped_call(): pl.pallas_call(kernel, grid_spec=pltpu.PrefetchScalarGridSpec(num_scalar_...  146 us
    pallas_call x1, Pallas kernels, start_exchange(): pl.pallas_call(start_kernel, in_specs=[anywhere] + [vmem] * (7 + len(vect...  77.5 us
    pallas_call x1, Pallas kernels, finish_exchange(): pl.pallas_call(tail_kernel, in_specs=[anywhere, vmem, vmem], out_specs=[a...  44.9 us
    pallas_call x2, Pallas kernels, carry_over(): pl.pallas_call(functools.partial(carry_kernel, forward), in_specs=[vmem,...  26.5 us
  transfers between devices with their start and end apart: 2, of which 1 were waited for; matrix products, arithmetic and copies ran while one was open for 0% of the time, Pallas kernels for 18%

profile of v5, /device:TPU:0, one launch (start us, length us, event | category | flops | bytes accessed | tf_op | source)
XLA Modules:
  0.0 321.4 jit_solution(12548459706268236214)
XLA Ops:
  0.6 1.7 copy.45
  2.3 1.6 copy.46
  3.9 77.5 %shard_map.226 = (bf16[4,1040,256]{2,1,0:T(8,128)(2,1)}, bf16[8,4,432,512]{3,2,1,0:T(8,128)(2,1)}, bf16[4,256,384]{2,1,0:T(8,128)(2,1)}, f32[4,1,256]{2,1,0:T(1,...) custom-call(bf16[4096,256]{1,0:T(8,128)(2,1)} %x_ref.1, bf16[256,512]{1,0:T(8,128)(2,1)} %bitcast.42, ...), custom_call_target="tpu_custom_call" | custom-call | tf_op jit(solution)/shard_map/pallas_call | solution.py:908
  81.4 3.6 %all-to-all-start = ((bf16[4,1024,256]{2,1,0:T(8,128)(2,1)}), bf16[4,1024,256]{2,1,0:T(8,128)(2,1)S(1)}, u32[]{:S(2)}, u32[]{:S(2)}) async-start(bf16[4,1024,256]{2,1,0:T(8,128)(2,1)} %bitcast.8), calls=%async_computation | async-start | bytes 4194304 | tf_op jit(solution)/shard_map/all_to_all | solution.py:1225
  85.0 0.0 copy-start.4
  85.0 33.1 %shard_map.227 = (bf16[1040,1024]{1,0:T(8,128)(2,1)}, f32[1024,256]{1,0:T(8,128)}, f32[1024,128]{1,0:T(8,128)}, f32[1024,128]{1,0:T(8,128)}, f32[1024,128]{1,0:T...) custom-call(s32[2]{0:T(128)} %get-tuple-element.52.place_ref, ...), custom_call_target="tpu_custom_call" | custom-call | flops 44999999488 | bytes 40000000 | tf_op jit(solution)/shard_map/pallas_call | solution.py:1108
  118.2 0.0 copy-done.4
  118.2 0.5 broadcast_compare_fusion
  118.7 0.6 iota_compare_fusion
  119.3 0.0 all-to-all-done.g_ref
  119.3 0.0 copy-start
  119.3 12.6 %shard_map.228.ein_ref = f32[128,2048]{1,0:T(8,128)} custom-call(bf16[128,2048]{1,0:T(8,128)(2,1)} %get-tuple-element.66.state_ref, f32[8,2048]{1,0:T(8,128)} %get-tuple-element.67.decay_ref), custom_call_target="tpu_custom_call" | custom-call | tf_op jit(solution)/shard_map/pallas_call | solution.py:1010
  132.0 0.0 copy-done
  132.0 35.0 %shard_map.229 = (bf16[4,1024,256]{2,1,0:T(8,128)(2,1)}, bf16[1024,2048]{1,0:T(8,128)(2,1)}, bf16[4,128,2048]{2,1,0:T(8,128)(2,1)}, f32[1024,128]{1,0:T(8,128)},...) custom-call(s32[2]{0:T(128)} %get-tuple-element.52.place_ref, bf16[4,1040,256]{2,1,0:T(8,128)(2,1)} %get-tuple-element.54.x_ref, ...), custom_call_target="tpu_custom_call" | custom-call | flops 44999999488 | bytes 40000000 | tf_op jit(solution)/shard_map/pallas_call | solution.py:1108
  167.0 4.9 %all-to-all-start.1 = ((bf16[4,1024,256]{2,1,0:T(8,128)(2,1)}), bf16[4,1024,256]{2,1,0:T(8,128)(2,1)S(1)}, u32[]{:S(2)}, u32[]{:S(2)}) async-start(bf16[4,1024,256]{2,1,0:T(8,128)(2,1)} %get-tuple-element.77), calls=%async_computation.1 | async-start | bytes 4194304 | tf_op jit(solution)/shard_map/all_to_all | solution.py:1319
  171.9 24.4 %shard_map.230 = (bf16[1024,2048]{1,0:T(8,128)(2,1)}, bf16[1024,2048]{1,0:T(8,128)(2,1)}, bf16[4,128,2048]{2,1,0:T(8,128)(2,1)}, bf16[128,2048]{1,0:T(8,128)(2,1)}, f32[8,16,256]{2,1,0:T(8,128)}) custom-call(s32[2]{0:T(128)} %get-tuple-element.52.place_ref, bf16[4,1024,256]{2,1,0:T(8,128)(2,1)} %copy-done, ...), custom_call_target="tpu_custom_call" | custom-call | flops 24999999488 | bytes 40000000 | tf_op jit(solution)/shard_map/pallas_call | solution.py:1108
  196.3 2.0 all-to-all-done.1
  198.3 13.9 %shard_map.231.gin_ref = f32[128,2048]{1,0:T(8,128)} custom-call(bf16[128,2048]{1,0:T(8,128)(2,1)} %get-tuple-element.85.state_ref, f32[8,2048]{1,0:T(8,128)} %get-tuple-element.67.decay_ref), custom_call_target="tpu_custom_call" | custom-call | tf_op jit(solution)/shard_map/pallas_call | solution.py:1010
  212.2 53.5 %shard_map.232 = (bf16[4,1040,256]{2,1,0:T(8,128)(2,1)}, f32[4,8,4,768]{3,2,1,0:T(4,128)}, f32[4,32,256]{2,1,0:T(8,128)}) custom-call(s32[2]{0:T(128)} %get-tuple-element.52.place_ref, bf16[4,1040,256]{2,1,0:T(8,128)(2,1)} %get-tuple-element.54.x_ref, f32[4,1,256]{2,1,0:T(1,128)} %get-tuple-element.55.gain_ref, ...), custom_call_target="tpu_custom_call" | custom-call | flops 74999996416 | bytes 40000000 | tf_op jit(solution)/shard_map/pallas_call | solution.py:1108
  265.7 0.0 copy-start.2
  265.7 44.9 %shard_map.233 = (bf16[4,1040,256]{2,1,0:T(8,128)(2,1)}, f32[4,8,4,768]{3,2,1,0:T(4,128)}, f32[8,32,256]{2,1,0:T(8,128)}) custom-call(bf16[4,1040,256]{2,1,0:T(8,128)(2,1)} %get-tuple-element.92.corr_ref, f32[4,8,4,768]{3,2,1,0:T(4,128)} %get-tuple-element.93.wide_ref, f32[4,32,256]{2,1,0:T(8,128)} %get-tuple-element.94.thin_ref), custom_call_target="tpu_custom_call" | custom-call | tf_op jit(solution)/shard_map/pallas_call | solution.py:1033
  310.7 1.1 copy.36
  311.7 0.0 copy-start.1
  311.8 0.0 copy-start.3
  311.8 0.1 copy.37
  311.9 0.0 copy-done.2
  311.9 0.3 select_reduce_fusion
  312.2 0.7 slice.26
  312.9 0.7 slice.19
  313.6 0.1 copy.38
  313.8 0.8 copy.40
  314.6 0.0 copy-done.1
  314.6 0.0 copy-done.3
  314.6 0.1 select_reduce_fusion.1
  314.7 0.6 slice_bitcast_fusion
  315.3 4.7 %fusion = f32[4,1024,256]{2,1,0:T(8,128)} fusion(bf16[4,1024,256]{2,1,0:T(8,128)(2,1)} %bitcast.23, bf16[3,16,256]{2,1,0:T(8,128)(2,1)S(1)} %slice.19, bf16[4,1040,256]{2,1,0:T(8,128)(2,1)} %get-tuple-element.95), kind=kLoop, calls=%fused_computation.1 | loop fusion | flops 5242880 | bytes 8413184 | tf_op jit(solution)/shard_map/add | solution.py:1371
  320.0 1.3 copy.48
  (2 shorter events, 0.0 us)
Async XLA Ops:
  81.4 38.0 %all-to-all-start = ((bf16[4,1024,256]{2,1,0:T(8,128)(2,1)}), bf16[4,1024,256]{2,1,0:T(8,128)(2,1)S(1)}, u32[]{:S(2)}, u32[]{:S(2)}) async-start(bf16[4,1024,256]{2,1,0:T(8,128)(2,1)} %bitcast.8), calls=%async_computation | async-start | bytes 4194304 | tf_op jit(solution)/shard_map/all_to_all | solution.py:1225
  85.0 33.2 %copy-start.4 = (s32[8]{0:T(128)S(1)}, s32[8]{0:T(128)}, u32[]{:S(2)}) copy-start(s32[8]{0:T(128)} %adapter_ref.1) | copy-start | bytes 100
  119.3 12.7 %copy-start = (bf16[4,1024,256]{2,1,0:T(8,128)(2,1)}, bf16[4,1024,256]{2,1,0:T(8,128)(2,1)S(1)}, u32[]{:S(2)}) copy-start(bf16[4,1024,256]{2,1,0:T(8,128)(2,1)S(1)} %all-to-all-done.g_ref) | copy-start | bytes 6291460
  167.0 31.3 %all-to-all-start.1 = ((bf16[4,1024,256]{2,1,0:T(8,128)(2,1)}), bf16[4,1024,256]{2,1,0:T(8,128)(2,1)S(1)}, u32[]{:S(2)}, u32[]{:S(2)}) async-start(bf16[4,1024,256]{2,1,0:T(8,128)(2,1)} %get-tuple-element.77), calls=%async_computation.1 | async-start | bytes 4194304 | tf_op jit(solution)/shard_map/all_to_all | solution.py:1319
  265.7 46.2 %copy-start.2 = (pred[8,8]{1,0:T(8,128)(4,1)S(1)}, pred[8,8]{1,0:T(8,128)(4,1)}, u32[]{:S(2)}) copy-start(pred[8,8]{1,0:T(8,128)(4,1)} %iota_compare_fusion) | copy-start | bytes 196
  311.7 2.9 copy-start.1
  311.8 2.9 copy-start.3

commit v6 on v5

--- a/solution.py
+++ b/solution.py
@@ -540,8 +540,8 @@
 
 
 def tail_kernel(
-    corr_ref, wide_ref, thin_ref,
-    corr_out, wide_out, thin_out,
+    corr_ref, wide_ref, thin_ref, owner_ref,
+    corr_out, wide_out, thin_out, up_out, down_out, mine_out,
     wide_pair, thin_pair, wide_both, thin_both, wide_scr, thin_scr, wide_sum, thin_sum, wide_col,
     own_sem, corr_send, corr_recv, pair_send, pair_recv, row_send, row_recv, col_send, col_recv, last_send, last_recv,
     core_send, core_recv,
@@ -575,9 +575,17 @@
         first.append(send(wide_ref.at[theirs], wide_pair.at[j], pair_send, pair_recv, j, on_row(core)))
         first.append(send(thin_ref.at[theirs], thin_pair.at[j], pair_send, pair_recv, chips + j, on_row(core)))
     moved = []
-    for d in range(1, row_count):
-        peer = lax.rem(row + d, row_count)
-        moved.append(send(corr_ref.at[peer], corr_out.at[row], corr_send, corr_recv, d, on_row(peer)))
+    cuts = (0, 8 * corr_ref.shape[1] // 1040 * 16, 45 * corr_ref.shape[1] // 1040 * 16, corr_ref.shape[1])
+
+    def move(step):
+        for d in range(1, row_count):
+            peer = lax.rem(row + d, row_count)
+            part = pl.ds(cuts[step], cuts[step + 1] - cuts[step])
+            index = step * row_count + d
+            source = corr_ref.at[peer, part]
+            moved.append(send(source, corr_out.at[row, part], corr_send, corr_recv, index, on_row(peer)))
+
+    move(0)
     own = pltpu.make_async_copy(corr_ref.at[row], corr_out.at[row], own_sem.at[0])
     own.start()
     for copy in first:
@@ -591,6 +599,7 @@
         peer = on_row(2 * there + parity)
         across.append(send(wide_both.at[there], wide_scr.at[chip], row_send, row_recv, d, peer))
         across.append(send(thin_both.at[there], thin_scr.at[chip], row_send, row_recv, chips + d, peer))
+    move(1)
     for copy in across:
         copy.wait()
     wide = wide_both[chip]
@@ -615,6 +624,7 @@
         there = lax.rem(chip + d, chips)
         third.append(send(wide_col, wide_out.at[row], last_send, last_recv, d, on_row(2 * there + parity)))
     fourth = [send(wide_col, wide_out.at[row], core_send, core_recv, 0, on_row(core))]
+    move(2)
     wide_out[row] = wide_col[...]
     for d in range(1, chips):
         third[d - 1].wait_recv()
@@ -624,6 +634,28 @@
         copy.wait_send()
     for copy in fourth:
         copy.wait()
+    if up_out.shape[0] > RANK:
+        lane = iota((wide_out.shape[2], LANES), 1) < P_SIZE
+        share = wide_out.shape[2]
+        mine = jnp.zeros(mine_out.shape, F32)
+        for c in range(col_count):
+            mine = mine + jnp.where(owner_ref[c] == col, thin_out[c], 0.0)
+        mine_out[...] = mine
+        for a in range(up_out.shape[0] // RANK):
+            for r in range(row_count):
+                total = jnp.zeros(wide_out.shape[2:], F32)
+                for c in range(col_count):
+                    total = total + jnp.where(owner_ref[c] == a, wide_out[r, c], 0.0)
+                rows = slice(a * RANK + r * share, a * RANK + (r + 1) * share)
+                tiles = [total[:, i * LANES : (i + 1) * LANES] for i in range(QUAD)]
+                turned = [pltpu.roll(tile, P_SIZE, 1) for tile in tiles]
+                for h in range(QUAD):
+                    gate, value = h // 2, 2 + h // 2
+                    if h % 2 == 0:
+                        up_out[rows, h, :] = jnp.where(lane, tiles[gate], turned[value])
+                    else:
+                        up_out[rows, h, :] = jnp.where(lane, turned[gate], tiles[value])
+                down_out[rows, :] = total[:, 2 * WIDTH :]
     for copy in moved:
         copy.wait()
     own.wait()
@@ -1023,33 +1055,37 @@
     )(state, decay)
 
 
-def finish_exchange(corr, wide, thin):
+def finish_exchange(corr, wide, thin, owner, placed):
     row_count = corr.shape[0]
     col_count = wide.shape[1]
     share, width = wide.shape[2:]
+    ranks = RANK * col_count if placed else RANK
     vmem = pl.BlockSpec(memory_space=pltpu.VMEM)
     anywhere = pl.BlockSpec(memory_space=pl.ANY)
     dma = pltpu.SemaphoreType.DMA
     return pl.pallas_call(
         tail_kernel,
-        in_specs=[anywhere, vmem, vmem],
-        out_specs=[anywhere, vmem, vmem],
+        in_specs=[anywhere, vmem, vmem, pl.BlockSpec(memory_space=pltpu.SMEM)],
+        out_specs=[anywhere] + [vmem] * 5,
         out_shape=[
             jax.ShapeDtypeStruct(corr.shape, corr.dtype),
             jax.ShapeDtypeStruct((row_count, col_count, share, width), F32),
             jax.ShapeDtypeStruct((col_count,) + thin.shape[1:], F32),
+            jax.ShapeDtypeStruct((ranks, QUAD, LANES), F32),
+            jax.ShapeDtypeStruct((ranks, WIDTH), F32),
+            jax.ShapeDtypeStruct(thin.shape[1:], F32),
         ],
         scratch_shapes=[
             *[pltpu.VMEM((row_count // 2,) + value.shape[1:], F32) for value in (wide, thin) * 3],
             pltpu.VMEM(wide.shape[1:], F32), pltpu.VMEM(thin.shape[1:], F32), pltpu.VMEM(wide.shape[1:], F32),
-            dma((1,)), dma((row_count,)), dma((row_count,)), dma((row_count,)), dma((row_count,)),
+            dma((1,)), dma((3 * row_count,)), dma((3 * row_count,)), dma((row_count,)), dma((row_count,)),
             dma((row_count,)), dma((row_count,)), dma((2 * col_count,)), dma((2 * col_count,)),
             dma((row_count // 2,)), dma((row_count // 2,)), dma((row_count // 2,)), dma((row_count // 2,)),
         ],
         compiler_params=pltpu.CompilerParams(
             collective_id=0, has_side_effects=True, vmem_limit_bytes=VMEM_BYTES
         ),
-    )(corr, wide, thin)
+    )(corr, wide, thin, owner)
 
 
 def whole_spec(shape):
@@ -1208,7 +1244,7 @@
     rank_share = rank_total // col_count
     adapter = lax.dynamic_index_in_dim(adapter_id, col // seq_cols, keepdims=False)
 
-    relayed = row_count == 4 and heads_here == QUAD and seq_cols == 1 and part == WIDTH
+    relayed = row_count == 4 and heads_here == QUAD and seq_cols == 1 and part == WIDTH and rank_share == RANK
     place = jnp.zeros((2,), jnp.int32)
     if relayed:
         x_rows, w_all, w_state, gain_all, vectors, head_rows, place = start_exchange(
@@ -1360,7 +1396,7 @@
         wide = jnp.swapaxes(wide.reshape(row_count, GROUPS, share, 3, WIDTH), 0, 1)
         wide = to_cols(wide, heads_here, col_count)
         wide = jnp.swapaxes(wide, 0, 1).reshape(row_count, col_count, share, 3 * local)
-    corr, wide, thin = finish_exchange(corr, wide, thin)
+    corr, wide, thin, in_up, out_down, mine = finish_exchange(corr, wide, thin, adapter_id, relayed)
     late = jnp.zeros((1, HALO, part), BF16)
     if seq_cols > 1:
         pairs = [(i, (i - 1) % col_count) for i in range(col_count)]
@@ -1370,6 +1406,9 @@
     early = jnp.pad(early, ((0, 0), (chunk - HALO, 0), (0, 0))).astype(F32)
     input_grad = cotangent.reshape(row_count, chunk, part).astype(F32) + corr[:, HALO:].astype(F32) + early
     input_grad = input_grad.reshape(col_tokens, part)
+    if relayed:
+        mine = jnp.swapaxes(mine.reshape(2, RANK, part), 1, 2)
+        return block_out, input_grad, mine[0], in_up, out_down, mine[1]
     wide = jnp.swapaxes(wide, 0, 1).reshape(col_count, RANK, 3 * local)
     owner = jnp.repeat(adapter_id, seq_cols)
     adapters = rank_total // RANK

time: 322 us -> 309 us (0.960)
  Pallas kernels: 295 us -> 284 us
    pallas_call x1, Pallas kernels: 44.9 us -> 34.1 us  [finish_exchange(): pl.pallas_call(tail_kernel, in_specs=[anywhere, vmem, vmem, pl.BlockSpec(...]
  transfers between devices with their start and end apart: 2 -> 2, of which waited for: 1 -> 1; matrix products, arithmetic and copies ran while one was open for 0% -> 0% of each run, Pallas kernels for 18% -> 19%
where the time goes in v6:
time: 309 us; the launch traced here: 308 us
  Pallas kernels  284 us (92%)
  starting transfers between devices  8.56 us (3%)
  local copies, waits for them, and re-layouts  8.05 us (3%)
  other arithmetic  4.71 us (2%)
    pallas_call x4, Pallas kernels, grouped_call(): pl.pallas_call(kernel, grid_spec=pltpu.PrefetchScalarGridSpec(num_scalar_...  146 us
    pallas_call x1, Pallas kernels, start_exchange(): pl.pallas_call(start_kernel, in_specs=[anywhere] + [vmem] * (7 + len(vect...  77.5 us
    pallas_call x1, Pallas kernels, finish_exchange(): pl.pallas_call(tail_kernel, in_specs=[anywhere, vmem, vmem, pl.BlockSpec(...  34.1 us
    pallas_call x2, Pallas kernels, carry_over(): pl.pallas_call(functools.partial(carry_kernel, forward), in_specs=[vmem,...  26.5 us
  transfers between devices with their start and end apart: 2, of which 1 were waited for; matrix products, arithmetic and copies ran while one was open for 0% of the time, Pallas kernels for 19%

profile of v6, /device:TPU:0, one launch (start us, length us, event | category | flops | bytes accessed | tf_op | source)
XLA Modules:
  0.0 308.0 jit_solution(5216004162918891407)
XLA Ops:
  0.6 1.6 copy.30
  2.2 1.7 copy.29
  3.9 77.5 %shard_map.226 = (bf16[4,1040,256]{2,1,0:T(8,128)(2,1)}, bf16[8,4,432,512]{3,2,1,0:T(8,128)(2,1)}, bf16[4,256,384]{2,1,0:T(8,128)(2,1)}, f32[4,1,256]{2,1,0:T(1,...) custom-call(bf16[4096,256]{1,0:T(8,128)(2,1)} %x_ref.1, bf16[256,512]{1,0:T(8,128)(2,1)} %bitcast.30, ...), custom_call_target="tpu_custom_call" | custom-call | tf_op jit(solution)/shard_map/pallas_call | solution.py:940
  81.4 3.6 %all-to-all-start = ((bf16[4,1024,256]{2,1,0:T(8,128)(2,1)}), bf16[4,1024,256]{2,1,0:T(8,128)(2,1)S(1)}, u32[]{:S(2)}, u32[]{:S(2)}) async-start(bf16[4,1024,256]{2,1,0:T(8,128)(2,1)} %bitcast.8), calls=%async_computation | async-start | bytes 4194304 | tf_op jit(solution)/shard_map/all_to_all | solution.py:1261
  85.0 33.1 %shard_map.227 = (bf16[1040,1024]{1,0:T(8,128)(2,1)}, f32[1024,256]{1,0:T(8,128)}, f32[1024,128]{1,0:T(8,128)}, f32[1024,128]{1,0:T(8,128)}, f32[1024,128]{1,0:T...) custom-call(s32[2]{0:T(128)} %get-tuple-element.53.place_ref, ...), custom_call_target="tpu_custom_call" | custom-call | flops 44999999488 | bytes 40000000 | tf_op jit(solution)/shard_map/pallas_call | solution.py:1144
  118.1 0.0 all-to-all-done.g_ref
  118.1 0.0 copy-start
  118.1 12.6 %shard_map.228.ein_ref = f32[128,2048]{1,0:T(8,128)} custom-call(bf16[128,2048]{1,0:T(8,128)(2,1)} %get-tuple-element.67.state_ref, f32[8,2048]{1,0:T(8,128)} %get-tuple-element.68.decay_ref), custom_call_target="tpu_custom_call" | custom-call | tf_op jit(solution)/shard_map/pallas_call | solution.py:1042
  130.7 0.0 copy-done
  130.7 34.9 %shard_map.229 = (bf16[4,1024,256]{2,1,0:T(8,128)(2,1)}, bf16[1024,2048]{1,0:T(8,128)(2,1)}, bf16[4,128,2048]{2,1,0:T(8,128)(2,1)}, f32[1024,128]{1,0:T(8,128)},...) custom-call(s32[2]{0:T(128)} %get-tuple-element.53.place_ref, bf16[4,1040,256]{2,1,0:T(8,128)(2,1)} %get-tuple-element.55.x_ref, ...), custom_call_target="tpu_custom_call" | custom-call | flops 44999999488 | bytes 40000000 | tf_op jit(solution)/shard_map/pallas_call | solution.py:1144
  165.6 4.9 %all-to-all-start.1 = ((bf16[4,1024,256]{2,1,0:T(8,128)(2,1)}), bf16[4,1024,256]{2,1,0:T(8,128)(2,1)S(1)}, u32[]{:S(2)}, u32[]{:S(2)}) async-start(bf16[4,1024,256]{2,1,0:T(8,128)(2,1)} %get-tuple-element.78), calls=%async_computation.1 | async-start | bytes 4194304 | tf_op jit(solution)/shard_map/all_to_all | solution.py:1355
  170.6 24.4 %shard_map.230 = (bf16[1024,2048]{1,0:T(8,128)(2,1)}, bf16[1024,2048]{1,0:T(8,128)(2,1)}, bf16[4,128,2048]{2,1,0:T(8,128)(2,1)}, bf16[128,2048]{1,0:T(8,128)(2,1)}, f32[8,16,256]{2,1,0:T(8,128)}) custom-call(s32[2]{0:T(128)} %get-tuple-element.53.place_ref, bf16[4,1024,256]{2,1,0:T(8,128)(2,1)} %copy-done, ...), custom_call_target="tpu_custom_call" | custom-call | flops 24999999488 | bytes 40000000 | tf_op jit(solution)/shard_map/pallas_call | solution.py:1144
  195.0 1.9 all-to-all-done.1
  197.0 13.9 %shard_map.231.gin_ref = f32[128,2048]{1,0:T(8,128)} custom-call(bf16[128,2048]{1,0:T(8,128)(2,1)} %get-tuple-element.86.state_ref, f32[8,2048]{1,0:T(8,128)} %get-tuple-element.68.decay_ref), custom_call_target="tpu_custom_call" | custom-call | tf_op jit(solution)/shard_map/pallas_call | solution.py:1042
  210.9 53.5 %shard_map.232 = (bf16[4,1040,256]{2,1,0:T(8,128)(2,1)}, f32[4,8,4,768]{3,2,1,0:T(4,128)}, f32[4,32,256]{2,1,0:T(8,128)}) custom-call(s32[2]{0:T(128)} %get-tuple-element.53.place_ref, bf16[4,1040,256]{2,1,0:T(8,128)(2,1)} %get-tuple-element.55.x_ref, f32[4,1,256]{2,1,0:T(1,128)} %get-tuple-element.56.gain_ref, ...), custom_call_target="tpu_custom_call" | custom-call | flops 74999996416 | bytes 40000000 | tf_op jit(solution)/shard_map/pallas_call | solution.py:1144
  264.4 34.1 %shard_map.233 = (bf16[4,1040,256]{2,1,0:T(8,128)(2,1)}, f32[4,8,4,768]{3,2,1,0:T(4,128)}, f32[8,32,256]{2,1,0:T(8,128)}, f32[128,4,128]{2,1,0:T(4,128)}, f32[128,256]{1,0:T(8,128)}, /*index=5*/f32[32,256]{1,0:T(8,128)}) custom-call(bf16[4,1040,256]{2,1,0:T(8,128)(2,1)} %get-tuple-element.93.corr_ref, f32[4,8,4,768]{3,2,1,0:T(4,128)} %get-tuple-element.94.wide_ref, ...), custom_call_target="tpu_custom_call" | custom-call | tf_op jit(solution)/shard_map/pallas_call | solution.py:1066
  298.5 1.3 slice_bitcast_fusion
  299.9 0.7 slice.13
  300.6 4.7 %fusion = f32[4,1024,256]{2,1,0:T(8,128)} fusion(bf16[4,1024,256]{2,1,0:T(8,128)(2,1)} %bitcast.17, bf16[3,16,256]{2,1,0:T(8,128)(2,1)S(1)} %slice.13, bf16[4,1040,256]{2,1,0:T(8,128)(2,1)} %get-tuple-element.96), kind=kLoop, calls=%fused_computation.1 | loop fusion | flops 5242880 | bytes 8413184 | tf_op jit(solution)/shard_map/add | solution.py:1407
  305.3 0.0 copy-start.1
  305.3 0.0 copy-start.2
  305.3 1.3 copy.34
  306.6 0.0 copy-done.1
  306.6 0.7 copy.35
  307.3 0.0 copy-done.2
  307.4 0.7 copy.36
Async XLA Ops:
  81.4 36.7 %all-to-all-start = ((bf16[4,1024,256]{2,1,0:T(8,128)(2,1)}), bf16[4,1024,256]{2,1,0:T(8,128)(2,1)S(1)}, u32[]{:S(2)}, u32[]{:S(2)}) async-start(bf16[4,1024,256]{2,1,0:T(8,128)(2,1)} %bitcast.8), calls=%async_computation | async-start | bytes 4194304 | tf_op jit(solution)/shard_map/all_to_all | solution.py:1261
  118.1 12.6 %copy-start = (bf16[4,1024,256]{2,1,0:T(8,128)(2,1)}, bf16[4,1024,256]{2,1,0:T(8,128)(2,1)S(1)}, u32[]{:S(2)}) copy-start(bf16[4,1024,256]{2,1,0:T(8,128)(2,1)S(1)} %all-to-all-done.g_ref) | copy-start | bytes 6291460
  165.6 31.3 %all-to-all-start.1 = ((bf16[4,1024,256]{2,1,0:T(8,128)(2,1)}), bf16[4,1024,256]{2,1,0:T(8,128)(2,1)S(1)}, u32[]{:S(2)}, u32[]{:S(2)}) async-start(bf16[4,1024,256]{2,1,0:T(8,128)(2,1)} %get-tuple-element.78), calls=%async_computation.1 | async-start | bytes 4194304 | tf_op jit(solution)/shard_map/all_to_all | solution.py:1355
  305.3 1.3 copy-start.1
  305.3 2.0 copy-start.2

commit v7 on v6

--- a/solution.py
+++ b/solution.py
@@ -688,15 +688,15 @@
 
     def paired(value):
         lane = iota((value.shape[0], LANES), 1) < P_SIZE
-        tiles = [value[:, h * LANES : (h + 1) * LANES].astype(F32) for h in range(QUAD)]
+        tiles = [value[:, h, :].astype(F32) for h in range(QUAD)]
         turned = [pltpu.roll(tile, P_SIZE, 1) for tile in tiles]
         gates = [jnp.where(lane, tiles[h], turned[h + 1]) for h in (0, 2)]
         values = [jnp.where(lane, turned[h], tiles[h + 1]) for h in (0, 2)]
         return jnp.concatenate(gates + values, axis=1).astype(BF16)
 
-    block_scr[0:part, :] = paired(w_ref[...])
+    block_scr[0:part, :] = paired(w_ref)
     ranks = pl.ds(pl.multiple_of(row * rank_part, rank_part), rank_part)
-    block_scr[part : part + rank_part, :] = paired(up_ref[ranks, :])
+    block_scr[part : part + rank_part, :] = paired(up_ref.at[ranks])
     first = part + rank_part
     half = WIDTH // 2
     block_scr[first : first + half, :WIDTH] = p_ref[:half, :]
@@ -1248,7 +1248,7 @@
     place = jnp.zeros((2,), jnp.int32)
     if relayed:
         x_rows, w_all, w_state, gain_all, vectors, head_rows, place = start_exchange(
-            block_in, proj_inner.reshape(part, 2 * local), adapt_in_up.reshape(rank_total, 2 * local), proj_out,
+            block_in, proj_inner, adapt_in_up, proj_out,
             adapt_out_down, (proj_state.T, adapt_in_down, adapt_out_up),
             (
                 norm_gain[None], conv_inner, conv_inner_bias[None], gate_gain[None], step_bias[None],

time: 309 us -> 306 us (level)
  local copies, waits for them, and re-layouts: 8.05 us -> 4.78 us
    unnamed x11 -> x9, local copies, waits for them, and re-layouts: 5.96 us -> 2.69 us
where the time goes in v7:
time: 306 us; the launch traced here: 305 us
  Pallas kernels  284 us (93%)
  starting transfers between devices  8.72 us (3%)
  local copies, waits for them, and re-layouts  4.78 us (2%)
  other arithmetic  4.71 us (2%)
    pallas_call x4, Pallas kernels, grouped_call(): pl.pallas_call(kernel, grid_spec=pltpu.PrefetchScalarGridSpec(num_scalar_...  146 us
    pallas_call x1, Pallas kernels, start_exchange(): pl.pallas_call(start_kernel, in_specs=[anywhere] + [vmem] * (7 + len(vect...  77.5 us
    pallas_call x1, Pallas kernels, finish_exchange(): pl.pallas_call(tail_kernel, in_specs=[anywhere, vmem, vmem, pl.BlockSpec(...  34.1 us
    pallas_call x2, Pallas kernels, carry_over(): pl.pallas_call(functools.partial(carry_kernel, forward), in_specs=[vmem,...  26.7 us
  transfers between devices with their start and end apart: 2, of which 1 were waited for; matrix products, arithmetic and copies ran while one was open for 0% of the time, Pallas kernels for 19%

profile of v7, /device:TPU:0, one launch (start us, length us, event | category | flops | bytes accessed | tf_op | source)
XLA Modules:
  0.0 305.0 jit_solution(11171479867008116486)
XLA Ops:
  0.6 77.5 %shard_map.226 = (bf16[4,1040,256]{2,1,0:T(8,128)(2,1)}, bf16[8,4,432,512]{3,2,1,0:T(8,128)(2,1)}, bf16[4,256,384]{2,1,0:T(8,128)(2,1)}, f32[4,1,256]{2,1,0:T(1,...) custom-call(bf16[4096,256]{1,0:T(8,128)(2,1)} %x_ref.1, bf16[256,4,128]{2,1,0:T(4,128)(2,1)} %w_ref.1, ...), custom_call_target="tpu_custom_call" | custom-call | tf_op jit(solution)/shard_map/pallas_call | solution.py:940
  78.2 3.6 %all-to-all-start = ((bf16[4,1024,256]{2,1,0:T(8,128)(2,1)}), bf16[4,1024,256]{2,1,0:T(8,128)(2,1)S(1)}, u32[]{:S(2)}, u32[]{:S(2)}) async-start(bf16[4,1024,256]{2,1,0:T(8,128)(2,1)} %bitcast.8), calls=%async_computation | async-start | bytes 4194304 | tf_op jit(solution)/shard_map/all_to_all | solution.py:1261
  81.8 33.1 %shard_map.227 = (bf16[1040,1024]{1,0:T(8,128)(2,1)}, f32[1024,256]{1,0:T(8,128)}, f32[1024,128]{1,0:T(8,128)}, f32[1024,128]{1,0:T(8,128)}, f32[1024,128]{1,0:T...) custom-call(s32[2]{0:T(128)} %get-tuple-element.53.place_ref, ...), custom_call_target="tpu_custom_call" | custom-call | flops 44999999488 | bytes 40000000 | tf_op jit(solution)/shard_map/pallas_call | solution.py:1144
  114.9 0.0 all-to-all-done.g_ref
  114.9 0.0 copy-start
  114.9 12.6 %shard_map.228.ein_ref = f32[128,2048]{1,0:T(8,128)} custom-call(bf16[128,2048]{1,0:T(8,128)(2,1)} %get-tuple-element.67.state_ref, f32[8,2048]{1,0:T(8,128)} %get-tuple-element.68.decay_ref), custom_call_target="tpu_custom_call" | custom-call | tf_op jit(solution)/shard_map/pallas_call | solution.py:1042
  127.5 0.0 copy-done
  127.5 34.9 %shard_map.229 = (bf16[4,1024,256]{2,1,0:T(8,128)(2,1)}, bf16[1024,2048]{1,0:T(8,128)(2,1)}, bf16[4,128,2048]{2,1,0:T(8,128)(2,1)}, f32[1024,128]{1,0:T(8,128)},...) custom-call(s32[2]{0:T(128)} %get-tuple-element.53.place_ref, bf16[4,1040,256]{2,1,0:T(8,128)(2,1)} %get-tuple-element.55.x_ref, ...), custom_call_target="tpu_custom_call" | custom-call | flops 44999999488 | bytes 40000000 | tf_op jit(solution)/shard_map/pallas_call | solution.py:1144
  162.4 5.1 %all-to-all-start.1 = ((bf16[4,1024,256]{2,1,0:T(8,128)(2,1)}), bf16[4,1024,256]{2,1,0:T(8,128)(2,1)S(1)}, u32[]{:S(2)}, u32[]{:S(2)}) async-start(bf16[4,1024,256]{2,1,0:T(8,128)(2,1)} %get-tuple-element.78), calls=%async_computation.1 | async-start | bytes 4194304 | tf_op jit(solution)/shard_map/all_to_all | solution.py:1355
  167.5 24.4 %shard_map.230 = (bf16[1024,2048]{1,0:T(8,128)(2,1)}, bf16[1024,2048]{1,0:T(8,128)(2,1)}, bf16[4,128,2048]{2,1,0:T(8,128)(2,1)}, bf16[128,2048]{1,0:T(8,128)(2,1)}, f32[8,16,256]{2,1,0:T(8,128)}) custom-call(s32[2]{0:T(128)} %get-tuple-element.53.place_ref, bf16[4,1024,256]{2,1,0:T(8,128)(2,1)} %copy-done, ...), custom_call_target="tpu_custom_call" | custom-call | flops 24999999488 | bytes 40000000 | tf_op jit(solution)/shard_map/pallas_call | solution.py:1144
  191.9 1.8 all-to-all-done.1
  193.7 14.1 %shard_map.231.gin_ref = f32[128,2048]{1,0:T(8,128)} custom-call(bf16[128,2048]{1,0:T(8,128)(2,1)} %get-tuple-element.86.state_ref, f32[8,2048]{1,0:T(8,128)} %get-tuple-element.68.decay_ref), custom_call_target="tpu_custom_call" | custom-call | tf_op jit(solution)/shard_map/pallas_call | solution.py:1042
  207.8 53.5 %shard_map.232 = (bf16[4,1040,256]{2,1,0:T(8,128)(2,1)}, f32[4,8,4,768]{3,2,1,0:T(4,128)}, f32[4,32,256]{2,1,0:T(8,128)}) custom-call(s32[2]{0:T(128)} %get-tuple-element.53.place_ref, bf16[4,1040,256]{2,1,0:T(8,128)(2,1)} %get-tuple-element.55.x_ref, f32[4,1,256]{2,1,0:T(1,128)} %get-tuple-element.56.gain_ref, ...), custom_call_target="tpu_custom_call" | custom-call | flops 74999996416 | bytes 40000000 | tf_op jit(solution)/shard_map/pallas_call | solution.py:1144
  261.4 34.1 %shard_map.233 = (bf16[4,1040,256]{2,1,0:T(8,128)(2,1)}, f32[4,8,4,768]{3,2,1,0:T(4,128)}, f32[8,32,256]{2,1,0:T(8,128)}, f32[128,4,128]{2,1,0:T(4,128)}, f32[128,256]{1,0:T(8,128)}, /*index=5*/f32[32,256]{1,0:T(8,128)}) custom-call(bf16[4,1040,256]{2,1,0:T(8,128)(2,1)} %get-tuple-element.93.corr_ref, f32[4,8,4,768]{3,2,1,0:T(4,128)} %get-tuple-element.94.wide_ref, ...), custom_call_target="tpu_custom_call" | custom-call | tf_op jit(solution)/shard_map/pallas_call | solution.py:1066
  295.5 1.3 slice_bitcast_fusion
  296.9 0.7 slice.13
  297.6 4.7 %fusion = f32[4,1024,256]{2,1,0:T(8,128)} fusion(bf16[4,1024,256]{2,1,0:T(8,128)(2,1)} %bitcast.17, bf16[3,16,256]{2,1,0:T(8,128)(2,1)S(1)} %slice.13, bf16[4,1040,256]{2,1,0:T(8,128)(2,1)} %get-tuple-element.96), kind=kLoop, calls=%fused_computation.1 | loop fusion | flops 5242880 | bytes 8413184 | tf_op jit(solution)/shard_map/add | solution.py:1407
  302.3 0.0 copy-start.1
  302.3 0.0 copy-start.2
  302.3 1.3 copy.28
  303.6 0.0 copy-done.1
  303.6 0.7 copy.29
  304.3 0.0 copy-done.2
  304.3 0.7 copy.30
Async XLA Ops:
  78.2 36.7 %all-to-all-start = ((bf16[4,1024,256]{2,1,0:T(8,128)(2,1)}), bf16[4,1024,256]{2,1,0:T(8,128)(2,1)S(1)}, u32[]{:S(2)}, u32[]{:S(2)}) async-start(bf16[4,1024,256]{2,1,0:T(8,128)(2,1)} %bitcast.8), calls=%async_computation | async-start | bytes 4194304 | tf_op jit(solution)/shard_map/all_to_all | solution.py:1261
  114.9 12.6 %copy-start = (bf16[4,1024,256]{2,1,0:T(8,128)(2,1)}, bf16[4,1024,256]{2,1,0:T(8,128)(2,1)S(1)}, u32[]{:S(2)}) copy-start(bf16[4,1024,256]{2,1,0:T(8,128)(2,1)S(1)} %all-to-all-done.g_ref) | copy-start | bytes 6291460
  162.4 31.3 %all-to-all-start.1 = ((bf16[4,1024,256]{2,1,0:T(8,128)(2,1)}), bf16[4,1024,256]{2,1,0:T(8,128)(2,1)S(1)}, u32[]{:S(2)}, u32[]{:S(2)}) async-start(bf16[4,1024,256]{2,1,0:T(8,128)(2,1)} %get-tuple-element.78), calls=%async_computation.1 | async-start | bytes 4194304 | tf_op jit(solution)/shard_map/all_to_all | solution.py:1355
  302.3 1.3 copy-start.1
  302.3 2.0 copy-start.2

commit v8 on v7

--- a/solution.py
+++ b/solution.py
@@ -22,6 +22,7 @@
 IN_LANE = 32
 OUT_LANE = 48
 CAP = 80.0
+SHARE_STEP = 4
 QUAD = 4
 WIDTH = QUAD * P_SIZE
 GROUPS = HEADS // QUAD
@@ -235,8 +236,18 @@
     dec_ref[...] = jnp.broadcast_to(decay, (8, WIDTH))
 
 
+def inner_products(score, cum, turned_ref, rows, xs):
+    total = None
+    for h in range(QUAD):
+        spread = cum[:, h : h + 1] + turned_ref[0, QUAD + h : QUAD + h + 1, rows]
+        weights = (score * jnp.exp2(jnp.minimum(spread, CAP))).astype(BF16)
+        term = mm(weights, head_only(xs, h))
+        total = term if total is None else total + term
+    return total
+
+
 def scan_kernel(
-    place_ref, x_ref, g_ref, wst_ref, w_ref, down_ref, vp_ref, gate_ref, u_ref, eloc_ref, ein_ref,
+    ready, place_ref, x_ref, g_ref, wst_ref, w_ref, down_ref, vp_ref, gate_ref, u_ref, eloc_ref, ein_ref,
     cum_ref, turned_ref, bs_ref, cs_ref,
     out_ref, o_ref, ent_ref, aux_ref, sg_ref, gup_ref,
     score_scr, gained_scr, side_scr, square_scr,
@@ -251,10 +262,12 @@
         square_scr[...] = jnp.zeros_like(square_scr)
         keep = iota((BLOCK, BLOCK), 0) >= iota((BLOCK, BLOCK), 1)
 
-        @pl.loop(0, blocks)
-        def _(k):
-            score = mm_nt(cs_ref[at_block(k), :], bs_ref[at_block(k), :])
-            score_scr[k] = jnp.where(keep, score, 0.0)
+        if not ready:
+
+            @pl.loop(0, blocks)
+            def _(k):
+                score = mm_nt(cs_ref[at_block(k), :], bs_ref[at_block(k), :])
+                score_scr[k] = jnp.where(keep, score, 0.0)
 
     taps = vp_ref[0]
 
@@ -265,15 +278,14 @@
         pre = u_ref[rows, :].astype(F32)
         conv = pre * sigmoid(pre)
         cum = to_front(cum_ref[rows, :], group)
-        xs = conv.astype(BF16)
-        score = score_scr[k]
         entering = (eloc_ref[k].astype(F32) + before * ein_ref[...]).astype(BF16)
         ent_ref[k] = entering
         total = widen(jnp.exp2(cum)) * mm(cs_ref[rows, :], entering)
-        for h in range(QUAD):
-            spread = cum[:, h : h + 1] + turned_ref[0, QUAD + h : QUAD + h + 1, rows]
-            weights = (score * jnp.exp2(jnp.minimum(spread, CAP))).astype(BF16)
-            total = total + mm(weights, head_only(xs, h))
+        if ready:
+            total = total + turned_ref[rows, :].astype(F32)
+        else:
+            score = score_scr[k]
+            total = total + inner_products(score, cum, turned_ref, rows, conv.astype(BF16))
         output = total + taps[6:7] * conv
         o_ref[rows, :] = output.astype(BF16)
         gate = gate_ref[rows, :].astype(F32)
@@ -1035,6 +1047,136 @@
                 out_ref[part, cols] = jnp.where(second, later, total)
 
 
+def within_kernel(
+    state_ref, decay_ref, u_ref, cum_ref, turned_ref, bs_ref, cs_ref,
+    within_ref, out_ref,
+    score_scr, other_scr, other_decay, total_scr, total_in,
+    core_send, core_recv, across_send, across_recv, share_send, share_recv,
+):
+    group = pl.program_id(0)
+    blocks = score_scr.shape[0]
+    row = lax.axis_index("row")
+    parity = lax.rem(row, 2)
+    sends = row // 2 == 0
+    core = row + 1 - 2 * parity
+    across = lax.rem(row + 2, 4)
+    half = state_ref.shape[1] // 2
+    depth = state_ref.shape[0] // 2
+
+    def remote(source, target, sending, receiving, index, peer):
+        return pltpu.make_async_remote_copy(
+            src_ref=source, dst_ref=target, send_sem=sending.at[index], recv_sem=receiving.at[index],
+            device_id=on_row(peer), device_id_type=MESH,
+        )
+
+    def swaps():
+        return (
+            remote(state_ref, other_scr, core_send, core_recv, 0, core),
+            remote(decay_ref, other_decay, core_send, core_recv, 1, core),
+        )
+
+    def crossing(q):
+        return remote(total_scr.at[q], total_in.at[parity, q], across_send, across_recv, q, across)
+
+    @pl.when(group == 0)
+    def _():
+        barrier = pltpu.get_barrier_semaphore()
+        for peer in (core, across):
+            pl.semaphore_signal(barrier, inc=1, device_id=on_row(peer), device_id_type=MESH)
+        pl.semaphore_wait(barrier, 2)
+        for copy in swaps():
+            copy.start()
+        keep = iota((BLOCK, BLOCK), 0) >= iota((BLOCK, BLOCK), 1)
+        for k in range(blocks):
+            score = mm_nt(cs_ref[at_block(k), :], bs_ref[at_block(k), :])
+            score_scr[k] = jnp.where(keep, score, 0.0)
+        for copy in swaps():
+            copy.wait()
+
+        @pl.when(sends)
+        def _():
+            for p in range(2):
+
+                @pl.when(parity == p)
+                def _():
+                    cols = slice(p * half, (p + 1) * half)
+                    for q in range(2):
+                        part = slice(q * depth, (q + 1) * depth)
+                        mine = state_ref[part, cols].astype(F32)
+                        other = other_scr[part, cols].astype(F32)
+                        if p == 1:
+                            total_scr[q] = (mine + other * decay_ref[0:1, cols]).astype(BF16)
+                        else:
+                            total_scr[q] = (other + mine * other_decay[0:1, cols]).astype(BF16)
+            for q in range(2):
+                crossing(q).start()
+
+    for k in range(blocks):
+        rows = at_block(k)
+        pre = u_ref[rows, :].astype(F32)
+        conv = pre * sigmoid(pre)
+        cum = to_front(cum_ref[rows, :], group)
+        total = inner_products(score_scr[k], cum, turned_ref, rows, conv.astype(BF16))
+        within_ref[rows, :] = total.astype(BF16)
+
+    @pl.when((group == SHARE_STEP) & jnp.logical_not(sends))
+    def _():
+        for q in range(2):
+            crossing(q).wait_recv()
+            mine = total_in.at[parity, q]
+            remote(mine, mine, share_send, share_recv, q, core).start()
+
+    @pl.when((group == SHARE_STEP + 1) & jnp.logical_not(sends))
+    def _():
+        for q in range(2):
+            remote(
+                total_in.at[parity, q], total_in.at[1 - parity, q], share_send, share_recv, q, core
+            ).wait()
+        for p in range(2):
+            for q in range(2):
+                cols = slice(p * half, (p + 1) * half)
+                part = slice(q * depth, (q + 1) * depth)
+                total = total_in[p, q].astype(F32)
+                later = other_scr[part, cols].astype(F32) + total * other_decay[0:1, cols]
+                out_ref[part, cols] = jnp.where(parity == 1, later, total)
+
+    @pl.when((group == SHARE_STEP + 1) & sends)
+    def _():
+        for q in range(2):
+            crossing(q).wait_send()
+        out_ref[...] = jnp.where(parity == 1, other_scr[...].astype(F32), 0.0)
+
+
+def within_and_carry(state, decay, u, cum, turned, bs, cs):
+    dma = pltpu.SemaphoreType.DMA
+    rows, cols = state.shape
+    tokens = u.shape[0]
+
+    def fixed(shape):
+        return pl.BlockSpec(shape, lambda c: (0,) * len(shape))
+
+    lanes = pl.BlockSpec((tokens, WIDTH), lambda c: (0, c))
+    return pl.pallas_call(
+        within_kernel,
+        grid=(GROUPS,),
+        in_specs=[
+            fixed(state.shape), fixed(decay.shape), lanes, fixed(cum.shape),
+            pl.BlockSpec((1,) + turned.shape[1:], lambda c: (c, 0, 0)), fixed(bs.shape), fixed(cs.shape),
+        ],
+        out_specs=[lanes, fixed(state.shape)],
+        out_shape=[jax.ShapeDtypeStruct(u.shape, BF16), jax.ShapeDtypeStruct(state.shape, F32)],
+        scratch_shapes=[
+            pltpu.VMEM((tokens // BLOCK, BLOCK, BLOCK), F32),
+            pltpu.VMEM(state.shape, BF16), pltpu.VMEM(decay.shape, F32),
+            pltpu.VMEM((2, rows // 2, cols // 2), BF16), pltpu.VMEM((2, 2, rows // 2, cols // 2), BF16),
+            dma((2,)), dma((2,)), dma((2,)), dma((2,)), dma((2,)), dma((2,)),
+        ],
+        compiler_params=pltpu.CompilerParams(
+            collective_id=2, has_side_effects=True, vmem_limit_bytes=VMEM_BYTES
+        ),
+    )(state, decay, u, cum, turned, bs, cs)
+
+
 def carry_over(state, decay, forward):
     vmem = pl.BlockSpec(memory_space=pltpu.VMEM)
     dma = pltpu.SemaphoreType.DMA
@@ -1336,14 +1478,14 @@
     decay = dec[0:1]
     fin, g_rows = lax.optimization_barrier((fin, g_rows))
     if relayed:
-        entry = carry_over(fin, dec, True)
+        within, entry = within_and_carry(fin, dec, u, cum, turned, bs, cs)
     else:
         entry = carry_in(fin, decay, row_count, col_count, seq_cols, True)
     out_rows, o, ent, aux, side_grad, out_up_grad = grouped_call(
-        scan_kernel,
+        functools.partial(scan_kernel, relayed),
         place,
-        (x_rows, g_rows, w_state, p_all, down_all, vectors, gate, u, eloc, entry, cum, turned, bs, cs),
-        "aaafdcllllacaa",
+        (x_rows, g_rows, w_state, p_all, down_all, vectors, gate, u, eloc, entry, cum, within if relayed else turned, bs, cs),
+        "aaafdclllla" + ("l" if relayed else "c") + "aa",
         [
             ((row_count, chunk, part), BF16), inner_low, ((blocks, STATES, DI), BF16), token_f32, token_low,
             ((RANK, D), F32),

time: 306 us -> 303 us (level)
    pallas_call x0 -> x1, Pallas kernels: none -> 18.8 us  [within_and_carry(): pl.pallas_call(within_kernel, grid=(GROUPS,), in_specs=[fixed(state.shape...]
    pallas_call x2 -> x1, Pallas kernels: 26.7 us -> 14.1 us  [carry_over(): pl.pallas_call(functools.partial(carry_kernel, forward), in_specs=[vmem,...]
    pallas_call x4, Pallas kernels: 146 us -> 139 us  [grouped_call(): pl.pallas_call(kernel, grid_spec=pltpu.PrefetchScalarGridSpec(num_scalar_...]
where the time goes in v8:
time: 303 us; the launch traced here: 302 us
  Pallas kernels  283 us (93%)
  starting transfers between devices  7.42 us (2%)
  local copies, waits for them, and re-layouts  4.78 us (2%)
  other arithmetic  4.71 us (2%)
    pallas_call x4, Pallas kernels, grouped_call(): pl.pallas_call(kernel, grid_spec=pltpu.PrefetchScalarGridSpec(num_scalar_...  139 us
    pallas_call x1, Pallas kernels, start_exchange(): pl.pallas_call(start_kernel, in_specs=[anywhere] + [vmem] * (7 + len(vect...  77.5 us
    pallas_call x1, Pallas kernels, finish_exchange(): pl.pallas_call(tail_kernel, in_specs=[anywhere, vmem, vmem, pl.BlockSpec(...  34.2 us
    pallas_call x1, Pallas kernels, within_and_carry(): pl.pallas_call(within_kernel, grid=(GROUPS,), in_specs=[fixed(state.shape...  18.8 us
    pallas_call x1, Pallas kernels, carry_over(): pl.pallas_call(functools.partial(carry_kernel, forward), in_specs=[vmem,...  14.1 us
  transfers between devices with their start and end apart: 2, of which 1 were waited for; matrix products, arithmetic and copies ran while one was open for 0% of the time, Pallas kernels for 19%

profile of v8, /device:TPU:0, one launch (start us, length us, event | category | flops | bytes accessed | tf_op | source)
XLA Modules:
  0.0 302.1 jit_solution(5000178161868306903)
XLA Ops:
  0.6 77.5 %shard_map.226 = (bf16[4,1040,256]{2,1,0:T(8,128)(2,1)}, bf16[8,4,432,512]{3,2,1,0:T(8,128)(2,1)}, bf16[4,256,384]{2,1,0:T(8,128)(2,1)}, f32[4,1,256]{2,1,0:T(1,...) custom-call(bf16[4096,256]{1,0:T(8,128)(2,1)} %x_ref.1, bf16[256,4,128]{2,1,0:T(4,128)(2,1)} %w_ref.1, ...), custom_call_target="tpu_custom_call" | custom-call | tf_op jit(solution)/shard_map/pallas_call | solution.py:952
  78.1 3.8 %all-to-all-start = ((bf16[4,1024,256]{2,1,0:T(8,128)(2,1)}), bf16[4,1024,256]{2,1,0:T(8,128)(2,1)S(1)}, u32[]{:S(2)}, u32[]{:S(2)}) async-start(bf16[4,1024,256]{2,1,0:T(8,128)(2,1)} %bitcast.8), calls=%async_computation | async-start | bytes 4194304 | tf_op jit(solution)/shard_map/all_to_all | solution.py:1403
  81.9 33.1 %shard_map.227 = (bf16[1040,1024]{1,0:T(8,128)(2,1)}, f32[1024,256]{1,0:T(8,128)}, f32[1024,128]{1,0:T(8,128)}, f32[1024,128]{1,0:T(8,128)}, f32[1024,128]{1,0:T...) custom-call(s32[2]{0:T(128)} %get-tuple-element.55.place_ref, ...), custom_call_target="tpu_custom_call" | custom-call | flops 44999999488 | bytes 40000000 | tf_op jit(solution)/shard_map/pallas_call | solution.py:1286
  115.0 0.0 all-to-all-done.g_ref
  115.0 0.0 copy-start
  115.1 18.8 %shard_map.228 = (bf16[1024,2048]{1,0:T(8,128)(2,1)}, f32[128,2048]{1,0:T(8,128)}) custom-call(bf16[128,2048]{1,0:T(8,128)(2,1)} %get-tuple-element.69.state_ref, f32[8,2048]{1,0:T(8,128)} %get-tuple-element.70.decay_ref, bf16[1024,2048]{1,0:T(8,128)(2,1)} %get-tuple-element.67.u_ref, f32[1024,128]{1,0:T(8,128)} %get-tuple-element.71.cum_ref, ...), custom_call_target="tpu_custom_call" | custom-call | tf_op jit(solution)/shard_map/pallas_call | solution.py:1159
  133.8 0.0 copy-done
  133.8 27.7 %shard_map.229 = (bf16[4,1024,256]{2,1,0:T(8,128)(2,1)}, bf16[1024,2048]{1,0:T(8,128)(2,1)}, bf16[4,128,2048]{2,1,0:T(8,128)(2,1)}, f32[1024,128]{1,0:T(8,128)},...) custom-call(s32[2]{0:T(128)} %get-tuple-element.55.place_ref, bf16[4,1040,256]{2,1,0:T(8,128)(2,1)} %get-tuple-element.57.x_ref, ...), custom_call_target="tpu_custom_call" | custom-call | flops 44999999488 | bytes 40000000 | tf_op jit(solution)/shard_map/pallas_call | solution.py:1286
  161.5 3.6 %all-to-all-start.1 = ((bf16[4,1024,256]{2,1,0:T(8,128)(2,1)}), bf16[4,1024,256]{2,1,0:T(8,128)(2,1)S(1)}, u32[]{:S(2)}, u32[]{:S(2)}) async-start(bf16[4,1024,256]{2,1,0:T(8,128)(2,1)} %get-tuple-element.82), calls=%async_computation.1 | async-start | bytes 4194304 | tf_op jit(solution)/shard_map/all_to_all | solution.py:1497
  165.1 24.4 %shard_map.230 = (bf16[1024,2048]{1,0:T(8,128)(2,1)}, bf16[1024,2048]{1,0:T(8,128)(2,1)}, bf16[4,128,2048]{2,1,0:T(8,128)(2,1)}, bf16[128,2048]{1,0:T(8,128)(2,1)}, f32[8,16,256]{2,1,0:T(8,128)}) custom-call(s32[2]{0:T(128)} %get-tuple-element.55.place_ref, bf16[4,1024,256]{2,1,0:T(8,128)(2,1)} %copy-done, ...), custom_call_target="tpu_custom_call" | custom-call | flops 24999999488 | bytes 40000000 | tf_op jit(solution)/shard_map/pallas_call | solution.py:1286
  189.5 1.3 all-to-all-done.1
  190.8 14.1 %shard_map.231.gin_ref = f32[128,2048]{1,0:T(8,128)} custom-call(bf16[128,2048]{1,0:T(8,128)(2,1)} %get-tuple-element.90.state_ref, f32[8,2048]{1,0:T(8,128)} %get-tuple-element.70.decay_ref), custom_call_target="tpu_custom_call" | custom-call | tf_op jit(solution)/shard_map/pallas_call | solution.py:1184
  204.9 53.5 %shard_map.232 = (bf16[4,1040,256]{2,1,0:T(8,128)(2,1)}, f32[4,8,4,768]{3,2,1,0:T(4,128)}, f32[4,32,256]{2,1,0:T(8,128)}) custom-call(s32[2]{0:T(128)} %get-tuple-element.55.place_ref, bf16[4,1040,256]{2,1,0:T(8,128)(2,1)} %get-tuple-element.57.x_ref, f32[4,1,256]{2,1,0:T(1,128)} %get-tuple-element.58.gain_ref, ...), custom_call_target="tpu_custom_call" | custom-call | flops 74999996416 | bytes 40000000 | tf_op jit(solution)/shard_map/pallas_call | solution.py:1286
  258.4 34.2 %shard_map.233 = (bf16[4,1040,256]{2,1,0:T(8,128)(2,1)}, f32[4,8,4,768]{3,2,1,0:T(4,128)}, f32[8,32,256]{2,1,0:T(8,128)}, f32[128,4,128]{2,1,0:T(4,128)}, f32[128,256]{1,0:T(8,128)}, /*index=5*/f32[32,256]{1,0:T(8,128)}) custom-call(bf16[4,1040,256]{2,1,0:T(8,128)(2,1)} %get-tuple-element.97.corr_ref, f32[4,8,4,768]{3,2,1,0:T(4,128)} %get-tuple-element.98.wide_ref, ...), custom_call_target="tpu_custom_call" | custom-call | tf_op jit(solution)/shard_map/pallas_call | solution.py:1208
  292.6 1.3 slice_bitcast_fusion
  294.0 0.7 slice.13
  294.7 4.7 %fusion = f32[4,1024,256]{2,1,0:T(8,128)} fusion(bf16[4,1024,256]{2,1,0:T(8,128)(2,1)} %bitcast.17, bf16[3,16,256]{2,1,0:T(8,128)(2,1)S(1)} %slice.13, bf16[4,1040,256]{2,1,0:T(8,128)(2,1)} %get-tuple-element.100), kind=kLoop, calls=%fused_computation.1 | loop fusion | flops 5242880 | bytes 8413184 | tf_op jit(solution)/shard_map/add | solution.py:1549
  299.4 0.0 copy-start.1
  299.4 0.0 copy-start.2
  299.4 1.3 copy.28
  300.7 0.0 copy-done.1
  300.7 0.7 copy.29
  301.4 0.0 copy-done.2
  301.4 0.7 copy.30
Async XLA Ops:
  78.1 36.9 %all-to-all-start = ((bf16[4,1024,256]{2,1,0:T(8,128)(2,1)}), bf16[4,1024,256]{2,1,0:T(8,128)(2,1)S(1)}, u32[]{:S(2)}, u32[]{:S(2)}) async-start(bf16[4,1024,256]{2,1,0:T(8,128)(2,1)} %bitcast.8), calls=%async_computation | async-start | bytes 4194304 | tf_op jit(solution)/shard_map/all_to_all | solution.py:1403
  115.0 18.8 %copy-start = (bf16[4,1024,256]{2,1,0:T(8,128)(2,1)}, bf16[4,1024,256]{2,1,0:T(8,128)(2,1)S(1)}, u32[]{:S(2)}) copy-start(bf16[4,1024,256]{2,1,0:T(8,128)(2,1)S(1)} %all-to-all-done.g_ref) | copy-start | bytes 6291460
  161.5 29.3 %all-to-all-start.1 = ((bf16[4,1024,256]{2,1,0:T(8,128)(2,1)}), bf16[4,1024,256]{2,1,0:T(8,128)(2,1)S(1)}, u32[]{:S(2)}, u32[]{:S(2)}) async-start(bf16[4,1024,256]{2,1,0:T(8,128)(2,1)} %get-tuple-element.82), calls=%async_computation.1 | async-start | bytes 4194304 | tf_op jit(solution)/shard_map/all_to_all | solution.py:1497
  299.4 1.3 copy-start.1
  299.4 2.0 copy-start.2
